TPU v7x, 32 devices: a whole 2x2x4 slice. The times are simulated.
32 devices in a mesh: ctx: 8 (over z, y), head: 4 (over x, core).
Axes of the slice: x: 2, y: 2, z: 4, core: 2. Of those that a mesh axis runs over, the one named last changes fastest.
Arguments:
- features: bfloat16 [8192, 16384], P('ctx', 'head'), may hold values from -6 to 6
- gates: bfloat16 [8192, 16384], P('ctx', 'head'), may hold values from -6 to 6
- state_io: bfloat16 [8192, 2, 2048], P('ctx', None, 'head'), may hold values from -6 to 6
- step_size: float32 [256, 8192], P('head', 'ctx'), may hold values from 0.004 to 0.02
- log_decay: float32 [256, 8192], P('head', 'ctx'), may hold values from -2 to 0, as said below
- conv_feat: bfloat16 [4, 16384], P(None, 'head'), may hold values from -3 to 3
- conv_state: bfloat16 [4, 2, 2048], P(None, None, 'head'), may hold values from -3 to 3
- skip_gain: float32 [256], P('head'), may hold values from 0.5 to 1.5
- norm_gain: float32 [16384], P('head'), may hold values from 0.25 to 1.75
Outputs:
- mixed: bfloat16 [8192, 16384], P(('ctx', 'head'))
Inputs may be any that keep to these rules, and one draw needn't show every extreme that they name: `log_decay`: every entry is negative.
All inputs are finite; a program needn't handle non-finite values.
Results may differ from a plain program's by a relative error of at most 0.0034.
Values may be sent and summed in bfloat16 or wider, within the bound.
No kernel may reach another device: no remote copies, remote signals or barrier semaphores. Data moves between devices by JAX's collectives and lax.ppermute only.
A program may use at most 256 MiB of HBM per device.

v0:
```python
import functools

import jax
import jax.numpy as jnp
import numpy as np
from jax import lax
from jax.experimental import pallas as pl
from jax.experimental.pallas import tpu as pltpu
from jax.sharding import PartitionSpec as P

STATE = 256
SPAN = 128
HALO = 16
EPS = 1e-05
LOC, ECUM, DEV, EDEV = range(4)
F32 = jnp.float32
BF16 = jnp.bfloat16
VMEM_BYTES = 48 * 1024 * 1024
VMEM_SMALL = 8 * 1024 * 1024
COST_SCALE = 10**9
MSG = STATE + 16
KEPT = STATE + 8


def dot(a, b):
    return jnp.dot(a, b, preferred_element_type=F32)


def silu(v):
    half = 0.5 * v
    return half * jnp.tanh(half) + half


def cost(micros):
    return pl.CostEstimate(flops=int(micros * COST_SCALE), bytes_accessed=1, transcendentals=0)


def params(limit=VMEM_BYTES):
    return pltpu.CompilerParams(vmem_limit_bytes=limit)


def lanes_of(heads):
    return -(-2 * heads // 128) * 128


def spread_table(heads, head_dim):
    row = np.arange(lanes_of(heads))
    head = np.where(row < 2 * heads, row % heads, heads)
    return (head[:, None] == (np.arange(heads * head_dim) // head_dim)[None, :]).astype(np.float32)


def decay_kernel(log_ref, step_ref, skip_ref, col_ref, row_ref, table_ref, skips_ref):
    heads, tokens = log_ref.shape
    lanes = lanes_of(heads)
    spans = tokens // SPAN
    r = lax.broadcasted_iota(jnp.int32, (SPAN, SPAN), 0)
    c = lax.broadcasted_iota(jnp.int32, (SPAN, SPAN), 1)
    upper = (r <= c).astype(F32)
    cums = []
    for k in range(spans):
        cums.append(
            jnp.dot(
                log_ref[:, k * SPAN : (k + 1) * SPAN],
                upper,
                precision=lax.Precision.HIGHEST,
                preferred_element_type=F32,
            )
        )
    totals = [cum[:, SPAN - 1 :] for cum in cums]
    before = [jnp.zeros_like(totals[0])]
    for k in range(spans - 1):
        before.append(before[-1] + totals[k])
    after = [jnp.zeros_like(totals[0])]
    for k in range(spans - 1, 0, -1):
        after.insert(0, after[0] + totals[k])

    def put(index, k, value):
        high = value.astype(BF16).astype(F32)
        rest = [jnp.zeros((lanes - 2 * heads, SPAN), F32)] if lanes > 2 * heads else []
        both = jnp.concatenate([high, value - high, *rest], axis=0)
        table_ref[k * SPAN : (k + 1) * SPAN, index * lanes : (index + 1) * lanes] = both.T.astype(BF16)

    skip = skip_ref[...]
    high = skip.astype(BF16).astype(F32)
    none = [jnp.zeros((1, lanes - 2 * heads), F32)] if lanes > 2 * heads else []
    parts = jnp.concatenate([high, skip - high, *none], axis=1)
    skips_ref[...] = jnp.broadcast_to(parts, skips_ref.shape).astype(BF16)
    for k in range(spans):
        cum = cums[k]
        step = step_ref[:, k * SPAN : (k + 1) * SPAN]
        col_ref[k * SPAN : (k + 1) * SPAN, :] = jnp.concatenate([cum] * (lanes // heads), axis=0).T
        row_ref[:, k * SPAN : (k + 1) * SPAN] = cum - jnp.log(step)
        to_end = totals[k] - cum
        put(LOC, k, jnp.exp(to_end) * step)
        put(DEV, k, jnp.exp(to_end + after[k]) * step)
        put(ECUM, k, jnp.exp(cum))
        put(EDEV, k, jnp.exp(cum + before[k]))


def behind(count):
    return [pl.BlockSpec(memory_space=pl.ANY)] * count


def decay_tables(log_decay, step_size, skip_gain):
    heads, tokens = log_decay.shape
    lanes = lanes_of(heads)
    return pl.pallas_call(
        decay_kernel,
        out_shape=(
            jax.ShapeDtypeStruct((tokens, lanes), F32),
            jax.ShapeDtypeStruct((heads, tokens), F32),
            jax.ShapeDtypeStruct((tokens, 4 * lanes), BF16),
            jax.ShapeDtypeStruct((16, lanes), BF16),
        ),
        compiler_params=params(),
        name="decays",
        cost_estimate=cost(1.5),
    )(log_decay, step_size, skip_gain[None])


def conv_rows(read, rows, halo, taps, store):
    count, width = taps.shape
    tile = SPAN
    for b in range(rows // tile):
        for c in range(1):
            cols = slice(0, width)
            own = read(b * tile, (b + 1) * tile, cols).astype(F32)
            prev = (halo[:, cols] if b == 0 else read(b * tile - HALO, b * tile, cols)).astype(F32)
            both = jnp.concatenate([prev[HALO - 8 :], own], axis=0)
            total = own * taps[count - 1 : count, cols]
            for k in range(1, count):
                total = total + both[8 - k : 8 - k + tile] * taps[count - 1 - k : count - k, cols]
            store(slice(b * tile, (b + 1) * tile), cols, silu(total))


def read_state(ref):
    if ref.dtype == F32:
        return ref[:STATE, :], ref[STATE : STATE + 1, :]
    tail = ref[STATE:MSG, :].astype(F32)
    return ref[:STATE, :].astype(F32), tail[0:1] + tail[8:9]


def write_kept(ref, value, decay):
    ref[:STATE, :] = value
    ref[STATE:KEPT, :] = jnp.broadcast_to(decay, (KEPT - STATE, decay.shape[1]))


def write_sent(ref, value, decay):
    ref[:STATE, :] = value.astype(BF16)
    high = decay.astype(BF16).astype(F32)
    shape = (8, decay.shape[1])
    rows = jnp.concatenate([jnp.broadcast_to(high, shape), jnp.broadcast_to(decay - high, shape)], axis=0)
    ref[STATE:MSG, :] = rows.astype(BF16)


def maps_kernel(order, io_ref, halo_ref, taps_ref, *refs):
    map_ref, turned_ref = refs[order:]

    def put_in(rows, cols, value):
        map_ref[rows, :STATE] = value.astype(BF16)

    def put_out(rows, cols, value):
        map_ref[rows, STATE:] = value.astype(BF16)

    tokens = io_ref.shape[0]
    for i, put in ((0, put_in), (1, put_out)):
        conv_rows(
            lambda lo, hi, cols: io_ref[lo:hi, i, cols], tokens, halo_ref[:, i, :], taps_ref[:, i, :].astype(F32), put
        )
    for b in range(tokens // SPAN):
        rows = slice(b * SPAN, (b + 1) * SPAN)
        turned_ref[:, rows] = map_ref[rows, :STATE].T


def maps_of(group, state_io, halo, conv_state, after):
    tokens = state_io.shape[0]
    count = conv_state.shape[0]

    def mine(j):
        return (0, 0, group)

    return pl.pallas_call(
        functools.partial(maps_kernel, len(after)),
        grid=(1,),
        in_specs=[
            pl.BlockSpec((tokens, 2, STATE), mine),
            pl.BlockSpec((HALO, 2, STATE), mine),
            pl.BlockSpec((count, 2, STATE), mine),
            *behind(len(after)),
        ],
        out_specs=[
            pl.BlockSpec((tokens, 2 * STATE), lambda j: (0, 0)),
            pl.BlockSpec((STATE, tokens), lambda j: (0, 0)),
        ],
        out_shape=[
            jax.ShapeDtypeStruct((tokens, 2 * STATE), BF16),
            jax.ShapeDtypeStruct((STATE, tokens), BF16),
        ],
        compiler_params=params(),
        name="maps",
        cost_estimate=cost(3),
    )(state_io, halo, conv_state, *after)


def front_kernel(order, blocks, where_ref, feat_ref, halo_ref, taps_ref, dev_ref, edev_ref, spread_ref, turned_ref, *refs):
    xh_ref, sent_ref, kept_ref, scaled, wide = refs[order:]
    j = pl.program_id(0)
    spread = spread_ref[...]
    wide[...] = dot(dev_ref[...], spread)

    def put_feat(rows, cols, value):
        value = value.astype(BF16)
        xh_ref[rows, cols] = value
        scaled[rows, cols] = (value.astype(F32) * wide[rows, cols]).astype(BF16)

    conv_rows(
        lambda lo, hi, cols: feat_ref[lo:hi, cols], feat_ref.shape[0], halo_ref[...], taps_ref[...].astype(F32), put_feat
    )
    state = dot(turned_ref[...], scaled[...])
    decay = dot(edev_ref[...], spread)[15:16]

    @pl.when(j < blocks)
    def _():
        write_sent(sent_ref, state, decay)

    @pl.when(j >= blocks)
    def _():
        write_kept(kept_ref, state, decay)


def front(chunk, where, features, halo, conv_feat, table, spread, turned, after):
    tokens = features.shape[0]
    start, width = chunk
    half = width // 2
    block = min(512, half)
    blocks = half // block
    base = start // block
    count = conv_feat.shape[0]
    heads2 = spread.shape[0]

    def place(j, where):
        sending = (j < blocks).astype(jnp.int32)
        which = sending * (1 - where[1]) + (1 - sending) * where[1]
        return which * blocks + j - (1 - sending) * blocks

    def cols(j, where):
        return (0, base + place(j, where))

    def same(j, where):
        return (0, 0)

    return pl.pallas_call(
        functools.partial(front_kernel, len(after), blocks),
        grid_spec=pltpu.PrefetchScalarGridSpec(
            num_scalar_prefetch=1,
            grid=(2 * blocks,),
            in_specs=[
                pl.BlockSpec((tokens, block), cols),
                pl.BlockSpec((HALO, block), cols),
                pl.BlockSpec((count, block), cols),
                pl.BlockSpec((tokens, heads2), lambda j, where: (0, DEV)),
                pl.BlockSpec((16, heads2), lambda j, where: (tokens // 16 - 1, EDEV)),
                pl.BlockSpec((heads2, block), cols),
                pl.BlockSpec((STATE, tokens), same),
                *behind(len(after)),
            ],
            out_specs=[
                pl.BlockSpec((tokens, block), lambda j, where: (0, place(j, where))),
                pl.BlockSpec((MSG, block), lambda j, where: (0, jnp.minimum(j, blocks - 1))),
                pl.BlockSpec((KEPT, block), lambda j, where: (0, jnp.maximum(j - blocks, 0))),
            ],
            scratch_shapes=[pltpu.VMEM((tokens, block), BF16), pltpu.VMEM((tokens, block), F32)],
        ),
        out_shape=[
            jax.ShapeDtypeStruct((tokens, width), BF16),
            jax.ShapeDtypeStruct((MSG, half), BF16),
            jax.ShapeDtypeStruct((KEPT, half), F32),
        ],
        compiler_params=params(),
        name="front",
        cost_estimate=cost(4),
    )(where, features, halo, conv_feat, table, table, spread, turned, *after)


def span_kernel(
    first_head, order, xh_ref, map_ref, col_ref, row_ref, table_ref, spread_ref, skips_ref, halves_ref,
    *refs,
):
    y_ref, state = refs[order:]
    width = xh_ref.shape[1]
    head_dim = width // row_ref.shape[0]
    heads2 = spread_ref.shape[0]

    @pl.when(pl.program_id(0) == 0)
    def _():
        state[...] = jnp.zeros_like(state)

    t = lax.broadcasted_iota(jnp.int32, (SPAN, SPAN), 0)
    s = lax.broadcasted_iota(jnp.int32, (SPAN, SPAN), 1)
    first = halves_ref[0:1, :]
    second = halves_ref[1:2, :]
    block = 256
    for k in range(xh_ref.shape[0] // SPAN):
        rows = slice(k * SPAN, (k + 1) * SPAN)
        in_map = map_ref[rows, :STATE]
        out_map = map_ref[rows, STATE:]
        scores = lax.dot_general(out_map, in_map, (((1,), (1,)), ((), ())), preferred_element_type=F32)
        scores = jnp.where(s <= t, scores, 0.0)
        in_turned = in_map.T
        tables = jnp.concatenate([table_ref[rows, :heads2], table_ref[rows, heads2:], skips_ref[...]], axis=0)
        for q in range(width // block):
            cols = slice(q * block, (q + 1) * block)
            feats = xh_ref[rows, cols]
            feats32 = feats.astype(F32)
            wide = dot(tables, spread_ref[:, cols])
            scaled = (feats32 * wide[:SPAN]).astype(BF16)
            ecum = wide[SPAN : 2 * SPAN]
            skip = wide[2 * SPAN : 2 * SPAN + 1]
            pairs = []
            for p in range(block // 128):
                weights = []
                for i in range(2):
                    h = (q * block + p * 128) // head_dim + i
                    gap = col_ref[rows, first_head + h : first_head + h + 1] - row_ref[h : h + 1, rows]
                    weights.append((scores * jnp.exp(jnp.minimum(gap, 0.0))).astype(BF16))
                pair = feats[:, p * 128 : (p + 1) * 128]
                stacked = jnp.concatenate([pair * first, pair * second], axis=0)
                pairs.append(dot(jnp.concatenate(weights, axis=1), stacked))
            diag = jnp.concatenate(pairs, axis=1)
            held = state[:, cols]
            carried = dot(out_map, held.astype(BF16)) * ecum
            y_ref[rows, cols] = (diag + carried + skip * feats32).astype(BF16)
            state[:, cols] = ecum[SPAN - 1 :] * held + dot(in_turned, scaled)


def spans_of(chunk, part, parts, micros, head_dim, xh, both_maps, col, row, table, spread, skips, halves, after):
    tokens = xh.shape[0]
    width = chunk[1] // parts
    index = chunk[0] // width + part
    some = width // head_dim
    heads2 = spread.shape[0]
    tile = 2 * SPAN
    return pl.pallas_call(
        functools.partial(span_kernel, index * some, len(after)),
        grid=(tokens // tile,),
        in_specs=[
            pl.BlockSpec((tile, width), lambda k: (k, part)),
            pl.BlockSpec((tile, 2 * STATE), lambda k: (k, 0)),
            pl.BlockSpec((tile, heads2), lambda k: (k, 0)),
            pl.BlockSpec((some, tile), lambda k: (index, k)),
            pl.BlockSpec((tile, 2 * heads2), lambda k: (k, 0)),
            pl.BlockSpec((heads2, width), lambda k: (0, index)),
            pl.BlockSpec(skips.shape, lambda k: (0, 0)),
            pl.BlockSpec(halves.shape, lambda k: (0, 0)),
            *behind(len(after)),
        ],
        out_specs=pl.BlockSpec((tile, width), lambda k: (k, 0)),
        out_shape=jax.ShapeDtypeStruct((tokens, width), BF16),
        scratch_shapes=[pltpu.VMEM((STATE, width), F32)],
        compiler_params=params(),
        name="spans",
        cost_estimate=cost(micros),
    )(xh, both_maps, col, row, table, spread, skips, halves, *after)


def pair_kernel(where_ref, kept_ref, got_ref, *refs):
    total_ref, sent_ref = refs[-2:]
    kept, kept_decay = read_state(kept_ref)
    got, got_decay = read_state(got_ref)

    def put(first, second, decay):
        total = decay * first + second
        write_kept(total_ref, total, kept_decay * got_decay)
        write_sent(sent_ref, total, kept_decay * got_decay)

    @pl.when(where_ref[1] == 0)
    def _():
        put(kept, got, got_decay)

    @pl.when(where_ref[1] == 1)
    def _():
        put(got, kept, kept_decay)


def inclusive_kernel(total_ref, before_ref, *refs):
    sent_ref = refs[-1]
    total, decay = read_state(total_ref)
    before, before_decay = read_state(before_ref)
    write_sent(sent_ref, total + decay * before, decay * before_decay)


def extend_kernel(before_ref, far_ref, *refs):
    before, decay = read_state(before_ref)
    far, far_decay = read_state(far_ref)
    write_kept(refs[-1], before + decay * far, decay * far_decay)


def last_kernel(where_ref, before_ref, far_ref, kept_ref, got_ref, *refs):
    mine_ref, sent_ref = refs[-2:]
    before, before_decay = read_state(before_ref)
    far, _ = read_state(far_ref)
    carried = before + before_decay * far

    @pl.when(where_ref[1] == 0)
    def _():
        kept, decay = read_state(kept_ref)
        mine_ref[...] = carried.astype(BF16)
        sent_ref[...] = (decay * carried + kept).astype(BF16)

    @pl.when(where_ref[1] == 1)
    def _():
        got, decay = read_state(got_ref)
        mine_ref[...] = (decay * carried + got).astype(BF16)
        sent_ref[...] = carried.astype(BF16)


def join(kernel, name, where, operands, outs, after):
    width = operands[0].shape[1]
    shapes = {
        "kept": jax.ShapeDtypeStruct((KEPT, width), F32),
        "sent": jax.ShapeDtypeStruct((MSG, width), BF16),
        "state": jax.ShapeDtypeStruct((STATE, width), BF16),
    }
    scalars = [] if where is None else [where]
    return pl.pallas_call(
        kernel,
        in_specs=[pl.BlockSpec(memory_space=pltpu.SMEM)] * len(scalars)
        + [pl.BlockSpec(memory_space=pltpu.VMEM)] * len(operands)
        + behind(len(after)),
        out_specs=[pl.BlockSpec(memory_space=pltpu.VMEM)] * len(outs),
        out_shape=[shapes[out] for out in outs],
        compiler_params=params(VMEM_SMALL),
        name=name,
        cost_estimate=cost(0.7),
    )(*scalars, *operands, *after)


def back_kernel(mode, counts, partners, order, where_ref, out_ref, edev_ref, *refs):
    chunks = []
    for pieces in counts:
        chunks.append((refs[:pieces], *refs[pieces : pieces + 5]))
        refs = refs[pieces + 5 :]
    if mode == "rest":
        squares_ref, *refs = refs
    refs = refs[order:]
    o_refs = refs[:partners]
    if mode == "first":
        squares_ref = refs[partners]
    gated, sums = refs[-2:]
    out_map = out_ref[...]
    edev = edev_ref[...]
    rows = out_map.shape[0]
    block = 256
    steps = pl.num_programs(0) // partners
    odd = where_ref[1] == 1
    sums[...] = squares_ref[...] if mode == "rest" else jnp.zeros((rows, 128), F32)
    at = 0
    for y_refs, mine_ref, other_ref, spread_ref, gate_ref, gain_ref in chunks:
        half = mine_ref.shape[1]
        for q in range(2 * half // block):
            cols = slice(q * block, (q + 1) * block)
            inner = slice(q * block % half, q * block % half + block)
            mine = mine_ref[:, inner]
            other = other_ref[:, inner]
            state = jnp.where(odd, other, mine) if q * block < half else jnp.where(odd, mine, other)
            gated[:, at : at + block] = dot(out_map, state) * dot(edev, spread_ref[:, cols])
            y_ref = y_refs[q * block // y_refs[0].shape[1]]
            y_at = q * block % y_refs[0].shape[1]
            for c in range(block // 128):
                y_cols = slice(y_at + c * 128, y_at + (c + 1) * 128)
                to = slice(at + c * 128, at + (c + 1) * 128)
                cols = slice(q * block + c * 128, q * block + (c + 1) * 128)
                gain = gain_ref[:, cols]
                for b in range(rows // 64):
                    part = slice(b * 64, (b + 1) * 64)
                    value = (y_ref[part, y_cols].astype(F32) + gated[part, to]) * silu(gate_ref[part, cols].astype(F32))
                    sums[part, :] = sums[part, :] + value * value
                    gated[part, to] = value * gain
            at += block
    if mode == "first":
        squares_ref[...] = sums[...]
    else:
        width = at if mode == "whole" else 2 * at
        mean = jnp.sum(sums[...], axis=1, keepdims=True) * (1.0 / width)
        scale = lax.rsqrt(mean + EPS)
    for p in range(partners):

        @pl.when(pl.program_id(0) // steps == p)
        def _(o_ref=o_refs[p]):
            if mode == "rest":
                step = pl.program_id(0) - p * steps
                start = pl.multiple_of(step * rows, rows)
                high = scale.astype(BF16).astype(F32)
                parts = [jnp.broadcast_to(part, (rows, 128)).T[:8] for part in (high, scale - high)]
                o_ref[steps * rows :, pl.ds(start, rows)] = jnp.concatenate(parts, axis=0).astype(BF16)
            for q in range(at // block):
                cols = slice(q * block, (q + 1) * block)
                value = gated[:, cols] if mode == "first" else gated[:, cols] * scale
                if mode == "rest":
                    o_ref[pl.ds(start, rows), cols] = value.astype(BF16)
                else:
                    o_ref[:, cols] = value.astype(BF16)


def back(mode, some, where, rows, chunks, both_maps, table, spread, gates, gain_row, squares, after, own=None):
    heads2 = spread.shape[0]
    tile = 128
    steps = rows // tile
    partners = len(some)

    def at(i, where):
        turn = some[0]
        for p in range(1, partners):
            turn = jnp.where(i >= p * steps, some[p], turn)
        return ((where[0] ^ turn) * steps + i % steps, 0)

    specs = [
        pl.BlockSpec((tile, STATE), lambda i, where: (at(i, where)[0], 1)),
        pl.BlockSpec((tile, heads2), lambda i, where: (at(i, where)[0], EDEV)),
    ]
    operands = [both_maps, table]
    total = 0
    for (start, width), ys, mine, other in chunks:
        index = start // width
        half = width // 2
        total += width
        specs += [pl.BlockSpec((tile, y.shape[1]), at) for y in ys]
        specs += [
            pl.BlockSpec((STATE, half), lambda i, where: (0, 0)),
            pl.BlockSpec((STATE, half), lambda i, where: (0, 0)),
            pl.BlockSpec((heads2, width), lambda i, where, index=index: (0, index)),
            pl.BlockSpec((tile, width), lambda i, where, index=index: (at(i, where)[0], index)),
            pl.BlockSpec((1, width), lambda i, where, index=index: (0, index)),
        ]
        operands += [*ys, mine, other, spread, gates, gain_row]
    if mode == "rest":
        specs.append(pl.BlockSpec((tile, 128), lambda i, where: (i, 0)))
        operands.append(squares)
    aliases = {}
    if own is not None and own[2] is not None:
        after = [own[2], *after]
        aliases = {1 + len(operands): partners - 1}
    specs += behind(len(after))
    operands += after
    sent = rows + 16 if mode == "rest" else rows
    part = sent if mode == "rest" else tile

    def part_of(p):
        if mode == "rest":
            return lambda i, where: (0, 0)
        return lambda i, where: (jnp.clip(i - p * steps, 0, steps - 1), 0)

    out_specs = [pl.BlockSpec((part, total), part_of(p)) for p in range(partners)]
    out_shape = [jax.ShapeDtypeStruct((sent, total), BF16)] * partners
    if own is not None:
        group, groups, _ = own
        out_specs[-1] = pl.BlockSpec(
            (tile, total),
            lambda i, where: (jnp.clip(i - (partners - 1) * steps, 0, steps - 1), (where[0] ^ some[-1]) * groups + group),
        )
        out_shape[-1] = jax.ShapeDtypeStruct((rows, groups * total * (gates.shape[0] // rows)), BF16)
    if mode == "first":
        out_specs.append(pl.BlockSpec((tile, 128), lambda i, where: (i, 0)))
        out_shape.append(jax.ShapeDtypeStruct((partners * rows, 128), F32))
    return pl.pallas_call(
        functools.partial(back_kernel, mode, [len(ys) for _, ys, _, _ in chunks], partners, len(after)),
        grid_spec=pltpu.PrefetchScalarGridSpec(
            num_scalar_prefetch=1,
            grid=(partners * steps,),
            in_specs=specs,
            out_specs=out_specs,
            scratch_shapes=[pltpu.VMEM((tile, total), F32), pltpu.VMEM((tile, 128), F32)],
        ),
        out_shape=out_shape,
        input_output_aliases=aliases,
        compiler_params=params(),
        name=f"back_{mode}",
        cost_estimate=cost(1),
    )(where, *operands)


def mark_kernel(order, *refs):
    refs[order][...] = jnp.zeros((8, 128), F32)


def mark(after):
    return pl.pallas_call(
        functools.partial(mark_kernel, len(after)),
        grid=(1,),
        in_specs=behind(len(after)),
        out_specs=pl.BlockSpec((8, 128), lambda i: (0, 0)),
        out_shape=jax.ShapeDtypeStruct((8, 128), F32),
        compiler_params=params(VMEM_SMALL),
        name="mark",
        cost_estimate=cost(200),
    )(*after)


def shifted(value, pairs, steps):
    return lax.ppermute(
        value,
        "ctx",
        [(2 * q + y, 2 * (q + steps) + y) for q in range(pairs - steps) for y in range(2)],
    )


def swapped(value, pairs):
    return lax.ppermute(value, "ctx", [(2 * q + y, 2 * q + 1 - y) for q in range(pairs) for y in range(2)])


class Line:
    def __init__(self):
        self.last = []

    def run(self, make, *args, **kwargs):
        made = make(*args, after=self.last, **kwargs)
        self.last = [made[0] if isinstance(made, (list, tuple)) else made]
        return made


class Exchange:
    def __init__(self, line, where, pairs, sent, kept):
        self.line = line
        self.where = where
        self.pairs = pairs
        self.kept = kept
        self.got = swapped(sent, pairs)

    def pair(self):
        self.total, sent = self.line.run(
            join, pair_kernel, "pair", self.where, [self.kept, self.got], ["kept", "sent"]
        )
        self.before = shifted(sent, self.pairs, 1)
        self.reach = 1

    def double(self):
        (sent,) = self.line.run(join, inclusive_kernel, "inclusive", None, [self.total, self.before], ["sent"])
        self.far = shifted(sent, self.pairs, self.reach + 1)
        self.reach = 2 * self.reach + 1

    def extend(self):
        while self.reach < self.pairs - 1:
            (self.before,) = self.line.run(join, extend_kernel, "extend", None, [self.before, self.far], ["kept"])
            self.double()

    def finish(self):
        self.extend()
        self.mine, sent = self.line.run(
            join, last_kernel, "last", self.where, [self.before, self.far, self.kept, self.got], ["state", "state"]
        )
        self.other = swapped(sent, self.pairs)


def shards(
    features, gates, state_io, step_size, log_decay, conv_feat, conv_state, skip_gain, norm_gain
):
    tokens, channels = features.shape
    heads = step_size.shape[0]
    head_dim = channels // heads
    groups = state_io.shape[2] // STATE
    group_width = channels // groups
    width = group_width // 2
    count = conv_feat.shape[0]
    rim = count - 1
    ctx_size = lax.axis_size("ctx")
    head_size = lax.axis_size("head")
    pairs = ctx_size // 2
    rows = tokens // head_size
    me = lax.axis_index("head").astype(jnp.int32)
    where = jnp.stack([me, lax.axis_index("ctx").astype(jnp.int32) % 2])

    onward = [(i, i + 1) for i in range(ctx_size - 1)]
    pad = HALO - rim
    halo = jnp.pad(lax.ppermute(features[tokens - rim :], "ctx", onward), ((pad, 0), (0, 0)))
    io_halo = jnp.pad(lax.ppermute(state_io[tokens - rim :], "ctx", onward), ((pad, 0), (0, 0), (0, 0)))
    spread = jnp.asarray(spread_table(heads, head_dim), BF16)
    halves = jnp.asarray(np.arange(128)[None, :] // head_dim == np.arange(2)[:, None], BF16)
    col, row, table, skips = decay_tables(log_decay, step_size, skip_gain)
    gain_row = norm_gain[None]

    line = Line()
    chunks = [(0, width), (width, width)] + [(g * group_width, group_width) for g in range(1, groups)]
    of_group = [[0, 1]] + [[g + 1] for g in range(1, groups)]
    group_of = [0, 0] + list(range(1, groups))
    fronts = {}
    maps = {}
    exchanges = {}
    ys = {}

    def run_maps(g):
        maps[g] = line.run(maps_of, g, state_io, io_halo, conv_state)

    def run_front(c):
        made = line.run(
            front, chunks[c], where, features, halo, conv_feat, table, spread, maps[group_of[c]][1]
        )
        fronts[c] = made[0]
        exchanges[c] = Exchange(line, where, pairs, made[1], made[2])

    def run_spans(c, part=0, parts=1, micros=200):
        g = group_of[c]
        made = line.run(
            spans_of, chunks[c], part, parts, micros, head_dim, fronts[c], maps[g][0], col, row, table, spread,
            skips, halves,
        )
        ys.setdefault(c, []).append(made)

    def part(c):
        return (chunks[c], ys[c], exchanges[c].mine, exchanges[c].other)

    partners = list(range(head_size - 1, 1, -1))
    squares = {}
    pieces = {}

    def ship(piece, r):
        return lax.ppermute(piece, "head", [(i, i ^ r) for i in range(head_size)])

    def run_back(mode, some, g, parts, squares, own=None):
        return line.run(
            back, mode, some, where, rows, [part(c) for c in parts], maps[g][0], table, spread, gates, gain_row,
            squares, own=own,
        )

    def arrived(g, index, some):
        line.last += [pieces[g, r][index] for r in some]

    def run_first(g, apart=False):
        squares[g] = []
        for some in [[r] for r in partners] if apart else [partners]:
            *made, square = run_back("first", some, g, [0], None)
            squares[g].append((some, square))
            for r, piece in zip(some, made):
                pieces[g, r] = [ship(piece, r)]

    def run_rest(g):
        for some, square in squares[g]:
            made = run_back("rest", some, g, [1], square)
            for r, piece in zip(some, made):
                pieces[g, r].append(ship(piece, r))

    result = None

    def run_one(g, r):
        (piece,) = run_back("whole", [r], g, of_group[g], None)
        pieces[g, r] = [ship(piece, r)]

    def run_own(g):
        nonlocal result
        before = line.last
        (result,) = run_back("whole", [0], g, of_group[g], None, own=(g, groups, result))
        line.last = before

    def run_put(g, r):
        nonlocal result
        start = (me ^ r) * channels + g * group_width
        zero = jnp.int32(0)
        if len(pieces[g, r]) == 2:
            first, rest = pieces[g, r]
            scale = rest[rows, :rows].astype(F32) + rest[rows + 8, :rows].astype(F32)
            first = (first.astype(F32) * scale[:, None]).astype(BF16)
            result = lax.dynamic_update_slice(result, first, (zero, start))
            result = lax.dynamic_update_slice(result, rest[:rows], (zero, start + width))
        else:
            result = lax.dynamic_update_slice(result, pieces[g, r][0], (zero, start))

    ex = exchanges
    later = range(1, groups)
    run_maps(0)
    run_front(0)
    run_front(1)
    ex[0].pair()
    for g in later:
        run_maps(g)
    ex[0].double()
    ex[1].pair()
    for g in later:
        run_front(g + 1)
    run_spans(0)
    ex[0].finish()
    ex[1].double()
    for g in later:
        ex[g + 1].pair()
    run_first(0, apart=True)
    if groups > 1:
        line.run(mark)
    run_spans(1, micros=1)
    ex[1].finish()
    for g in later:
        ex[g + 1].double()
    for g in later:
        run_spans(g + 1, 0, 2, 1)
    arrived(0, 0, partners)
    run_rest(0)
    for g in later:
        run_spans(g + 1, 1, 2, 1)
        ex[g + 1].finish()
    run_one(0, 1)
    for g in later:
        arrived(0, 1, partners[:1])
        run_one(g, partners[0])
        run_one(g, 1)
        arrived(0, 1, partners[1:])
        for r in partners[1:]:
            run_one(g, r)
    run_own(0)
    for r in [*partners, 1]:
        run_put(0, r)
    for g in later:
        run_own(g)
        for r in [partners[0], 1, *partners[1:]]:
            run_put(g, r)
    return result


def solution(mesh):
    in_specs = (
        P("ctx", "head"),
        P("ctx", "head"),
        P("ctx", None, "head"),
        P("head", "ctx"),
        P("head", "ctx"),
        P(None, "head"),
        P(None, None, "head"),
        P("head"),
        P("head"),
    )
    out_specs = P(("ctx", "head"), None)
    return jax.shard_map(shards, mesh=mesh, in_specs=in_specs, out_specs=out_specs, check_vma=False)
```

profile of v0, /device:TPU:0, one launch (start us, length us, event | category | flops | bytes accessed | tf_op | source)
XLA Modules:
  0.0 208.1 jit_solution(9726519128465236533)
XLA Ops:
  0.7 4.9 %collective-permute-start = (bf16[3,2,512]{2,1,0:T(2,128)(2,1)S(1)}, bf16[3,2,512]{2,1,0:T(2,128)(2,1)S(1)}, u32[]{:S(2)}, u32[]{:S(2)}) collective-permute-start(bf16[3,2,512]{2,1,0:T(2,128)(2,1)S(1)} %slice.24), channel_id=1, source_target_pairs={{0,4},{4,8},{8,12},{12,16},{16,20},{20,24},{24,28},{1,5},{5,9},{9,... | collective-permute-start | bytes 18440 | tf_op jit(solution)/shard_map/ppermute | solution.py:675
  6.4 3.4 %collective-permute-start.1 = (bf16[3,4096]{1,0:T(4,128)(2,1)S(1)}, bf16[3,4096]{1,0:T(4,128)(2,1)S(1)}, u32[]{:S(2)}, u32[]{:S(2)}) collective-permute-start(bf16[3,4096]{1,0:T(4,128)(2,1)S(1)} %slice.25), channel_id=1, source_target_pairs={{0,4},{4,8},{8,12},{12,16},{16,20},{20,24},{24,28},{1,5},{5,9},{9,... | collective-permute-start | bytes 73736 | tf_op jit(solution)/shard_map/ppermute | solution.py:674
  13.9 2.1 %copy-done.50 = bf16[1024,2,512]{2,1,0:T(2,128)(2,1)S(1)} copy-done((bf16[1024,2,512]{2,1,0:T(2,128)(2,1)S(1)}, bf16[1024,2,512]{2,1,0:T(2,128)(2,1)}, u32[]{:S(2)}) %copy-start.50) | copy-done | bytes 2097176
  16.7 2.8 %maps.2 = (bf16[1024,512]{1,0:T(8,128)(2,1)S(1)}, bf16[256,1024]{1,0:T(8,128)(2,1)S(1)}) custom-call(bf16[1024,2,512]{2,1,0:T(2,128)(2,1)S(1)} %copy-done.50, bf16[16,2,512]{2,1,0:T(2,128)(2,1)S(1)} %pad.8.halo_ref, bf16[4,2,512]{2,1,0:T(2,128)(2,1)S(1)} %copy-done.55), custom_call_target="tpu_custom_call" | custom-call | flops 3000000000 | bytes 1 | tf_op jit(solution)/shard_map/maps/pallas_call | solution.py:182
  19.5 7.0 %front.3 = (bf16[1024,1024]{1,0:T(8,128)(2,1)}, bf16[272,512]{1,0:T(8,128)(2,1)S(1)}, f32[264,512]{1,0:T(8,128)S(1)}) custom-call(s32[2]{0:T(128)S(1)} %pad_add_fusion.where_ref, bf16[1024,4096]{1,0:T(8,128)(2,1)} %feat_ref.5, bf16[16,4096]{1,0:T(8,128)(2,1)S(1)} %pad.9.halo_ref, bf16[4,4096]{1,0:T(4,128)(2,1)S(1)} %copy-done.54, ...), custom_call_target="tpu_custom_call" | custom-call | flops 4000000000 | bytes 1 | tf_op jit(solution)/shard_map/front/pallas_call | solution.py:252
  26.5 1.5 collective-permute-start.2
  28.0 6.1 %front.4 = (bf16[1024,1024]{1,0:T(8,128)(2,1)S(1)}, bf16[272,512]{1,0:T(8,128)(2,1)S(1)}, f32[264,512]{1,0:T(8,128)S(1)}) custom-call(s32[2]{0:T(128)S(1)} %pad_add_fusion.where_ref, bf16[1024,4096]{1,0:T(8,128)(2,1)} %feat_ref.5, bf16[16,4096]{1,0:T(8,128)(2,1)S(1)} %pad.9.halo_ref, bf16[4,4096]{1,0:T(4,128)(2,1)S(1)} %copy-done.54, ...), custom_call_target="tpu_custom_call" | custom-call | flops 4000000000 | bytes 1 | tf_op jit(solution)/shard_map/front/pallas_call | solution.py:252
  35.5 3.7 %collective-permute-start.4 = (bf16[272,512]{1,0:T(8,128)(2,1)S(1)}, bf16[272,512]{1,0:T(8,128)(2,1)S(1)}, u32[]{:S(2)}, u32[]{:S(2)}) collective-permute-start(bf16[272,512]{1,0:T(8,128)(2,1)S(1)} %get-tuple-element.50), channel_id=1, source_target_pairs={{0,8},{4,12},{8,16},{12,20},{16,24},{20,28},{1,9},{5,13},{9,17},{1... | collective-permute-start | bytes 835592 | tf_op jit(solution)/shard_map/ppermute | solution.py:600
  39.2 2.8 %maps.3 = (bf16[1024,512]{1,0:T(8,128)(2,1)S(1)}, bf16[256,1024]{1,0:T(8,128)(2,1)S(1)}) custom-call(bf16[1024,2,512]{2,1,0:T(2,128)(2,1)S(1)} %copy-done.51, bf16[16,2,512]{2,1,0:T(2,128)(2,1)S(1)} %pad.8.halo_ref, bf16[4,2,512]{2,1,0:T(2,128)(2,1)S(1)} %copy-done.55, f32[264,512]{1,0:T(8,128)S(1)} %get-tuple-element.45.refs_0_.total_ref), custom_call_target="tpu_custom_call" | custom-call | flops 3000000000 | bytes 1 | tf_op jit(solution)/shard_map/maps/pallas_call | solution.py:182
  42.0 1.7 collective-permute-done.4.before_ref
  45.6 6.1 %collective-permute-start.7 = (bf16[272,512]{1,0:T(8,128)(2,1)}, bf16[272,512]{1,0:T(8,128)(2,1)}, u32[]{:S(2)}, u32[]{:S(2)}) collective-permute-start(bf16[272,512]{1,0:T(8,128)(2,1)} %inclusive.3.refs_0_), channel_id=1, source_target_pairs={{0,16},{4,20},{8,24},{12,28},{1,17},{5,21},{9,25},{13,29},{2,18},{... | collective-permute-start | bytes 835592 | tf_op jit(solution)/shard_map/ppermute | solution.py:600
  51.8 1.4 pair.4
  53.2 3.0 %collective-permute-start.6 = (bf16[272,512]{1,0:T(8,128)(2,1)}, bf16[272,512]{1,0:T(8,128)(2,1)}, u32[]{:S(2)}, u32[]{:S(2)}) collective-permute-start(bf16[272,512]{1,0:T(8,128)(2,1)} %get-tuple-element.58), channel_id=1, source_target_pairs={{0,8},{4,12},{8,16},{12,20},{16,24},{20,28},{1,9},{5,13},{9,17},{1... | collective-permute-start | bytes 835592 | tf_op jit(solution)/shard_map/ppermute | solution.py:600
  56.1 11.3 %front.5 = (bf16[1024,2048]{1,0:T(8,128)(2,1)}, bf16[272,1024]{1,0:T(8,128)(2,1)}, f32[264,1024]{1,0:T(8,128)S(1)}) custom-call(s32[2]{0:T(128)S(1)} %pad_add_fusion.where_ref, bf16[1024,4096]{1,0:T(8,128)(2,1)} %feat_ref.5, bf16[16,4096]{1,0:T(8,128)(2,1)S(1)} %pad.9.halo_ref, bf16[4,4096]{1,0:T(4,128)(2,1)S(1)} %copy-done.54, ...), custom_call_target="tpu_custom_call" | custom-call | flops 4000000000 | bytes 1 | tf_op jit(solution)/shard_map/front/pallas_call | solution.py:252
  67.5 1.5 collective-permute-start.5
  69.0 7.3 %spans.4.refs_0_ = bf16[1024,1024]{1,0:T(8,128)(2,1)S(1)} custom-call(bf16[1024,1024]{1,0:T(8,128)(2,1)} %get-tuple-element.43.refs_0_.xh_ref, bf16[1024,512]{1,0:T(8,128)(2,1)S(1)} %get-tuple-element.40.refs_0_.map_ref.out_ref, f32[1024,128]{1,0:T(8,128)S(1)} %get-tuple-element.53.col_ref, f32[64,1024]{1,0:T(8,128)S(1)} %get-tuple-element.54.row_ref, ...), custom_call_target="tpu_custom_call" | custom-call | flops 199999995904 | bytes 1 | tf_op jit(solution)/shard_map/spans/pallas_call | solution.py:343
  76.3 1.4 last.3
  78.4 1.8 inclusive.4.refs_0_
  80.1 2.0 collective-permute-start.9
  82.1 2.2 %pair.5 = (f32[264,1024]{1,0:T(8,128)S(1)}, bf16[272,1024]{1,0:T(8,128)(2,1)}) custom-call(s32[2]{0:T(128)S(1)} %pad_add_fusion.where_ref, f32[264,1024]{1,0:T(8,128)S(1)} %get-tuple-element.56.kept_ref, bf16[272,1024]{1,0:T(8,128)(2,1)} %collective-permute-done.5.got_ref, bf16[272,512]{1,0:T(8,128)(2,1)} %inclusive.4.refs_0_), custom_call_target="tpu_custom_call" | custom-call | flops 700000000 | bytes 1 | tf_op jit(solution)/shard_map/pair/pallas_call | solution.py:425
  84.3 2.2 %collective-permute-start.8 = (bf16[272,1024]{1,0:T(8,128)(2,1)}, bf16[272,1024]{1,0:T(8,128)(2,1)}, u32[]{:S(2)}, u32[]{:S(2)}) collective-permute-start(bf16[272,1024]{1,0:T(8,128)(2,1)} %get-tuple-element.61), channel_id=1, source_target_pairs={{0,8},{4,12},{8,16},{12,20},{16,24},{20,28},{1,9},{5,13},{9,17},{1... | collective-permute-start | bytes 1671176 | tf_op jit(solution)/shard_map/ppermute | solution.py:600
  86.6 3.1 %back_first.2 = (bf16[256,1024]{1,0:T(8,128)(2,1)}, f32[256,128]{1,0:T(8,128)S(1)}) custom-call(s32[2]{0:T(128)S(1)} %pad_add_fusion.where_ref, bf16[1024,512]{1,0:T(8,128)(2,1)S(1)} %get-tuple-element.40.refs_0_.map_ref.out_ref, bf16[1024,512]{1,0:T(8,128)(2,1)S(1)} %get-tuple-element.38.dev_ref.edev_ref.table_ref, bf16[1024,1024]{1,0:T(8,128)(2,1)} %copy-done.7, ...), custom_call_target="tpu_custom_call" | custom-call | flops 1000000000 | bytes 1 | tf_op jit(solution)/shard_map/back_first/pallas_call | solution.py:565
  89.7 3.1 %back_first.3 = (bf16[256,1024]{1,0:T(8,128)(2,1)}, f32[256,128]{1,0:T(8,128)S(1)}) custom-call(s32[2]{0:T(128)S(1)} %pad_add_fusion.where_ref, bf16[1024,512]{1,0:T(8,128)(2,1)S(1)} %get-tuple-element.40.refs_0_.map_ref.out_ref, bf16[1024,512]{1,0:T(8,128)(2,1)S(1)} %get-tuple-element.38.dev_ref.edev_ref.table_ref, bf16[1024,1024]{1,0:T(8,128)(2,1)} %copy-done.7, ...), custom_call_target="tpu_custom_call" | custom-call | flops 1000000000 | bytes 1 | tf_op jit(solution)/shard_map/back_first/pallas_call | solution.py:565
  92.9 1.4 collective-permute-start.13
  95.6 7.3 %spans.5.refs_0_.refs_6_ = bf16[1024,1024]{1,0:T(8,128)(2,1)S(1)} custom-call(bf16[1024,1024]{1,0:T(8,128)(2,1)} %copy-done.13, bf16[1024,512]{1,0:T(8,128)(2,1)S(1)} %get-tuple-element.40.refs_0_.map_ref.out_ref, f32[1024,128]{1,0:T(8,128)S(1)} %get-tuple-element.53.col_ref, f32[64,1024]{1,0:T(8,128)S(1)} %copy-done.26, ...), custom_call_target="tpu_custom_call" | custom-call | flops 1000000000 | bytes 1 | tf_op jit(solution)/shard_map/spans/pallas_call | solution.py:343
  103.0 1.7 last.4
  104.7 2.2 %collective-permute-start.11 = (bf16[256,512]{1,0:T(8,128)(2,1)S(1)}, bf16[256,512]{1,0:T(8,128)(2,1)S(1)}, u32[]{:S(2)}, u32[]{:S(2)}) collective-permute-start(bf16[256,512]{1,0:T(8,128)(2,1)S(1)} %get-tuple-element.66), channel_id=1, source_target_pairs={{0,4},{4,0},{8,12},{12,8},{16,20},{20,16},{24,28},{28,24},{1,5},{5... | collective-permute-start | bytes 786440 | tf_op jit(solution)/shard_map/ppermute | solution.py:608
  106.9 2.0 inclusive.5.refs_0_
  108.9 2.3 %collective-permute-start.14 = (bf16[272,1024]{1,0:T(8,128)(2,1)}, bf16[272,1024]{1,0:T(8,128)(2,1)}, u32[]{:S(2)}, u32[]{:S(2)}) collective-permute-start(bf16[272,1024]{1,0:T(8,128)(2,1)} %inclusive.5.refs_0_), channel_id=1, source_target_pairs={{0,16},{4,20},{8,24},{12,28},{1,17},{5,21},{9,25},{13,29},{2,18},{... | collective-permute-start | bytes 1671176 | tf_op jit(solution)/shard_map/ppermute | solution.py:600
  111.3 8.2 %spans.6.refs_7_.refs_0_ = bf16[1024,1024]{1,0:T(8,128)(2,1)} custom-call(bf16[1024,2048]{1,0:T(8,128)(2,1)} %get-tuple-element.52.refs_0_.xh_ref, bf16[1024,512]{1,0:T(8,128)(2,1)S(1)} %copy-done.11, f32[1024,128]{1,0:T(8,128)S(1)} %get-tuple-element.53.col_ref, f32[64,1024]{1,0:T(8,128)S(1)} %copy-done.26, ...), custom_call_target="tpu_custom_call" | custom-call | flops 1000000000 | bytes 1 | tf_op jit(solution)/shard_map/spans/pallas_call | solution.py:343
  119.5 3.5 %back_rest.2.refs_7_ = bf16[272,1024]{1,0:T(8,128)(2,1)} custom-call(s32[2]{0:T(128)S(1)} %copy-done.45, bf16[1024,512]{1,0:T(8,128)(2,1)S(1)} %get-tuple-element.40.refs_0_.map_ref.out_ref, bf16[1024,512]{1,0:T(8,128)(2,1)S(1)} %get-tuple-element.38.dev_ref.edev_ref.table_ref, bf16[1024,1024]{1,0:T(8,128)(2,1)} %copy-done.6, ...), custom_call_target="tpu_custom_call" | custom-call | flops 1000000000 | bytes 1 | tf_op jit(solution)/shard_map/back_rest/pallas_call | solution.py:565
  124.2 3.6 %back_rest.3.refs_0_ = bf16[272,1024]{1,0:T(8,128)(2,1)} custom-call(s32[2]{0:T(128)S(1)} %copy-done.45, bf16[1024,512]{1,0:T(8,128)(2,1)S(1)} %get-tuple-element.40.refs_0_.map_ref.out_ref, bf16[1024,512]{1,0:T(8,128)(2,1)S(1)} %get-tuple-element.38.dev_ref.edev_ref.table_ref, bf16[1024,1024]{1,0:T(8,128)(2,1)} %copy-done.6, ...), custom_call_target="tpu_custom_call" | custom-call | flops 1000000000 | bytes 1 | tf_op jit(solution)/shard_map/back_rest/pallas_call | solution.py:565
  130.5 8.4 %spans.7.refs_0_.refs_1_ = bf16[1024,1024]{1,0:T(8,128)(2,1)} custom-call(bf16[1024,2048]{1,0:T(8,128)(2,1)} %get-tuple-element.52.refs_0_.xh_ref, bf16[1024,512]{1,0:T(8,128)(2,1)S(1)} %copy-done.12, f32[1024,128]{1,0:T(8,128)S(1)} %copy-done.15, f32[64,1024]{1,0:T(8,128)S(1)} %copy-done.27, bf16[1024,512]{1,0:T(8,128)(2,1)S(1)} %copy-done.3, ...), custom_call_target="tpu_custom_call" | custom-call | flops 1000000000 | bytes 1 | tf_op jit(solution)/shard_map/spans/pallas_call | solution.py:343
  138.9 1.6 copy-done.5
  140.5 1.8 last.5
  142.7 3.5 %back_whole.6.refs_7_ = bf16[256,2048]{1,0:T(8,128)(2,1)S(1)} custom-call(s32[2]{0:T(128)S(1)} %copy-done.45, bf16[1024,512]{1,0:T(8,128)(2,1)S(1)} %copy-done.9, bf16[1024,512]{1,0:T(8,128)(2,1)S(1)} %copy-done.4, bf16[1024,1024]{1,0:T(8,128)(2,1)} %copy-done.7, bf16[256,512]{1,0:T(8,128)(2,1)S(1)} %copy-done.17, bf16[256,512]{1,0:T(8,128)(2,1)S(1)} %copy-done.19, ...), custom_call_target="tpu_custom_call" | custom-call | flops 1000000000 | bytes 1 | tf_op jit(solution)/shard_map/back_whole/pallas_call | solution.py:565
  147.0 3.2 %collective-permute-done.17.refs_8_ = bf16[272,1024]{1,0:T(8,128)(2,1)} collective-permute-done((bf16[272,1024]{1,0:T(8,128)(2,1)}, bf16[272,1024]{1,0:T(8,128)(2,1)}, u32[]{:S(2)}, u32[]{:S(2)}) %collective-permute-start.17) | collective-permute-done | bytes 557088 | tf_op jit(solution)/shard_map/ppermute | solution.py:716
  150.9 5.5 %collective-permute-done.15.refs_3_ = bf16[256,1024]{1,0:T(8,128)(2,1)S(1)} collective-permute-done((bf16[256,1024]{1,0:T(8,128)(2,1)S(1)}, bf16[256,1024]{1,0:T(8,128)(2,1)S(1)}, u32[]{:S(2)}, u32[]{:S(2)}) %collective-permute-start.15) | collective-permute-done | bytes 524320 | tf_op jit(solution)/shard_map/ppermute | solution.py:608
  156.4 3.5 %back_whole.7.refs_7_ = bf16[256,2048]{1,0:T(8,128)(2,1)S(1)} custom-call(s32[2]{0:T(128)S(1)} %copy-done.45, bf16[1024,512]{1,0:T(8,128)(2,1)S(1)} %copy-done.12, bf16[1024,512]{1,0:T(8,128)(2,1)S(1)} %copy-done.4, bf16[1024,1024]{1,0:T(8,128)(2,1)} %spans.6.refs_7_.refs_0_, bf16[1024,1024]{1,0:T(8,128)(2,1)} %spans.7.refs_0_.refs_1_, ...), custom_call_target="tpu_custom_call" | custom-call | flops 1000000000 | bytes 1 | tf_op jit(solution)/shard_map/back_whole/pallas_call | solution.py:565
  160.9 3.5 %back_whole.8.refs_7_ = bf16[256,2048]{1,0:T(8,128)(2,1)S(1)} custom-call(s32[2]{0:T(128)S(1)} %copy-done.45, bf16[1024,512]{1,0:T(8,128)(2,1)S(1)} %copy-done.12, bf16[1024,512]{1,0:T(8,128)(2,1)S(1)} %copy-done.4, bf16[1024,1024]{1,0:T(8,128)(2,1)} %spans.6.refs_7_.refs_0_, bf16[1024,1024]{1,0:T(8,128)(2,1)} %spans.7.refs_0_.refs_1_, ...), custom_call_target="tpu_custom_call" | custom-call | flops 1000000000 | bytes 1 | tf_op jit(solution)/shard_map/back_whole/pallas_call | solution.py:565
  165.3 3.5 %back_whole.9.refs_12_.refs_8_ = bf16[256,2048]{1,0:T(8,128)(2,1)S(1)} custom-call(s32[2]{0:T(128)S(1)} %copy-done.45, bf16[1024,512]{1,0:T(8,128)(2,1)S(1)} %copy-done.12, bf16[1024,512]{1,0:T(8,128)(2,1)S(1)} %copy-done.4, bf16[1024,1024]{1,0:T(8,128)(2,1)} %spans.6.refs_7_.refs_0_, bf16[1024,1024]{1,0:T(8,128)(2,1)} %spans.7.refs_0_.refs_1_, ...), custom_call_target="tpu_custom_call" | custom-call | flops 1000000000 | bytes 1 | tf_op jit(solution)/shard_map/back_whole/pallas_call | solution.py:565
  169.5 4.2 %back_whole.10 = bf16[256,16384]{1,0:T(8,128)(2,1)} custom-call(s32[2]{0:T(128)S(1)} %copy-done.45, bf16[1024,512]{1,0:T(8,128)(2,1)S(1)} %copy-done.9, bf16[1024,512]{1,0:T(8,128)(2,1)S(1)} %copy-done.4, bf16[1024,1024]{1,0:T(8,128)(2,1)} %copy-done.7, bf16[256,512]{1,0:T(8,128)(2,1)S(1)} %copy-done.17, bf16[256,512]{1,0:T(8,128)(2,1)S(1)} %copy-done.19, ...), custom_call_target="tpu_custom_call" | custom-call | flops 1000000000 | bytes 1 | tf_op jit(solution)/shard_map/back_whole/pallas_call | solution.py:565
  173.7 2.0 fusion
  175.7 1.9 slice_dynamic-update-slice_fusion.1
  177.5 2.0 fusion.1
  179.5 1.9 slice_dynamic-update-slice_fusion
  182.5 4.3 %back_whole.11 = bf16[256,16384]{1,0:T(8,128)(2,1)} custom-call(s32[2]{0:T(128)S(1)} %copy-done.45, bf16[1024,512]{1,0:T(8,128)(2,1)S(1)} %copy-done.12, bf16[1024,512]{1,0:T(8,128)(2,1)S(1)} %copy-done.4, bf16[1024,1024]{1,0:T(8,128)(2,1)} %spans.6.refs_7_.refs_0_, bf16[1024,1024]{1,0:T(8,128)(2,1)} %spans.7.refs_0_.refs_1_, ...), custom_call_target="tpu_custom_call", output_to_operand_aliasing={{}: (10, {})} | custom-call | flops 1000000000 | bytes 1 | tf_op jit(solution)/shard_map/back_whole/pallas_call | solution.py:565
  188.9 18.1 %collective-permute-done.21 = bf16[256,2048]{1,0:T(8,128)(2,1)S(1)} collective-permute-done((bf16[256,2048]{1,0:T(8,128)(2,1)S(1)}, bf16[256,2048]{1,0:T(8,128)(2,1)S(1)}, u32[]{:S(2)}, u32[]{:S(2)}) %collective-permute-start.21) | collective-permute-done | bytes 1048608 | tf_op jit(solution)/shard_map/ppermute | solution.py:716
  (155 shorter events, 24.0 us)
Async XLA Ops:
  0.7 13.1 %collective-permute-start = (bf16[3,2,512]{2,1,0:T(2,128)(2,1)S(1)}, bf16[3,2,512]{2,1,0:T(2,128)(2,1)S(1)}, u32[]{:S(2)}, u32[]{:S(2)}) collective-permute-start(bf16[3,2,512]{2,1,0:T(2,128)(2,1)S(1)} %slice.24), channel_id=1, source_target_pairs={{0,4},{4,8},{8,12},{12,16},{16,20},{20,24},{24,28},{1,5},{5,9},{9,... | collective-permute-start | bytes 18440 | tf_op jit(solution)/shard_map/ppermute | solution.py:675
  6.4 13.0 %collective-permute-start.1 = (bf16[3,4096]{1,0:T(4,128)(2,1)S(1)}, bf16[3,4096]{1,0:T(4,128)(2,1)S(1)}, u32[]{:S(2)}, u32[]{:S(2)}) collective-permute-start(bf16[3,4096]{1,0:T(4,128)(2,1)S(1)} %slice.25), channel_id=1, source_target_pairs={{0,4},{4,8},{8,12},{12,16},{16,20},{20,24},{24,28},{1,5},{5,9},{9,... | collective-permute-start | bytes 73736 | tf_op jit(solution)/shard_map/ppermute | solution.py:674
  13.7 55.3 %copy-start.25 = (f32[64,1024]{1,0:T(8,128)}, f32[64,1024]{1,0:T(8,128)S(1)}, u32[]{:S(2)}) copy-start(f32[64,1024]{1,0:T(8,128)S(1)} %get-tuple-element.54.row_ref) | copy-start | bytes 786436
  13.7 55.3 %copy-start.46 = (bf16[16,128]{1,0:T(8,128)(2,1)}, bf16[16,128]{1,0:T(8,128)(2,1)S(1)}, u32[]{:S(2)}) copy-start(bf16[16,128]{1,0:T(8,128)(2,1)S(1)} %get-tuple-element.55.skips_ref) | copy-start | bytes 12292
  13.7 97.5 %copy-start.14 = (f32[1024,128]{1,0:T(8,128)}, f32[1024,128]{1,0:T(8,128)S(1)}, u32[]{:S(2)}) copy-start(f32[1024,128]{1,0:T(8,128)S(1)} %get-tuple-element.53.col_ref) | copy-start | bytes 1572868
  13.7 110.4 %copy-start.2 = (bf16[1024,512]{1,0:T(8,128)(2,1)}, bf16[1024,512]{1,0:T(8,128)(2,1)S(1)}, u32[]{:S(2)}) copy-start(bf16[1024,512]{1,0:T(8,128)(2,1)S(1)} %get-tuple-element.38.dev_ref.edev_ref.table_ref) | copy-start | bytes 3145732
  13.8 75.9 %copy-start.44 = (s32[2]{0:T(128)}, s32[2]{0:T(128)S(1)}, u32[]{:S(2)}) copy-start(s32[2]{0:T(128)S(1)} %pad_add_fusion.where_ref) | copy-start | bytes 28
  19.5 104.7 %copy-start.8 = (bf16[1024,512]{1,0:T(8,128)(2,1)}, bf16[1024,512]{1,0:T(8,128)(2,1)S(1)}, u32[]{:S(2)}) copy-start(bf16[1024,512]{1,0:T(8,128)(2,1)S(1)} %get-tuple-element.40.refs_0_.map_ref.out_ref) | copy-start | bytes 3145732
  26.5 8.3 %collective-permute-start.2 = (bf16[272,512]{1,0:T(8,128)(2,1)S(1)}, bf16[272,512]{1,0:T(8,128)(2,1)S(1)}, u32[]{:S(2)}, u32[]{:S(2)}) collective-permute-start(bf16[272,512]{1,0:T(8,128)(2,1)S(1)} %get-tuple-element.42), channel_id=1, source_target_pairs={{0,4},{4,0},{8,12},{12,8},{16,20},{20,16},{24,28},{28,24},{1,5},{5... | collective-permute-start | bytes 835592 | tf_op jit(solution)/shard_map/ppermute | solution.py:608
  28.0 11.2 %copy-start.51 = (bf16[1024,2,512]{2,1,0:T(2,128)(2,1)S(1)}, bf16[1024,2,512]{2,1,0:T(2,128)(2,1)}, u32[]{:S(2)}) copy-start(bf16[1024,2,512]{2,1,0:T(2,128)(2,1)} %io_ref.3) | copy-start | bytes 6291460
  34.1 19.0 %copy-start.13 = (bf16[1024,1024]{1,0:T(8,128)(2,1)}, bf16[1024,1024]{1,0:T(8,128)(2,1)S(1)}, u32[]{:S(2)}) copy-start(bf16[1024,1024]{1,0:T(8,128)(2,1)S(1)} %get-tuple-element.44.refs_0_.xh_ref) | copy-start | bytes 6291460
  34.1 19.0 %copy-start.38 = (f32[264,512]{1,0:T(8,128)}, f32[264,512]{1,0:T(8,128)S(1)}, u32[]{:S(2)}) copy-start(f32[264,512]{1,0:T(8,128)S(1)} %get-tuple-element.48.kept_ref) | copy-start | bytes 1622020
  34.1 17.6 %collective-permute-start.3 = (bf16[272,512]{1,0:T(8,128)(2,1)S(1)}, bf16[272,512]{1,0:T(8,128)(2,1)S(1)}, u32[]{:S(2)}, u32[]{:S(2)}) collective-permute-start(bf16[272,512]{1,0:T(8,128)(2,1)S(1)} %get-tuple-element.49), channel_id=1, source_target_pairs={{0,4},{4,0},{8,12},{12,8},{16,20},{20,16},{24,28},{28,24},{1,5},{5... | collective-permute-start | bytes 835592 | tf_op jit(solution)/shard_map/ppermute | solution.py:608
  35.5 8.3 %collective-permute-start.4 = (bf16[272,512]{1,0:T(8,128)(2,1)S(1)}, bf16[272,512]{1,0:T(8,128)(2,1)S(1)}, u32[]{:S(2)}, u32[]{:S(2)}) collective-permute-start(bf16[272,512]{1,0:T(8,128)(2,1)S(1)} %get-tuple-element.50), channel_id=1, source_target_pairs={{0,8},{4,12},{8,16},{12,20},{16,24},{20,28},{1,9},{5,13},{9,17},{1... | collective-permute-start | bytes 835592 | tf_op jit(solution)/shard_map/ppermute | solution.py:600
  43.7 23.7 %copy-start.42 = (bf16[272,512]{1,0:T(8,128)(2,1)}, bf16[272,512]{1,0:T(8,128)(2,1)S(1)}, u32[]{:S(2)}) copy-start(bf16[272,512]{1,0:T(8,128)(2,1)S(1)} %collective-permute-done.4.before_ref) | copy-start | bytes 835588
  45.6 30.7 %collective-permute-start.7 = (bf16[272,512]{1,0:T(8,128)(2,1)}, bf16[272,512]{1,0:T(8,128)(2,1)}, u32[]{:S(2)}, u32[]{:S(2)}) collective-permute-start(bf16[272,512]{1,0:T(8,128)(2,1)} %inclusive.3.refs_0_), channel_id=1, source_target_pairs={{0,16},{4,20},{8,24},{12,28},{1,17},{5,21},{9,25},{13,29},{2,18},{... | collective-permute-start | bytes 835592 | tf_op jit(solution)/shard_map/ppermute | solution.py:600
  51.8 15.7 %copy-start.40 = (bf16[272,512]{1,0:T(8,128)(2,1)}, bf16[272,512]{1,0:T(8,128)(2,1)S(1)}, u32[]{:S(2)}) copy-start(bf16[272,512]{1,0:T(8,128)(2,1)S(1)} %collective-permute-done.3.got_ref) | copy-start | bytes 835588
  51.8 17.2 %copy-start.48 = (bf16[2,128]{1,0:T(2,128)(2,1)S(1)}, bf16[2,128]{1,0:T(2,128)(2,1)}, u32[]{:S(2)}) copy-start(bf16[2,128]{1,0:T(2,128)(2,1)} %constant.48.clone.halves_ref) | copy-start | bytes 1540
  53.2 25.2 %collective-permute-start.6 = (bf16[272,512]{1,0:T(8,128)(2,1)}, bf16[272,512]{1,0:T(8,128)(2,1)}, u32[]{:S(2)}, u32[]{:S(2)}) collective-permute-start(bf16[272,512]{1,0:T(8,128)(2,1)} %get-tuple-element.58), channel_id=1, source_target_pairs={{0,8},{4,12},{8,16},{12,20},{16,24},{20,28},{1,9},{5,13},{9,17},{1... | collective-permute-start | bytes 835592 | tf_op jit(solution)/shard_map/ppermute | solution.py:600
  67.5 14.7 %copy-start.34 = (f32[264,1024]{1,0:T(8,128)}, f32[264,1024]{1,0:T(8,128)S(1)}, u32[]{:S(2)}) copy-start(f32[264,1024]{1,0:T(8,128)S(1)} %get-tuple-element.56.kept_ref) | copy-start | bytes 3244036
  67.5 14.7 %collective-permute-start.5 = (bf16[272,1024]{1,0:T(8,128)(2,1)}, bf16[272,1024]{1,0:T(8,128)(2,1)}, u32[]{:S(2)}, u32[]{:S(2)}) collective-permute-start(bf16[272,1024]{1,0:T(8,128)(2,1)} %get-tuple-element.57), channel_id=1, source_target_pairs={{0,4},{4,0},{8,12},{12,8},{16,20},{20,16},{24,28},{28,24},{1,5},{5... | collective-permute-start | bytes 1671176 | tf_op jit(solution)/shard_map/ppermute | solution.py:608
  76.3 10.3 %copy-start.7 = (bf16[1024,1024]{1,0:T(8,128)(2,1)}, bf16[1024,1024]{1,0:T(8,128)(2,1)S(1)}, u32[]{:S(2)}) copy-start(bf16[1024,1024]{1,0:T(8,128)(2,1)S(1)} %spans.4.refs_0_) | copy-start | bytes 6291460
  76.3 10.3 %copy-start.28 = (f32[4096]{0:T(1024)S(1)}, f32[4096]{0:T(1024)}, u32[]{:S(2)}) copy-start(f32[4096]{0:T(1024)} %param.19) | copy-start | bytes 49156
  77.7 12.0 %copy-start.16 = (bf16[256,512]{1,0:T(8,128)(2,1)}, bf16[256,512]{1,0:T(8,128)(2,1)S(1)}, u32[]{:S(2)}) copy-start(bf16[256,512]{1,0:T(8,128)(2,1)S(1)} %get-tuple-element.59.refs_0_.refs_1_) | copy-start | bytes 786436
  77.7 8.8 %collective-permute-start.10 = (bf16[256,512]{1,0:T(8,128)(2,1)S(1)}, bf16[256,512]{1,0:T(8,128)(2,1)S(1)}, u32[]{:S(2)}, u32[]{:S(2)}) collective-permute-start(bf16[256,512]{1,0:T(8,128)(2,1)S(1)} %get-tuple-element.62), channel_id=1, source_target_pairs={{0,4},{4,0},{8,12},{12,8},{16,20},{20,16},{24,28},{28,24},{1,5},{5... | collective-permute-start | bytes 786440 | tf_op jit(solution)/shard_map/ppermute | solution.py:608
  80.1 22.8 %collective-permute-start.9 = (bf16[272,512]{1,0:T(8,128)(2,1)}, bf16[272,512]{1,0:T(8,128)(2,1)}, u32[]{:S(2)}, u32[]{:S(2)}) collective-permute-start(bf16[272,512]{1,0:T(8,128)(2,1)} %inclusive.4.refs_0_), channel_id=1, source_target_pairs={{0,16},{4,20},{8,24},{12,28},{1,17},{5,21},{9,25},{13,29},{2,18},{... | collective-permute-start | bytes 835592 | tf_op jit(solution)/shard_map/ppermute | solution.py:600
  84.3 22.6 %collective-permute-start.8 = (bf16[272,1024]{1,0:T(8,128)(2,1)}, bf16[272,1024]{1,0:T(8,128)(2,1)}, u32[]{:S(2)}, u32[]{:S(2)}) collective-permute-start(bf16[272,1024]{1,0:T(8,128)(2,1)} %get-tuple-element.61), channel_id=1, source_target_pairs={{0,8},{4,12},{8,16},{12,20},{16,24},{20,28},{1,9},{5,13},{9,17},{1... | collective-permute-start | bytes 1671176 | tf_op jit(solution)/shard_map/ppermute | solution.py:600
  89.7 29.7 %collective-permute-start.12 = (bf16[256,1024]{1,0:T(8,128)(2,1)}, bf16[256,1024]{1,0:T(8,128)(2,1)}, u32[]{:S(2)}, u32[]{:S(2)}) collective-permute-start(bf16[256,1024]{1,0:T(8,128)(2,1)} %get-tuple-element.63.refs_6_), channel_id=1, source_target_pairs={{0,3},{1,2},{2,1},{3,0},{4,7},{5,6},{6,5},{7,4},{8,11},{9,10},{10,... | collective-permute-start | bytes 1572872 | tf_op jit(solution)/shard_map/ppermute | solution.py:716
  92.9 26.6 %collective-permute-start.13 = (bf16[256,1024]{1,0:T(8,128)(2,1)}, bf16[256,1024]{1,0:T(8,128)(2,1)}, u32[]{:S(2)}, u32[]{:S(2)}) collective-permute-start(bf16[256,1024]{1,0:T(8,128)(2,1)} %get-tuple-element.64.refs_0_), channel_id=1, source_target_pairs={{0,2},{1,3},{2,0},{3,1},{4,6},{5,7},{6,4},{7,5},{8,10},{9,11},{10,... | collective-permute-start | bytes 1572872 | tf_op jit(solution)/shard_map/ppermute | solution.py:716
  95.6 11.3 %copy-start.37 = (f32[264,1024]{1,0:T(8,128)S(1)}, f32[264,1024]{1,0:T(8,128)}, u32[]{:S(2)}) copy-start(f32[264,1024]{1,0:T(8,128)} %copy-done.36) | copy-start | bytes 3244036
  95.6 15.7 %copy-start.11 = (bf16[1024,512]{1,0:T(8,128)(2,1)S(1)}, bf16[1024,512]{1,0:T(8,128)(2,1)}, u32[]{:S(2)}) copy-start(bf16[1024,512]{1,0:T(8,128)(2,1)} %copy-done.10) | copy-start | bytes 3145732
  103.0 16.5 %copy-start.6 = (bf16[1024,1024]{1,0:T(8,128)(2,1)}, bf16[1024,1024]{1,0:T(8,128)(2,1)S(1)}, u32[]{:S(2)}) copy-start(bf16[1024,1024]{1,0:T(8,128)(2,1)S(1)} %spans.5.refs_0_.refs_6_) | copy-start | bytes 6291460
  104.7 14.8 %collective-permute-start.11 = (bf16[256,512]{1,0:T(8,128)(2,1)S(1)}, bf16[256,512]{1,0:T(8,128)(2,1)S(1)}, u32[]{:S(2)}, u32[]{:S(2)}) collective-permute-start(bf16[256,512]{1,0:T(8,128)(2,1)S(1)} %get-tuple-element.66), channel_id=1, source_target_pairs={{0,4},{4,0},{8,12},{12,8},{16,20},{20,16},{24,28},{28,24},{1,5},{5... | collective-permute-start | bytes 786440 | tf_op jit(solution)/shard_map/ppermute | solution.py:608
  108.9 30.0 %collective-permute-start.14 = (bf16[272,1024]{1,0:T(8,128)(2,1)}, bf16[272,1024]{1,0:T(8,128)(2,1)}, u32[]{:S(2)}, u32[]{:S(2)}) collective-permute-start(bf16[272,1024]{1,0:T(8,128)(2,1)} %inclusive.5.refs_0_), channel_id=1, source_target_pairs={{0,16},{4,20},{8,24},{12,28},{1,17},{5,21},{9,25},{13,29},{2,18},{... | collective-permute-start | bytes 1671176 | tf_op jit(solution)/shard_map/ppermute | solution.py:600
  123.0 23.3 %collective-permute-start.16 = (bf16[272,1024]{1,0:T(8,128)(2,1)}, bf16[272,1024]{1,0:T(8,128)(2,1)}, u32[]{:S(2)}, u32[]{:S(2)}) collective-permute-start(bf16[272,1024]{1,0:T(8,128)(2,1)} %back_rest.2.refs_7_), channel_id=1, source_target_pairs={{0,3},{1,2},{2,1},{3,0},{4,7},{5,6},{6,5},{7,4},{8,11},{9,10},{10,... | collective-permute-start | bytes 1671176 | tf_op jit(solution)/shard_map/ppermute | solution.py:716
  124.2 18.5 %copy-start.17 = (bf16[256,512]{1,0:T(8,128)(2,1)S(1)}, bf16[256,512]{1,0:T(8,128)(2,1)}, u32[]{:S(2)}) copy-start(bf16[256,512]{1,0:T(8,128)(2,1)} %copy-done.16) | copy-start | bytes 786436
  124.2 18.5 %copy-start.19 = (bf16[256,512]{1,0:T(8,128)(2,1)S(1)}, bf16[256,512]{1,0:T(8,128)(2,1)}, u32[]{:S(2)}) copy-start(bf16[256,512]{1,0:T(8,128)(2,1)} %copy-done.18) | copy-start | bytes 786436
  127.7 15.0 %copy-start.29 = (f32[4096]{0:T(1024)S(1)}, f32[4096]{0:T(1024)}, u32[]{:S(2)}) copy-start(f32[4096]{0:T(1024)} %param.19) | copy-start | bytes 49156
  127.7 22.4 %collective-permute-start.17 = (bf16[272,1024]{1,0:T(8,128)(2,1)}, bf16[272,1024]{1,0:T(8,128)(2,1)}, u32[]{:S(2)}, u32[]{:S(2)}) collective-permute-start(bf16[272,1024]{1,0:T(8,128)(2,1)} %back_rest.3.refs_0_), channel_id=1, source_target_pairs={{0,2},{1,3},{2,0},{3,1},{4,6},{5,7},{6,4},{7,5},{8,10},{9,11},{10,... | collective-permute-start | bytes 1671176 | tf_op jit(solution)/shard_map/ppermute | solution.py:716
  130.5 12.3 %copy-start.4 = (bf16[1024,512]{1,0:T(8,128)(2,1)S(1)}, bf16[1024,512]{1,0:T(8,128)(2,1)}, u32[]{:S(2)}) copy-start(bf16[1024,512]{1,0:T(8,128)(2,1)} %copy-done.2) | copy-start | bytes 3145732
  130.5 12.3 %copy-start.9 = (bf16[1024,512]{1,0:T(8,128)(2,1)S(1)}, bf16[1024,512]{1,0:T(8,128)(2,1)}, u32[]{:S(2)}) copy-start(bf16[1024,512]{1,0:T(8,128)(2,1)} %copy-done.8) | copy-start | bytes 3145732
  130.5 12.3 %copy-start.21 = (bf16[256,512]{1,0:T(8,128)(2,1)S(1)}, bf16[256,512]{1,0:T(8,128)(2,1)}, u32[]{:S(2)}) copy-start(bf16[256,512]{1,0:T(8,128)(2,1)} %copy-done.20) | copy-start | bytes 786436
  142.3 14.1 %collective-permute-start.15 = (bf16[256,1024]{1,0:T(8,128)(2,1)S(1)}, bf16[256,1024]{1,0:T(8,128)(2,1)S(1)}, u32[]{:S(2)}, u32[]{:S(2)}) collective-permute-start(bf16[256,1024]{1,0:T(8,128)(2,1)S(1)} %get-tuple-element.70), channel_id=1, source_target_pairs={{0,4},{4,0},{8,12},{12,8},{16,20},{20,16},{24,28},{28,24},{1,5},{5... | collective-permute-start | bytes 1572872 | tf_op jit(solution)/shard_map/ppermute | solution.py:608
  146.2 10.2 %copy-start.23 = (bf16[256,2048]{1,0:T(8,128)(2,1)}, bf16[256,2048]{1,0:T(8,128)(2,1)S(1)}, u32[]{:S(2)}) copy-start(bf16[256,2048]{1,0:T(8,128)(2,1)S(1)} %back_whole.6.refs_7_) | copy-start | bytes 3145732
  146.2 35.2 %collective-permute-start.18 = (bf16[256,2048]{1,0:T(8,128)(2,1)S(1)}, bf16[256,2048]{1,0:T(8,128)(2,1)S(1)}, u32[]{:S(2)}, u32[]{:S(2)}) collective-permute-start(bf16[256,2048]{1,0:T(8,128)(2,1)S(1)} %back_whole.6.refs_7_), channel_id=1, source_target_pairs={{0,1},{1,0},{2,3},{3,2},{4,5},{5,4},{6,7},{7,6},{8,9},{9,8},{10,11... | collective-permute-start | bytes 3145736 | tf_op jit(solution)/shard_map/ppermute | solution.py:716
  159.9 26.9 %collective-permute-start.19 = (bf16[256,2048]{1,0:T(8,128)(2,1)S(1)}, bf16[256,2048]{1,0:T(8,128)(2,1)S(1)}, u32[]{:S(2)}, u32[]{:S(2)}) collective-permute-start(bf16[256,2048]{1,0:T(8,128)(2,1)S(1)} %back_whole.7.refs_7_), channel_id=1, source_target_pairs={{0,3},{1,2},{2,1},{3,0},{4,7},{5,6},{6,5},{7,4},{8,11},{9,10},{10,... | collective-permute-start | bytes 3145736 | tf_op jit(solution)/shard_map/ppermute | solution.py:716
  164.4 23.5 %collective-permute-start.20 = (bf16[256,2048]{1,0:T(8,128)(2,1)S(1)}, bf16[256,2048]{1,0:T(8,128)(2,1)S(1)}, u32[]{:S(2)}, u32[]{:S(2)}) collective-permute-start(bf16[256,2048]{1,0:T(8,128)(2,1)S(1)} %back_whole.8.refs_7_), channel_id=1, source_target_pairs={{0,1},{1,0},{2,3},{3,2},{4,5},{5,4},{6,7},{7,6},{8,9},{9,8},{10,11... | collective-permute-start | bytes 3145736 | tf_op jit(solution)/shard_map/ppermute | solution.py:716
  168.9 38.1 %collective-permute-start.21 = (bf16[256,2048]{1,0:T(8,128)(2,1)S(1)}, bf16[256,2048]{1,0:T(8,128)(2,1)S(1)}, u32[]{:S(2)}, u32[]{:S(2)}) collective-permute-start(bf16[256,2048]{1,0:T(8,128)(2,1)S(1)} %back_whole.9.refs_12_.refs_8_), channel_id=1, source_target_pairs={{0,2},{1,3},{2,0},{3,1},{4,6},{5,7},{6,4},{7,5},{8,10},{9,11},{10,... | collective-permute-start | bytes 3145736 | tf_op jit(solution)/shard_map/ppermute | solution.py:716
  (31 other events, 130.2 us)
where the time goes:
time: 210 us; the launch traced here: 208 us
  Pallas kernels  112 us (53%)
  starting transfers between devices  38.4 us (18%)
  waiting for transfers between devices  28.5 us (14%)
  local copies, waits for them, and re-layouts  23 us (11%)
  other arithmetic  5.43 us (3%)
    pallas_call x10, Pallas kernels, back(): pl.pallas_call(functools.partial(back_kernel, mode, [len(ys) for _, ys, _...  35.9 us
    pallas_call x4, Pallas kernels, spans_of(): pl.pallas_call(functools.partial(span_kernel, index * some, len(after)),...  31.2 us
    pallas_call x3, Pallas kernels, front(): pl.pallas_call(functools.partial(front_kernel, len(after), blocks), grid_...  24.4 us
    ppermute x8, waiting for transfers between devices, ship(): return lax.ppermute(piece, 'head', [(i, i ^ r) for i in range(head_size)])  21.3 us
    ppermute x6, starting transfers between devices, shifted(): lax.ppermute(value, 'ctx', [(2 * q + y, 2 * (q + steps) + y) for q in ran...  19.3 us
    pallas_call x9, Pallas kernels, join(): pl.pallas_call(kernel, in_specs=[pl.BlockSpec(memory_space=pltpu.SMEM)] *...  13.7 us
    unnamed x114, local copies, waits for them, and re-layouts  13.4 us
    ppermute x6, starting transfers between devices, swapped(): lax.ppermute(value, 'ctx', [(2 * q + y, 2 * q + 1 - y) for q in range(pai...  6.89 us
  transfers between devices with their start and end apart: 22, of which 4 were waited for; matrix products, arithmetic and copies ran while one was open for 6% of the time, Pallas kernels for 50%

commit v1 on v0

--- a/solution.py
+++ b/solution.py
@@ -732,8 +732,8 @@
             for r, piece in zip(some, made):
                 pieces[g, r] = [ship(piece, r)]
 
-    def run_rest(g):
-        for some, square in squares[g]:
+    def run_rest(g, turns):
+        for some, square in squares[g][turns]:
             made = run_back("rest", some, g, [1], square)
             for r, piece in zip(some, made):
                 pieces[g, r].append(ship(piece, r))
@@ -788,12 +788,12 @@
     for g in later:
         ex[g + 1].double()
     for g in later:
-        run_spans(g + 1, 0, 2, 1)
+        run_spans(g + 1, micros=1)
     arrived(0, 0, partners)
-    run_rest(0)
+    run_rest(0, slice(0, 1))
     for g in later:
-        run_spans(g + 1, 1, 2, 1)
         ex[g + 1].finish()
+    run_rest(0, slice(1, None))
     run_one(0, 1)
     for g in later:
         arrived(0, 1, partners[:1])

time: 210 us -> 201 us (0.957)
  waiting for transfers between devices: 28.5 us -> 24.7 us
  Pallas kernels: 112 us -> 109 us
    ppermute x6, waiting for transfers between devices: 5.52 us -> 2.2 us  [swapped(): lax.ppermute(value, 'ctx', [(2 * q + y, 2 * q + 1 - y) for q in range(pai...]
    pallas_call x4 -> x3, Pallas kernels: 31.2 us -> 28 us  [spans_of(): pl.pallas_call(functools.partial(span_kernel, index * some, len(after)),...]
    unnamed x114 -> x92, local copies, waits for them, and re-layouts: 13.4 us -> 11.6 us
  transfers between devices with their start and end apart: 22 -> 22, of which waited for: 4 -> 4; matrix products, arithmetic and copies ran while one was open for 6% -> 7% of each run, Pallas kernels for 50% -> 51%
where the time goes in v1:
time: 201 us; the launch traced here: 199 us
  Pallas kernels  109 us (54%)
  starting transfers between devices  38.6 us (19%)
  waiting for transfers between devices  24.7 us (12%)
  local copies, waits for them, and re-layouts  21.3 us (11%)
  other arithmetic  5.44 us (3%)
    pallas_call x10, Pallas kernels, back(): pl.pallas_call(functools.partial(back_kernel, mode, [len(ys) for _, ys, _...  35.9 us
    pallas_call x3, Pallas kernels, spans_of(): pl.pallas_call(functools.partial(span_kernel, index * some, len(after)),...  28 us
    pallas_call x3, Pallas kernels, front(): pl.pallas_call(functools.partial(front_kernel, len(after), blocks), grid_...  24.4 us
    ppermute x8, waiting for transfers between devices, ship(): return lax.ppermute(piece, 'head', [(i, i ^ r) for i in range(head_size)])  20.7 us
    ppermute x6, starting transfers between devices, shifted(): lax.ppermute(value, 'ctx', [(2 * q + y, 2 * (q + steps) + y) for q in ran...  18.9 us
    pallas_call x9, Pallas kernels, join(): pl.pallas_call(kernel, in_specs=[pl.BlockSpec(memory_space=pltpu.SMEM)] *...  13.6 us
    unnamed x92, local copies, waits for them, and re-layouts  11.6 us
    ppermute x6, starting transfers between devices, swapped(): lax.ppermute(value, 'ctx', [(2 * q + y, 2 * q + 1 - y) for q in range(pai...  6.34 us
  transfers between devices with their start and end apart: 22, of which 4 were waited for; matrix products, arithmetic and copies ran while one was open for 7% of the time, Pallas kernels for 51%

profile of v1, /device:TPU:0, one launch (start us, length us, event | category | flops | bytes accessed | tf_op | source)
XLA Modules:
  0.0 199.2 jit_solution(3258728607886554550)
XLA Ops:
  0.7 4.9 %collective-permute-start = (bf16[3,2,512]{2,1,0:T(2,128)(2,1)S(1)}, bf16[3,2,512]{2,1,0:T(2,128)(2,1)S(1)}, u32[]{:S(2)}, u32[]{:S(2)}) collective-permute-start(bf16[3,2,512]{2,1,0:T(2,128)(2,1)S(1)} %slice.24), channel_id=1, source_target_pairs={{0,4},{4,8},{8,12},{12,16},{16,20},{20,24},{24,28},{1,5},{5,9},{9,... | collective-permute-start | bytes 18440 | tf_op jit(solution)/shard_map/ppermute | solution.py:675
  6.4 3.4 %collective-permute-start.1 = (bf16[3,4096]{1,0:T(4,128)(2,1)S(1)}, bf16[3,4096]{1,0:T(4,128)(2,1)S(1)}, u32[]{:S(2)}, u32[]{:S(2)}) collective-permute-start(bf16[3,4096]{1,0:T(4,128)(2,1)S(1)} %slice.25), channel_id=1, source_target_pairs={{0,4},{4,8},{8,12},{12,16},{16,20},{20,24},{24,28},{1,5},{5,9},{9,... | collective-permute-start | bytes 73736 | tf_op jit(solution)/shard_map/ppermute | solution.py:674
  12.4 1.2 decays.1
  13.8 1.9 copy-done.39
  16.4 2.8 %maps.2 = (bf16[1024,512]{1,0:T(8,128)(2,1)S(1)}, bf16[256,1024]{1,0:T(8,128)(2,1)S(1)}) custom-call(bf16[1024,2,512]{2,1,0:T(2,128)(2,1)S(1)} %copy-done.39, bf16[16,2,512]{2,1,0:T(2,128)(2,1)S(1)} %pad.8.halo_ref, bf16[4,2,512]{2,1,0:T(2,128)(2,1)S(1)} %copy-done.44), custom_call_target="tpu_custom_call" | custom-call | flops 3000000000 | bytes 1 | tf_op jit(solution)/shard_map/maps/pallas_call | solution.py:182
  19.2 6.9 %front.3 = (bf16[1024,1024]{1,0:T(8,128)(2,1)}, bf16[272,512]{1,0:T(8,128)(2,1)S(1)}, f32[264,512]{1,0:T(8,128)S(1)}) custom-call(s32[2]{0:T(128)S(1)} %pad_add_fusion.where_ref, bf16[1024,4096]{1,0:T(8,128)(2,1)} %feat_ref.5, bf16[16,4096]{1,0:T(8,128)(2,1)S(1)} %pad.9.halo_ref, bf16[4,4096]{1,0:T(4,128)(2,1)S(1)} %copy-done.43, ...), custom_call_target="tpu_custom_call" | custom-call | flops 4000000000 | bytes 1 | tf_op jit(solution)/shard_map/front/pallas_call | solution.py:252
  26.2 1.6 collective-permute-start.2
  27.8 6.1 %front.4 = (bf16[1024,1024]{1,0:T(8,128)(2,1)S(1)}, bf16[272,512]{1,0:T(8,128)(2,1)S(1)}, f32[264,512]{1,0:T(8,128)S(1)}) custom-call(s32[2]{0:T(128)S(1)} %pad_add_fusion.where_ref, bf16[1024,4096]{1,0:T(8,128)(2,1)} %feat_ref.5, bf16[16,4096]{1,0:T(8,128)(2,1)S(1)} %pad.9.halo_ref, bf16[4,4096]{1,0:T(4,128)(2,1)S(1)} %copy-done.43, ...), custom_call_target="tpu_custom_call" | custom-call | flops 4000000000 | bytes 1 | tf_op jit(solution)/shard_map/front/pallas_call | solution.py:252
  35.2 3.7 %collective-permute-start.4 = (bf16[272,512]{1,0:T(8,128)(2,1)S(1)}, bf16[272,512]{1,0:T(8,128)(2,1)S(1)}, u32[]{:S(2)}, u32[]{:S(2)}) collective-permute-start(bf16[272,512]{1,0:T(8,128)(2,1)S(1)} %get-tuple-element.50), channel_id=1, source_target_pairs={{0,8},{4,12},{8,16},{12,20},{16,24},{20,28},{1,9},{5,13},{9,17},{1... | collective-permute-start | bytes 835592 | tf_op jit(solution)/shard_map/ppermute | solution.py:600
  38.9 2.8 %maps.3 = (bf16[1024,512]{1,0:T(8,128)(2,1)S(1)}, bf16[256,1024]{1,0:T(8,128)(2,1)S(1)}) custom-call(bf16[1024,2,512]{2,1,0:T(2,128)(2,1)S(1)} %copy-done.40, bf16[16,2,512]{2,1,0:T(2,128)(2,1)S(1)} %pad.8.halo_ref, bf16[4,2,512]{2,1,0:T(2,128)(2,1)S(1)} %copy-done.44, f32[264,512]{1,0:T(8,128)S(1)} %get-tuple-element.45.refs_0_.total_ref), custom_call_target="tpu_custom_call" | custom-call | flops 3000000000 | bytes 1 | tf_op jit(solution)/shard_map/maps/pallas_call | solution.py:182
  41.7 1.8 collective-permute-done.4.before_ref
  45.3 6.1 %collective-permute-start.7 = (bf16[272,512]{1,0:T(8,128)(2,1)}, bf16[272,512]{1,0:T(8,128)(2,1)}, u32[]{:S(2)}, u32[]{:S(2)}) collective-permute-start(bf16[272,512]{1,0:T(8,128)(2,1)} %inclusive.3.refs_0_), channel_id=1, source_target_pairs={{0,16},{4,20},{8,24},{12,28},{1,17},{5,21},{9,25},{13,29},{2,18},{... | collective-permute-start | bytes 835592 | tf_op jit(solution)/shard_map/ppermute | solution.py:600
  51.4 1.4 pair.4
  52.8 2.9 %collective-permute-start.6 = (bf16[272,512]{1,0:T(8,128)(2,1)}, bf16[272,512]{1,0:T(8,128)(2,1)}, u32[]{:S(2)}, u32[]{:S(2)}) collective-permute-start(bf16[272,512]{1,0:T(8,128)(2,1)} %get-tuple-element.58), channel_id=1, source_target_pairs={{0,8},{4,12},{8,16},{12,20},{16,24},{20,28},{1,9},{5,13},{9,17},{1... | collective-permute-start | bytes 835592 | tf_op jit(solution)/shard_map/ppermute | solution.py:600
  55.7 11.3 %front.5 = (bf16[1024,2048]{1,0:T(8,128)(2,1)}, bf16[272,1024]{1,0:T(8,128)(2,1)}, f32[264,1024]{1,0:T(8,128)S(1)}) custom-call(s32[2]{0:T(128)S(1)} %pad_add_fusion.where_ref, bf16[1024,4096]{1,0:T(8,128)(2,1)} %feat_ref.5, bf16[16,4096]{1,0:T(8,128)(2,1)S(1)} %pad.9.halo_ref, bf16[4,4096]{1,0:T(4,128)(2,1)S(1)} %copy-done.43, ...), custom_call_target="tpu_custom_call" | custom-call | flops 4000000000 | bytes 1 | tf_op jit(solution)/shard_map/front/pallas_call | solution.py:252
  67.0 1.5 collective-permute-start.5
  68.5 7.3 %spans.3.refs_0_ = bf16[1024,1024]{1,0:T(8,128)(2,1)S(1)} custom-call(bf16[1024,1024]{1,0:T(8,128)(2,1)} %get-tuple-element.43.refs_0_.xh_ref, bf16[1024,512]{1,0:T(8,128)(2,1)S(1)} %get-tuple-element.40.refs_0_.map_ref.out_ref, f32[1024,128]{1,0:T(8,128)S(1)} %get-tuple-element.53.col_ref, f32[64,1024]{1,0:T(8,128)S(1)} %get-tuple-element.54.row_ref, ...), custom_call_target="tpu_custom_call" | custom-call | flops 199999995904 | bytes 1 | tf_op jit(solution)/shard_map/spans/pallas_call | solution.py:343
  75.9 1.4 last.3
  77.9 1.8 inclusive.4.refs_0_
  79.7 2.0 %collective-permute-start.9 = (bf16[272,512]{1,0:T(8,128)(2,1)}, bf16[272,512]{1,0:T(8,128)(2,1)}, u32[]{:S(2)}, u32[]{:S(2)}) collective-permute-start(bf16[272,512]{1,0:T(8,128)(2,1)} %inclusive.4.refs_0_), channel_id=1, source_target_pairs={{0,16},{4,20},{8,24},{12,28},{1,17},{5,21},{9,25},{13,29},{2,18},{... | collective-permute-start | bytes 835592 | tf_op jit(solution)/shard_map/ppermute | solution.py:600
  81.7 2.2 %pair.5 = (f32[264,1024]{1,0:T(8,128)S(1)}, bf16[272,1024]{1,0:T(8,128)(2,1)}) custom-call(s32[2]{0:T(128)S(1)} %pad_add_fusion.where_ref, f32[264,1024]{1,0:T(8,128)S(1)} %get-tuple-element.56.kept_ref, bf16[272,1024]{1,0:T(8,128)(2,1)} %collective-permute-done.5.got_ref, bf16[272,512]{1,0:T(8,128)(2,1)} %inclusive.4.refs_0_), custom_call_target="tpu_custom_call" | custom-call | flops 700000000 | bytes 1 | tf_op jit(solution)/shard_map/pair/pallas_call | solution.py:425
  83.9 2.1 %collective-permute-start.8 = (bf16[272,1024]{1,0:T(8,128)(2,1)}, bf16[272,1024]{1,0:T(8,128)(2,1)}, u32[]{:S(2)}, u32[]{:S(2)}) collective-permute-start(bf16[272,1024]{1,0:T(8,128)(2,1)} %get-tuple-element.61), channel_id=1, source_target_pairs={{0,8},{4,12},{8,16},{12,20},{16,24},{20,28},{1,9},{5,13},{9,17},{1... | collective-permute-start | bytes 1671176 | tf_op jit(solution)/shard_map/ppermute | solution.py:600
  86.0 3.1 %back_first.2 = (bf16[256,1024]{1,0:T(8,128)(2,1)}, f32[256,128]{1,0:T(8,128)S(1)}) custom-call(s32[2]{0:T(128)S(1)} %pad_add_fusion.where_ref, bf16[1024,512]{1,0:T(8,128)(2,1)S(1)} %get-tuple-element.40.refs_0_.map_ref.out_ref, bf16[1024,512]{1,0:T(8,128)(2,1)S(1)} %get-tuple-element.38.dev_ref.edev_ref.table_ref, bf16[1024,1024]{1,0:T(8,128)(2,1)} %copy-done.5, ...), custom_call_target="tpu_custom_call" | custom-call | flops 1000000000 | bytes 1 | tf_op jit(solution)/shard_map/back_first/pallas_call | solution.py:565
  89.2 3.2 %back_first.3 = (bf16[256,1024]{1,0:T(8,128)(2,1)}, f32[256,128]{1,0:T(8,128)S(1)}) custom-call(s32[2]{0:T(128)S(1)} %pad_add_fusion.where_ref, bf16[1024,512]{1,0:T(8,128)(2,1)S(1)} %get-tuple-element.40.refs_0_.map_ref.out_ref, bf16[1024,512]{1,0:T(8,128)(2,1)S(1)} %get-tuple-element.38.dev_ref.edev_ref.table_ref, bf16[1024,1024]{1,0:T(8,128)(2,1)} %copy-done.5, ...), custom_call_target="tpu_custom_call" | custom-call | flops 1000000000 | bytes 1 | tf_op jit(solution)/shard_map/back_first/pallas_call | solution.py:565
  92.4 1.4 collective-permute-start.14
  95.0 7.3 %spans.4.refs_0_.refs_6_ = bf16[1024,1024]{1,0:T(8,128)(2,1)S(1)} custom-call(bf16[1024,1024]{1,0:T(8,128)(2,1)} %copy-done.12, bf16[1024,512]{1,0:T(8,128)(2,1)S(1)} %get-tuple-element.40.refs_0_.map_ref.out_ref, f32[1024,128]{1,0:T(8,128)S(1)} %get-tuple-element.53.col_ref, f32[64,1024]{1,0:T(8,128)S(1)} %get-tuple-element.54.row_ref, ...), custom_call_target="tpu_custom_call" | custom-call | flops 1000000000 | bytes 1 | tf_op jit(solution)/shard_map/spans/pallas_call | solution.py:343
  102.4 1.7 last.4
  104.1 1.2 inclusive.5.refs_0_
  105.3 2.1 %collective-permute-start.11 = (bf16[272,1024]{1,0:T(8,128)(2,1)S(1)}, bf16[272,1024]{1,0:T(8,128)(2,1)S(1)}, u32[]{:S(2)}, u32[]{:S(2)}) collective-permute-start(bf16[272,1024]{1,0:T(8,128)(2,1)S(1)} %inclusive.5.refs_0_), channel_id=1, source_target_pairs={{0,16},{4,20},{8,24},{12,28},{1,17},{5,21},{9,25},{13,29},{2,18},{... | collective-permute-start | bytes 1671176 | tf_op jit(solution)/shard_map/ppermute | solution.py:600
  107.4 1.8 collective-permute-start.12
  109.2 13.4 %spans.5.refs_7_.refs_0_ = bf16[1024,2048]{1,0:T(8,128)(2,1)} custom-call(bf16[1024,2048]{1,0:T(8,128)(2,1)} %get-tuple-element.52.refs_0_.xh_ref, bf16[1024,512]{1,0:T(8,128)(2,1)S(1)} %copy-done.10, f32[1024,128]{1,0:T(8,128)S(1)} %get-tuple-element.53.col_ref, f32[64,1024]{1,0:T(8,128)S(1)} %get-tuple-element.54.row_ref, ...), custom_call_target="tpu_custom_call" | custom-call | flops 1000000000 | bytes 1 | tf_op jit(solution)/shard_map/spans/pallas_call | solution.py:343
  122.6 3.5 %back_rest.2.refs_0_ = bf16[272,1024]{1,0:T(8,128)(2,1)} custom-call(s32[2]{0:T(128)S(1)} %copy-done.37, bf16[1024,512]{1,0:T(8,128)(2,1)S(1)} %get-tuple-element.40.refs_0_.map_ref.out_ref, bf16[1024,512]{1,0:T(8,128)(2,1)S(1)} %get-tuple-element.38.dev_ref.edev_ref.table_ref, bf16[1024,1024]{1,0:T(8,128)(2,1)} %copy-done.4, ...), custom_call_target="tpu_custom_call" | custom-call | flops 1000000000 | bytes 1 | tf_op jit(solution)/shard_map/back_rest/pallas_call | solution.py:565
  127.3 2.5 %last.5 = (bf16[256,1024]{1,0:T(8,128)(2,1)S(1)}, bf16[256,1024]{1,0:T(8,128)(2,1)}) custom-call(s32[2]{0:T(128)S(1)} %copy-done.37, bf16[272,1024]{1,0:T(8,128)(2,1)} %collective-permute-done.8.before_ref, bf16[272,1024]{1,0:T(8,128)(2,1)S(1)} %collective-permute-done.11.far_ref, f32[264,1024]{1,0:T(8,128)S(1)} %copy-done.29, ...), custom_call_target="tpu_custom_call" | custom-call | flops 700000000 | bytes 1 | tf_op jit(solution)/shard_map/last/pallas_call | solution.py:425
  130.2 3.5 %back_rest.3.refs_12_ = bf16[272,1024]{1,0:T(8,128)(2,1)} custom-call(s32[2]{0:T(128)S(1)} %copy-done.37, bf16[1024,512]{1,0:T(8,128)(2,1)S(1)} %get-tuple-element.40.refs_0_.map_ref.out_ref, bf16[1024,512]{1,0:T(8,128)(2,1)S(1)} %get-tuple-element.38.dev_ref.edev_ref.table_ref, bf16[1024,1024]{1,0:T(8,128)(2,1)} %copy-done.4, ...), custom_call_target="tpu_custom_call" | custom-call | flops 1000000000 | bytes 1 | tf_op jit(solution)/shard_map/back_rest/pallas_call | solution.py:565
  137.6 3.4 %back_whole.6.refs_6_ = bf16[256,2048]{1,0:T(8,128)(2,1)S(1)} custom-call(s32[2]{0:T(128)S(1)} %copy-done.37, bf16[1024,512]{1,0:T(8,128)(2,1)S(1)} %copy-done.7, bf16[1024,512]{1,0:T(8,128)(2,1)S(1)} %copy-done.3, bf16[1024,1024]{1,0:T(8,128)(2,1)} %copy-done.5, bf16[256,512]{1,0:T(8,128)(2,1)S(1)} %copy-done.14, bf16[256,512]{1,0:T(8,128)(2,1)S(1)} %copy-done.16, ...), custom_call_target="tpu_custom_call" | custom-call | flops 1000000000 | bytes 1 | tf_op jit(solution)/shard_map/back_whole/pallas_call | solution.py:565
  141.9 2.2 %collective-permute-done.15.refs_2_ = bf16[256,1024]{1,0:T(8,128)(2,1)S(1)} collective-permute-done((bf16[256,1024]{1,0:T(8,128)(2,1)}, bf16[256,1024]{1,0:T(8,128)(2,1)S(1)}, u32[]{:S(2)}, u32[]{:S(2)}) %collective-permute-start.15) | collective-permute-done | bytes 524320 | tf_op jit(solution)/shard_map/ppermute | solution.py:608
  144.1 3.5 %back_whole.7.refs_6_ = bf16[256,2048]{1,0:T(8,128)(2,1)S(1)} custom-call(s32[2]{0:T(128)S(1)} %copy-done.37, bf16[1024,512]{1,0:T(8,128)(2,1)S(1)} %copy-done.11, bf16[1024,512]{1,0:T(8,128)(2,1)S(1)} %copy-done.3, bf16[1024,2048]{1,0:T(8,128)(2,1)} %spans.5.refs_7_.refs_0_, bf16[256,1024]{1,0:T(8,128)(2,1)S(1)} %get-tuple-element.68.refs_7_.refs_1_, ...), custom_call_target="tpu_custom_call" | custom-call | flops 1000000000 | bytes 1 | tf_op jit(solution)/shard_map/back_whole/pallas_call | solution.py:565
  148.6 3.5 %back_whole.8.refs_6_ = bf16[256,2048]{1,0:T(8,128)(2,1)S(1)} custom-call(s32[2]{0:T(128)S(1)} %copy-done.37, bf16[1024,512]{1,0:T(8,128)(2,1)S(1)} %copy-done.11, bf16[1024,512]{1,0:T(8,128)(2,1)S(1)} %copy-done.3, bf16[1024,2048]{1,0:T(8,128)(2,1)} %spans.5.refs_7_.refs_0_, bf16[256,1024]{1,0:T(8,128)(2,1)S(1)} %get-tuple-element.68.refs_7_.refs_1_, ...), custom_call_target="tpu_custom_call" | custom-call | flops 1000000000 | bytes 1 | tf_op jit(solution)/shard_map/back_whole/pallas_call | solution.py:565
  152.2 1.4 collective-permute-done.17.refs_7_
  153.6 3.5 %back_whole.9.refs_12_.refs_7_ = bf16[256,2048]{1,0:T(8,128)(2,1)S(1)} custom-call(s32[2]{0:T(128)S(1)} %copy-done.37, bf16[1024,512]{1,0:T(8,128)(2,1)S(1)} %copy-done.11, bf16[1024,512]{1,0:T(8,128)(2,1)S(1)} %copy-done.3, bf16[1024,2048]{1,0:T(8,128)(2,1)} %spans.5.refs_7_.refs_0_, bf16[256,1024]{1,0:T(8,128)(2,1)S(1)} %get-tuple-element.68.refs_7_.refs_1_, ...), custom_call_target="tpu_custom_call" | custom-call | flops 1000000000 | bytes 1 | tf_op jit(solution)/shard_map/back_whole/pallas_call | solution.py:565
  157.1 1.5 collective-permute-start.21
  158.6 4.2 %back_whole.10 = bf16[256,16384]{1,0:T(8,128)(2,1)} custom-call(s32[2]{0:T(128)S(1)} %copy-done.37, bf16[1024,512]{1,0:T(8,128)(2,1)S(1)} %copy-done.8, bf16[1024,512]{1,0:T(8,128)(2,1)S(1)} %copy-done.3, bf16[1024,1024]{1,0:T(8,128)(2,1)} %copy-done.5, bf16[256,512]{1,0:T(8,128)(2,1)S(1)} %copy-done.14, bf16[256,512]{1,0:T(8,128)(2,1)S(1)} %copy-done.16, ...), custom_call_target="tpu_custom_call" | custom-call | flops 1000000000 | bytes 1 | tf_op jit(solution)/shard_map/back_whole/pallas_call | solution.py:565
  162.8 2.0 fusion
  164.8 1.9 slice_dynamic-update-slice_fusion.1
  167.4 2.0 fusion.1
  169.4 1.9 slice_dynamic-update-slice_fusion
  172.3 4.3 %back_whole.11 = bf16[256,16384]{1,0:T(8,128)(2,1)} custom-call(s32[2]{0:T(128)S(1)} %copy-done.37, bf16[1024,512]{1,0:T(8,128)(2,1)S(1)} %copy-done.11, bf16[1024,512]{1,0:T(8,128)(2,1)S(1)} %copy-done.3, bf16[1024,2048]{1,0:T(8,128)(2,1)} %spans.5.refs_7_.refs_0_, ...), custom_call_target="tpu_custom_call", output_to_operand_aliasing={{}: (9, {})} | custom-call | flops 1000000000 | bytes 1 | tf_op jit(solution)/shard_map/back_whole/pallas_call | solution.py:565
  178.8 19.4 %collective-permute-done.21 = bf16[256,2048]{1,0:T(8,128)(2,1)S(1)} collective-permute-done((bf16[256,2048]{1,0:T(8,128)(2,1)S(1)}, bf16[256,2048]{1,0:T(8,128)(2,1)S(1)}, u32[]{:S(2)}, u32[]{:S(2)}) %collective-permute-start.21) | collective-permute-done | bytes 1048608 | tf_op jit(solution)/shard_map/ppermute | solution.py:716
  (132 shorter events, 22.3 us)
Async XLA Ops:
  0.7 13.1 %collective-permute-start = (bf16[3,2,512]{2,1,0:T(2,128)(2,1)S(1)}, bf16[3,2,512]{2,1,0:T(2,128)(2,1)S(1)}, u32[]{:S(2)}, u32[]{:S(2)}) collective-permute-start(bf16[3,2,512]{2,1,0:T(2,128)(2,1)S(1)} %slice.24), channel_id=1, source_target_pairs={{0,4},{4,8},{8,12},{12,16},{16,20},{20,24},{24,28},{1,5},{5,9},{9,... | collective-permute-start | bytes 18440 | tf_op jit(solution)/shard_map/ppermute | solution.py:675
  6.4 12.8 %collective-permute-start.1 = (bf16[3,4096]{1,0:T(4,128)(2,1)S(1)}, bf16[3,4096]{1,0:T(4,128)(2,1)S(1)}, u32[]{:S(2)}, u32[]{:S(2)}) collective-permute-start(bf16[3,4096]{1,0:T(4,128)(2,1)S(1)} %slice.25), channel_id=1, source_target_pairs={{0,4},{4,8},{8,12},{12,16},{16,20},{20,24},{24,28},{1,5},{5,9},{9,... | collective-permute-start | bytes 73736 | tf_op jit(solution)/shard_map/ppermute | solution.py:674
  12.4 6.8 %copy-start = (bf16[128,4096]{1,0:T(8,128)(2,1)S(1)}, bf16[128,4096]{1,0:T(8,128)(2,1)}, u32[]{:S(2)}) copy-start(bf16[128,4096]{1,0:T(8,128)(2,1)} %constant.47.clone.spread_ref.refs_3_.refs_9_) | copy-start | bytes 3145732
  12.4 6.8 %copy-start.43 = (bf16[4,4096]{1,0:T(4,128)(2,1)S(1)}, bf16[4,4096]{1,0:T(4,128)(2,1)}, u32[]{:S(2)}) copy-start(bf16[4,4096]{1,0:T(4,128)(2,1)} %taps_ref.9) | copy-start | bytes 98308
  13.7 116.5 %copy-start.2 = (bf16[1024,512]{1,0:T(8,128)(2,1)}, bf16[1024,512]{1,0:T(8,128)(2,1)S(1)}, u32[]{:S(2)}) copy-start(bf16[1024,512]{1,0:T(8,128)(2,1)S(1)} %get-tuple-element.38.dev_ref.edev_ref.table_ref) | copy-start | bytes 3145732
  13.8 88.6 %copy-start.36 = (s32[2]{0:T(128)}, s32[2]{0:T(128)S(1)}, u32[]{:S(2)}) copy-start(s32[2]{0:T(128)S(1)} %pad_add_fusion.where_ref) | copy-start | bytes 28
  19.2 111.0 %copy-start.6 = (bf16[1024,512]{1,0:T(8,128)(2,1)}, bf16[1024,512]{1,0:T(8,128)(2,1)S(1)}, u32[]{:S(2)}) copy-start(bf16[1024,512]{1,0:T(8,128)(2,1)S(1)} %get-tuple-element.40.refs_0_.map_ref.out_ref) | copy-start | bytes 3145732
  26.2 9.0 %copy-start.24 = (f32[264,512]{1,0:T(8,128)}, f32[264,512]{1,0:T(8,128)S(1)}, u32[]{:S(2)}) copy-start(f32[264,512]{1,0:T(8,128)S(1)} %get-tuple-element.41.kept_ref) | copy-start | bytes 1622020
  26.2 8.3 %collective-permute-start.2 = (bf16[272,512]{1,0:T(8,128)(2,1)S(1)}, bf16[272,512]{1,0:T(8,128)(2,1)S(1)}, u32[]{:S(2)}, u32[]{:S(2)}) collective-permute-start(bf16[272,512]{1,0:T(8,128)(2,1)S(1)} %get-tuple-element.42), channel_id=1, source_target_pairs={{0,4},{4,0},{8,12},{12,8},{16,20},{20,16},{24,28},{28,24},{1,5},{5... | collective-permute-start | bytes 835592 | tf_op jit(solution)/shard_map/ppermute | solution.py:608
  27.8 11.1 %copy-start.40 = (bf16[1024,2,512]{2,1,0:T(2,128)(2,1)S(1)}, bf16[1024,2,512]{2,1,0:T(2,128)(2,1)}, u32[]{:S(2)}) copy-start(bf16[1024,2,512]{2,1,0:T(2,128)(2,1)} %io_ref.3) | copy-start | bytes 6291460
  33.9 18.9 %copy-start.12 = (bf16[1024,1024]{1,0:T(8,128)(2,1)}, bf16[1024,1024]{1,0:T(8,128)(2,1)S(1)}, u32[]{:S(2)}) copy-start(bf16[1024,1024]{1,0:T(8,128)(2,1)S(1)} %get-tuple-element.44.refs_0_.xh_ref) | copy-start | bytes 6291460
  33.9 18.9 %copy-start.30 = (f32[264,512]{1,0:T(8,128)}, f32[264,512]{1,0:T(8,128)S(1)}, u32[]{:S(2)}) copy-start(f32[264,512]{1,0:T(8,128)S(1)} %get-tuple-element.48.kept_ref) | copy-start | bytes 1622020
  33.9 17.4 %collective-permute-start.3 = (bf16[272,512]{1,0:T(8,128)(2,1)S(1)}, bf16[272,512]{1,0:T(8,128)(2,1)S(1)}, u32[]{:S(2)}, u32[]{:S(2)}) collective-permute-start(bf16[272,512]{1,0:T(8,128)(2,1)S(1)} %get-tuple-element.49), channel_id=1, source_target_pairs={{0,4},{4,0},{8,12},{12,8},{16,20},{20,16},{24,28},{28,24},{1,5},{5... | collective-permute-start | bytes 835592 | tf_op jit(solution)/shard_map/ppermute | solution.py:608
  34.4 18.3 %copy-start.26 = (bf16[272,512]{1,0:T(8,128)(2,1)}, bf16[272,512]{1,0:T(8,128)(2,1)S(1)}, u32[]{:S(2)}) copy-start(bf16[272,512]{1,0:T(8,128)(2,1)S(1)} %collective-permute-done.2.got_ref) | copy-start | bytes 835588
  35.2 8.3 %collective-permute-start.4 = (bf16[272,512]{1,0:T(8,128)(2,1)S(1)}, bf16[272,512]{1,0:T(8,128)(2,1)S(1)}, u32[]{:S(2)}, u32[]{:S(2)}) collective-permute-start(bf16[272,512]{1,0:T(8,128)(2,1)S(1)} %get-tuple-element.50), channel_id=1, source_target_pairs={{0,8},{4,12},{8,16},{12,20},{16,24},{20,28},{1,9},{5,13},{9,17},{1... | collective-permute-start | bytes 835592 | tf_op jit(solution)/shard_map/ppermute | solution.py:600
  43.4 12.3 %copy-start.34 = (bf16[272,512]{1,0:T(8,128)(2,1)}, bf16[272,512]{1,0:T(8,128)(2,1)S(1)}, u32[]{:S(2)}) copy-start(bf16[272,512]{1,0:T(8,128)(2,1)S(1)} %collective-permute-done.4.before_ref) | copy-start | bytes 835588
  45.3 30.6 %collective-permute-start.7 = (bf16[272,512]{1,0:T(8,128)(2,1)}, bf16[272,512]{1,0:T(8,128)(2,1)}, u32[]{:S(2)}, u32[]{:S(2)}) collective-permute-start(bf16[272,512]{1,0:T(8,128)(2,1)} %inclusive.3.refs_0_), channel_id=1, source_target_pairs={{0,16},{4,20},{8,24},{12,28},{1,17},{5,21},{9,25},{13,29},{2,18},{... | collective-permute-start | bytes 835592 | tf_op jit(solution)/shard_map/ppermute | solution.py:600
  51.4 17.1 %copy-start.38 = (bf16[2,128]{1,0:T(2,128)(2,1)S(1)}, bf16[2,128]{1,0:T(2,128)(2,1)}, u32[]{:S(2)}) copy-start(bf16[2,128]{1,0:T(2,128)(2,1)} %constant.48.clone.halves_ref) | copy-start | bytes 1540
  52.8 25.1 %collective-permute-start.6 = (bf16[272,512]{1,0:T(8,128)(2,1)}, bf16[272,512]{1,0:T(8,128)(2,1)}, u32[]{:S(2)}, u32[]{:S(2)}) collective-permute-start(bf16[272,512]{1,0:T(8,128)(2,1)} %get-tuple-element.58), channel_id=1, source_target_pairs={{0,8},{4,12},{8,16},{12,20},{16,24},{20,28},{1,9},{5,13},{9,17},{1... | collective-permute-start | bytes 835592 | tf_op jit(solution)/shard_map/ppermute | solution.py:600
  67.0 14.6 %copy-start.28 = (f32[264,1024]{1,0:T(8,128)}, f32[264,1024]{1,0:T(8,128)S(1)}, u32[]{:S(2)}) copy-start(f32[264,1024]{1,0:T(8,128)S(1)} %get-tuple-element.56.kept_ref) | copy-start | bytes 3244036
  67.0 14.6 %collective-permute-start.5 = (bf16[272,1024]{1,0:T(8,128)(2,1)}, bf16[272,1024]{1,0:T(8,128)(2,1)}, u32[]{:S(2)}, u32[]{:S(2)}) collective-permute-start(bf16[272,1024]{1,0:T(8,128)(2,1)} %get-tuple-element.57), channel_id=1, source_target_pairs={{0,4},{4,0},{8,12},{12,8},{16,20},{20,16},{24,28},{28,24},{1,5},{5... | collective-permute-start | bytes 1671176 | tf_op jit(solution)/shard_map/ppermute | solution.py:608
  68.5 7.3 %copy-start.25 = (f32[264,512]{1,0:T(8,128)S(1)}, f32[264,512]{1,0:T(8,128)}, u32[]{:S(2)}) copy-start(f32[264,512]{1,0:T(8,128)} %copy-done.24) | copy-start | bytes 1622020
  68.5 7.4 %copy-start.27 = (bf16[272,512]{1,0:T(8,128)(2,1)S(1)}, bf16[272,512]{1,0:T(8,128)(2,1)}, u32[]{:S(2)}) copy-start(bf16[272,512]{1,0:T(8,128)(2,1)} %copy-done.26) | copy-start | bytes 835588
  68.5 7.4 %copy-start.35 = (bf16[272,512]{1,0:T(8,128)(2,1)S(1)}, bf16[272,512]{1,0:T(8,128)(2,1)}, u32[]{:S(2)}) copy-start(bf16[272,512]{1,0:T(8,128)(2,1)} %copy-done.34) | copy-start | bytes 835588
  75.8 10.2 %copy-start.5 = (bf16[1024,1024]{1,0:T(8,128)(2,1)}, bf16[1024,1024]{1,0:T(8,128)(2,1)S(1)}, u32[]{:S(2)}) copy-start(bf16[1024,1024]{1,0:T(8,128)(2,1)S(1)} %spans.3.refs_0_) | copy-start | bytes 6291460
  75.8 10.2 %copy-start.22 = (f32[4096]{0:T(1024)S(1)}, f32[4096]{0:T(1024)}, u32[]{:S(2)}) copy-start(f32[4096]{0:T(1024)} %param.19) | copy-start | bytes 49156
  77.3 11.9 %copy-start.13 = (bf16[256,512]{1,0:T(8,128)(2,1)}, bf16[256,512]{1,0:T(8,128)(2,1)S(1)}, u32[]{:S(2)}) copy-start(bf16[256,512]{1,0:T(8,128)(2,1)S(1)} %get-tuple-element.59.refs_0_.refs_1_) | copy-start | bytes 786436
  77.3 8.8 %collective-permute-start.10 = (bf16[256,512]{1,0:T(8,128)(2,1)S(1)}, bf16[256,512]{1,0:T(8,128)(2,1)S(1)}, u32[]{:S(2)}, u32[]{:S(2)}) collective-permute-start(bf16[256,512]{1,0:T(8,128)(2,1)S(1)} %get-tuple-element.62), channel_id=1, source_target_pairs={{0,4},{4,0},{8,12},{12,8},{16,20},{20,16},{24,28},{28,24},{1,5},{5... | collective-permute-start | bytes 786440 | tf_op jit(solution)/shard_map/ppermute | solution.py:608
  79.7 22.7 %collective-permute-start.9 = (bf16[272,512]{1,0:T(8,128)(2,1)}, bf16[272,512]{1,0:T(8,128)(2,1)}, u32[]{:S(2)}, u32[]{:S(2)}) collective-permute-start(bf16[272,512]{1,0:T(8,128)(2,1)} %inclusive.4.refs_0_), channel_id=1, source_target_pairs={{0,16},{4,20},{8,24},{12,28},{1,17},{5,21},{9,25},{13,29},{2,18},{... | collective-permute-start | bytes 835592 | tf_op jit(solution)/shard_map/ppermute | solution.py:600
  83.9 20.2 %collective-permute-start.8 = (bf16[272,1024]{1,0:T(8,128)(2,1)}, bf16[272,1024]{1,0:T(8,128)(2,1)}, u32[]{:S(2)}, u32[]{:S(2)}) collective-permute-start(bf16[272,1024]{1,0:T(8,128)(2,1)} %get-tuple-element.61), channel_id=1, source_target_pairs={{0,8},{4,12},{8,16},{12,20},{16,24},{20,28},{1,9},{5,13},{9,17},{1... | collective-permute-start | bytes 1671176 | tf_op jit(solution)/shard_map/ppermute | solution.py:600
  89.2 33.4 %collective-permute-start.13 = (bf16[256,1024]{1,0:T(8,128)(2,1)}, bf16[256,1024]{1,0:T(8,128)(2,1)}, u32[]{:S(2)}, u32[]{:S(2)}) collective-permute-start(bf16[256,1024]{1,0:T(8,128)(2,1)} %get-tuple-element.63.refs_6_), channel_id=1, source_target_pairs={{0,3},{1,2},{2,1},{3,0},{4,7},{5,6},{6,5},{7,4},{8,11},{9,10},{10,... | collective-permute-start | bytes 1572872 | tf_op jit(solution)/shard_map/ppermute | solution.py:716
  92.4 30.2 %collective-permute-start.14 = (bf16[256,1024]{1,0:T(8,128)(2,1)}, bf16[256,1024]{1,0:T(8,128)(2,1)}, u32[]{:S(2)}, u32[]{:S(2)}) collective-permute-start(bf16[256,1024]{1,0:T(8,128)(2,1)} %get-tuple-element.64.refs_0_), channel_id=1, source_target_pairs={{0,2},{1,3},{2,0},{3,1},{4,6},{5,7},{6,4},{7,5},{8,10},{9,11},{10,... | collective-permute-start | bytes 1572872 | tf_op jit(solution)/shard_map/ppermute | solution.py:716
  93.8 8.6 %copy-start.33 = (bf16[272,512]{1,0:T(8,128)(2,1)S(1)}, bf16[272,512]{1,0:T(8,128)(2,1)}, u32[]{:S(2)}) copy-start(bf16[272,512]{1,0:T(8,128)(2,1)} %copy-done.32) | copy-start | bytes 835588
  95.0 7.4 %copy-start.31 = (f32[264,512]{1,0:T(8,128)S(1)}, f32[264,512]{1,0:T(8,128)}, u32[]{:S(2)}) copy-start(f32[264,512]{1,0:T(8,128)} %copy-done.30) | copy-start | bytes 1622020
  95.0 14.1 %copy-start.10 = (bf16[1024,512]{1,0:T(8,128)(2,1)S(1)}, bf16[1024,512]{1,0:T(8,128)(2,1)}, u32[]{:S(2)}) copy-start(bf16[1024,512]{1,0:T(8,128)(2,1)} %copy-done.9) | copy-start | bytes 3145732
  102.4 20.2 %copy-start.4 = (bf16[1024,1024]{1,0:T(8,128)(2,1)}, bf16[1024,1024]{1,0:T(8,128)(2,1)S(1)}, u32[]{:S(2)}) copy-start(bf16[1024,1024]{1,0:T(8,128)(2,1)S(1)} %spans.4.refs_0_.refs_6_) | copy-start | bytes 6291460
  104.1 18.5 %copy-start.37 = (s32[2]{0:T(128)S(1)}, s32[2]{0:T(128)}, u32[]{:S(2)}) copy-start(s32[2]{0:T(128)} %copy-done.36) | copy-start | bytes 28
  105.3 22.0 %collective-permute-start.11 = (bf16[272,1024]{1,0:T(8,128)(2,1)S(1)}, bf16[272,1024]{1,0:T(8,128)(2,1)S(1)}, u32[]{:S(2)}, u32[]{:S(2)}) collective-permute-start(bf16[272,1024]{1,0:T(8,128)(2,1)S(1)} %inclusive.5.refs_0_), channel_id=1, source_target_pairs={{0,16},{4,20},{8,24},{12,28},{1,17},{5,21},{9,25},{13,29},{2,18},{... | collective-permute-start | bytes 1671176 | tf_op jit(solution)/shard_map/ppermute | solution.py:600
  107.4 15.2 %collective-permute-start.12 = (bf16[256,512]{1,0:T(8,128)(2,1)S(1)}, bf16[256,512]{1,0:T(8,128)(2,1)S(1)}, u32[]{:S(2)}, u32[]{:S(2)}) collective-permute-start(bf16[256,512]{1,0:T(8,128)(2,1)S(1)} %get-tuple-element.66), channel_id=1, source_target_pairs={{0,4},{4,0},{8,12},{12,8},{16,20},{20,16},{24,28},{28,24},{1,5},{5... | collective-permute-start | bytes 786440 | tf_op jit(solution)/shard_map/ppermute | solution.py:608
  122.6 7.6 %copy-start.17 = (bf16[256,512]{1,0:T(8,128)(2,1)}, bf16[256,512]{1,0:T(8,128)(2,1)S(1)}, u32[]{:S(2)}) copy-start(bf16[256,512]{1,0:T(8,128)(2,1)S(1)} %collective-permute-done.12.refs_2_.refs_8_) | copy-start | bytes 786436
  126.1 15.0 %collective-permute-start.16 = (bf16[272,1024]{1,0:T(8,128)(2,1)}, bf16[272,1024]{1,0:T(8,128)(2,1)}, u32[]{:S(2)}, u32[]{:S(2)}) collective-permute-start(bf16[272,1024]{1,0:T(8,128)(2,1)} %back_rest.2.refs_0_), channel_id=1, source_target_pairs={{0,3},{1,2},{2,1},{3,0},{4,7},{5,6},{6,5},{7,4},{8,11},{9,10},{10,... | collective-permute-start | bytes 1671176 | tf_op jit(solution)/shard_map/ppermute | solution.py:716
  129.8 14.3 %collective-permute-start.15 = (bf16[256,1024]{1,0:T(8,128)(2,1)}, bf16[256,1024]{1,0:T(8,128)(2,1)S(1)}, u32[]{:S(2)}, u32[]{:S(2)}) collective-permute-start(bf16[256,1024]{1,0:T(8,128)(2,1)} %get-tuple-element.69), channel_id=1, source_target_pairs={{0,4},{4,0},{8,12},{12,8},{16,20},{20,16},{24,28},{28,24},{1,5},{5... | collective-permute-start | bytes 1572872 | tf_op jit(solution)/shard_map/ppermute | solution.py:608
  133.7 19.9 %collective-permute-start.17 = (bf16[272,1024]{1,0:T(8,128)(2,1)}, bf16[272,1024]{1,0:T(8,128)(2,1)}, u32[]{:S(2)}, u32[]{:S(2)}) collective-permute-start(bf16[272,1024]{1,0:T(8,128)(2,1)} %back_rest.3.refs_12_), channel_id=1, source_target_pairs={{0,2},{1,3},{2,0},{3,1},{4,6},{5,7},{6,4},{7,5},{8,10},{9,11},{10,... | collective-permute-start | bytes 1671176 | tf_op jit(solution)/shard_map/ppermute | solution.py:716
  141.1 30.1 %collective-permute-start.18 = (bf16[256,2048]{1,0:T(8,128)(2,1)S(1)}, bf16[256,2048]{1,0:T(8,128)(2,1)S(1)}, u32[]{:S(2)}, u32[]{:S(2)}) collective-permute-start(bf16[256,2048]{1,0:T(8,128)(2,1)S(1)} %back_whole.6.refs_6_), channel_id=1, source_target_pairs={{0,1},{1,0},{2,3},{3,2},{4,5},{5,4},{6,7},{7,6},{8,9},{9,8},{10,11... | collective-permute-start | bytes 3145736 | tf_op jit(solution)/shard_map/ppermute | solution.py:716
  147.6 29.0 %collective-permute-start.19 = (bf16[256,2048]{1,0:T(8,128)(2,1)S(1)}, bf16[256,2048]{1,0:T(8,128)(2,1)S(1)}, u32[]{:S(2)}, u32[]{:S(2)}) collective-permute-start(bf16[256,2048]{1,0:T(8,128)(2,1)S(1)} %back_whole.7.refs_6_), channel_id=1, source_target_pairs={{0,3},{1,2},{2,1},{3,0},{4,7},{5,6},{6,5},{7,4},{8,11},{9,10},{10,... | collective-permute-start | bytes 3145736 | tf_op jit(solution)/shard_map/ppermute | solution.py:716
  152.1 6.5 %copy-start.8 = (bf16[1024,512]{1,0:T(8,128)(2,1)S(1)}, bf16[1024,512]{1,0:T(8,128)(2,1)}, u32[]{:S(2)}) copy-start(bf16[1024,512]{1,0:T(8,128)(2,1)} %copy-done.6) | copy-start | bytes 3145732
  152.1 25.6 %collective-permute-start.20 = (bf16[256,2048]{1,0:T(8,128)(2,1)S(1)}, bf16[256,2048]{1,0:T(8,128)(2,1)S(1)}, u32[]{:S(2)}, u32[]{:S(2)}) collective-permute-start(bf16[256,2048]{1,0:T(8,128)(2,1)S(1)} %back_whole.8.refs_6_), channel_id=1, source_target_pairs={{0,1},{1,0},{2,3},{3,2},{4,5},{5,4},{6,7},{7,6},{8,9},{9,8},{10,11... | collective-permute-start | bytes 3145736 | tf_op jit(solution)/shard_map/ppermute | solution.py:716
  157.1 41.1 %collective-permute-start.21 = (bf16[256,2048]{1,0:T(8,128)(2,1)S(1)}, bf16[256,2048]{1,0:T(8,128)(2,1)S(1)}, u32[]{:S(2)}, u32[]{:S(2)}) collective-permute-start(bf16[256,2048]{1,0:T(8,128)(2,1)S(1)} %back_whole.9.refs_12_.refs_7_), channel_id=1, source_target_pairs={{0,2},{1,3},{2,0},{3,1},{4,6},{5,7},{6,4},{7,5},{8,10},{9,11},{10,... | collective-permute-start | bytes 3145736 | tf_op jit(solution)/shard_map/ppermute | solution.py:716
  (20 other events, 51.3 us)

commit v2 on v1

--- a/solution.py
+++ b/solution.py
@@ -15,7 +15,7 @@
 LOC, ECUM, DEV, EDEV = range(4)
 F32 = jnp.float32
 BF16 = jnp.bfloat16
-VMEM_BYTES = 48 * 1024 * 1024
+VMEM_BYTES = 44 * 1024 * 1024
 VMEM_SMALL = 8 * 1024 * 1024
 COST_SCALE = 10**9
 MSG = STATE + 16
@@ -771,10 +771,9 @@
     ex[0].pair()
     for g in later:
         run_maps(g)
+        run_front(g + 1)
     ex[0].double()
     ex[1].pair()
-    for g in later:
-        run_front(g + 1)
     run_spans(0)
     ex[0].finish()
     ex[1].double()
@@ -783,10 +782,10 @@
     run_first(0, apart=True)
     if groups > 1:
         line.run(mark)
-    run_spans(1, micros=1)
-    ex[1].finish()
     for g in later:
         ex[g + 1].double()
+    ex[1].finish()
+    run_spans(1, micros=1)
     for g in later:
         run_spans(g + 1, micros=1)
     arrived(0, 0, partners)

time: 201 us -> 208 us (1.035)
  starting transfers between devices: 38.6 us -> 48.5 us
  Pallas kernels: 109 us -> 105 us
  local copies, waits for them, and re-layouts: 21.3 us -> 25 us
  waiting for transfers between devices: 24.7 us -> 22 us
    ppermute x6, starting transfers between devices: 18.9 us -> 27.8 us  [shifted(): lax.ppermute(value, 'ctx', [(2 * q + y, 2 * (q + steps) + y) for q in ran...]
    unnamed x92 -> x106, local copies, waits for them, and re-layouts: 11.6 us -> 15.4 us
    pallas_call x3, Pallas kernels: 28 us -> 25.1 us  [spans_of(): pl.pallas_call(functools.partial(span_kernel, index * some, len(after)),...]
    ppermute x8, waiting for transfers between devices: 20.7 us -> 18.5 us  [ship(): return lax.ppermute(piece, 'head', [(i, i ^ r) for i in range(head_size)])]
    ppermute x6, waiting for transfers between devices: 2.2 us -> 0.02 us  [swapped(): lax.ppermute(value, 'ctx', [(2 * q + y, 2 * q + 1 - y) for q in range(pai...]
  transfers between devices with their start and end apart: 22 -> 22, of which waited for: 4 -> 2; matrix products, arithmetic and copies ran while one was open for 7% -> 7% of each run, Pallas kernels for 51% -> 48%
where the time goes in v2:
time: 208 us; the launch traced here: 206 us
  Pallas kernels  105 us (50%)
  starting transfers between devices  48.5 us (23%)
  local copies, waits for them, and re-layouts  25 us (12%)
  waiting for transfers between devices  22 us (11%)
  other arithmetic  5.57 us (3%)
    pallas_call x10, Pallas kernels, back(): pl.pallas_call(functools.partial(back_kernel, mode, [len(ys) for _, ys, _...  35.5 us
    ppermute x6, starting transfers between devices, shifted(): lax.ppermute(value, 'ctx', [(2 * q + y, 2 * (q + steps) + y) for q in ran...  27.8 us
    pallas_call x3, Pallas kernels, spans_of(): pl.pallas_call(functools.partial(span_kernel, index * some, len(after)),...  25.1 us
    pallas_call x3, Pallas kernels, front(): pl.pallas_call(functools.partial(front_kernel, len(after), blocks), grid_...  23.5 us
    ppermute x8, waiting for transfers between devices, ship(): return lax.ppermute(piece, 'head', [(i, i ^ r) for i in range(head_size)])  18.5 us
    unnamed x106, local copies, waits for them, and re-layouts  15.4 us
    pallas_call x9, Pallas kernels, join(): pl.pallas_call(kernel, in_specs=[pl.BlockSpec(memory_space=pltpu.SMEM)] *...  13.7 us
    ppermute x6, starting transfers between devices, swapped(): lax.ppermute(value, 'ctx', [(2 * q + y, 2 * q + 1 - y) for q in range(pai...  6.63 us
  transfers between devices with their start and end apart: 22, of which 2 were waited for; matrix products, arithmetic and copies ran while one was open for 7% of the time, Pallas kernels for 48%

profile of v2, /device:TPU:0, one launch (start us, length us, event | category | flops | bytes accessed | tf_op | source)
XLA Modules:
  0.0 206.4 jit_solution(7634922806424301735)
XLA Ops:
  0.7 4.9 %collective-permute-start = (bf16[3,2,512]{2,1,0:T(2,128)(2,1)S(1)}, bf16[3,2,512]{2,1,0:T(2,128)(2,1)S(1)}, u32[]{:S(2)}, u32[]{:S(2)}) collective-permute-start(bf16[3,2,512]{2,1,0:T(2,128)(2,1)S(1)} %slice.24), channel_id=1, source_target_pairs={{0,4},{4,8},{8,12},{12,16},{16,20},{20,24},{24,28},{1,5},{5,9},{9,... | collective-permute-start | bytes 18440 | tf_op jit(solution)/shard_map/ppermute | solution.py:675
  6.4 3.4 %collective-permute-start.1 = (bf16[3,4096]{1,0:T(4,128)(2,1)S(1)}, bf16[3,4096]{1,0:T(4,128)(2,1)S(1)}, u32[]{:S(2)}, u32[]{:S(2)}) collective-permute-start(bf16[3,4096]{1,0:T(4,128)(2,1)S(1)} %slice.25), channel_id=1, source_target_pairs={{0,4},{4,8},{8,12},{12,16},{16,20},{20,24},{24,28},{1,5},{5,9},{9,... | collective-permute-start | bytes 73736 | tf_op jit(solution)/shard_map/ppermute | solution.py:674
  12.4 1.2 decays.1
  13.8 1.9 copy-done.44
  16.4 2.8 %maps.2 = (bf16[1024,512]{1,0:T(8,128)(2,1)S(1)}, bf16[256,1024]{1,0:T(8,128)(2,1)S(1)}) custom-call(bf16[1024,2,512]{2,1,0:T(2,128)(2,1)S(1)} %copy-done.44, bf16[16,2,512]{2,1,0:T(2,128)(2,1)S(1)} %pad.8.halo_ref, bf16[4,2,512]{2,1,0:T(2,128)(2,1)S(1)} %copy-done.51), custom_call_target="tpu_custom_call" | custom-call | flops 3000000000 | bytes 1 | tf_op jit(solution)/shard_map/maps/pallas_call | solution.py:182
  19.3 6.1 %front.3 = (bf16[1024,1024]{1,0:T(8,128)(2,1)S(1)}, bf16[272,512]{1,0:T(8,128)(2,1)S(1)}, f32[264,512]{1,0:T(8,128)S(1)}) custom-call(s32[2]{0:T(128)S(1)} %pad_add_fusion.where_ref, bf16[1024,4096]{1,0:T(8,128)(2,1)} %feat_ref.5, bf16[16,4096]{1,0:T(8,128)(2,1)S(1)} %pad.9.halo_ref, bf16[4,4096]{1,0:T(4,128)(2,1)S(1)} %copy-done.50, ...), custom_call_target="tpu_custom_call" | custom-call | flops 4000000000 | bytes 1 | tf_op jit(solution)/shard_map/front/pallas_call | solution.py:252
  25.4 1.6 collective-permute-start.2
  26.9 6.1 %front.4 = (bf16[1024,1024]{1,0:T(8,128)(2,1)S(1)}, bf16[272,512]{1,0:T(8,128)(2,1)S(1)}, f32[264,512]{1,0:T(8,128)S(1)}) custom-call(s32[2]{0:T(128)S(1)} %pad_add_fusion.where_ref, bf16[1024,4096]{1,0:T(8,128)(2,1)} %feat_ref.5, bf16[16,4096]{1,0:T(8,128)(2,1)S(1)} %pad.9.halo_ref, bf16[4,4096]{1,0:T(4,128)(2,1)S(1)} %copy-done.50, ...), custom_call_target="tpu_custom_call" | custom-call | flops 4000000000 | bytes 1 | tf_op jit(solution)/shard_map/front/pallas_call | solution.py:252
  34.6 2.8 %maps.3 = (bf16[1024,512]{1,0:T(8,128)(2,1)S(1)}, bf16[256,1024]{1,0:T(8,128)(2,1)S(1)}) custom-call(bf16[1024,2,512]{2,1,0:T(2,128)(2,1)S(1)} %copy-done.45, bf16[16,2,512]{2,1,0:T(2,128)(2,1)S(1)} %pad.8.halo_ref, bf16[4,2,512]{2,1,0:T(2,128)(2,1)S(1)} %copy-done.51, f32[264,512]{1,0:T(8,128)S(1)} %get-tuple-element.45.refs_0_.total_ref), custom_call_target="tpu_custom_call" | custom-call | flops 3000000000 | bytes 1 | tf_op jit(solution)/shard_map/maps/pallas_call | solution.py:182
  37.4 3.5 %collective-permute-start.4 = (bf16[272,512]{1,0:T(8,128)(2,1)S(1)}, bf16[272,512]{1,0:T(8,128)(2,1)S(1)}, u32[]{:S(2)}, u32[]{:S(2)}) collective-permute-start(bf16[272,512]{1,0:T(8,128)(2,1)S(1)} %get-tuple-element.54), channel_id=1, source_target_pairs={{0,8},{4,12},{8,16},{12,20},{16,24},{20,28},{1,9},{5,13},{9,17},{1... | collective-permute-start | bytes 835592 | tf_op jit(solution)/shard_map/ppermute | solution.py:600
  40.9 11.3 %front.5 = (bf16[1024,2048]{1,0:T(8,128)(2,1)S(1)}, bf16[272,1024]{1,0:T(8,128)(2,1)}, f32[264,1024]{1,0:T(8,128)S(1)}) custom-call(s32[2]{0:T(128)S(1)} %pad_add_fusion.where_ref, bf16[1024,4096]{1,0:T(8,128)(2,1)} %feat_ref.5, bf16[16,4096]{1,0:T(8,128)(2,1)S(1)} %pad.9.halo_ref, bf16[4,4096]{1,0:T(4,128)(2,1)S(1)} %copy-done.50, ...), custom_call_target="tpu_custom_call" | custom-call | flops 4000000000 | bytes 1 | tf_op jit(solution)/shard_map/front/pallas_call | solution.py:252
  52.2 1.5 collective-permute-start.8
  54.7 3.7 %collective-permute-start.6 = (bf16[272,512]{1,0:T(8,128)(2,1)}, bf16[272,512]{1,0:T(8,128)(2,1)}, u32[]{:S(2)}, u32[]{:S(2)}) collective-permute-start(bf16[272,512]{1,0:T(8,128)(2,1)} %inclusive.3.refs_0_), channel_id=1, source_target_pairs={{0,16},{4,20},{8,24},{12,28},{1,17},{5,21},{9,25},{13,29},{2,18},{... | collective-permute-start | bytes 835592 | tf_op jit(solution)/shard_map/ppermute | solution.py:600
  58.4 1.4 pair.4
  59.9 2.5 %collective-permute-start.5 = (bf16[272,512]{1,0:T(8,128)(2,1)}, bf16[272,512]{1,0:T(8,128)(2,1)}, u32[]{:S(2)}, u32[]{:S(2)}) collective-permute-start(bf16[272,512]{1,0:T(8,128)(2,1)} %get-tuple-element.55), channel_id=1, source_target_pairs={{0,8},{4,12},{8,16},{12,20},{16,24},{20,28},{1,9},{5,13},{9,17},{1... | collective-permute-start | bytes 835592 | tf_op jit(solution)/shard_map/ppermute | solution.py:600
  62.4 6.3 %spans.3.refs_0_ = bf16[1024,1024]{1,0:T(8,128)(2,1)S(1)} custom-call(bf16[1024,1024]{1,0:T(8,128)(2,1)S(1)} %get-tuple-element.43.refs_0_.xh_ref, bf16[1024,512]{1,0:T(8,128)(2,1)S(1)} %get-tuple-element.40.refs_0_.map_ref.out_ref, f32[1024,128]{1,0:T(8,128)S(1)} %get-tuple-element.49.col_ref, f32[64,1024]{1,0:T(8,128)S(1)} %get-tuple-element.50.row_ref, ...), custom_call_target="tpu_custom_call" | custom-call | flops 199999995904 | bytes 1 | tf_op jit(solution)/shard_map/spans/pallas_call | solution.py:343
  72.0 1.7 inclusive.4.refs_0_
  73.7 7.1 %collective-permute-start.7 = (bf16[272,512]{1,0:T(8,128)(2,1)}, bf16[272,512]{1,0:T(8,128)(2,1)}, u32[]{:S(2)}, u32[]{:S(2)}) collective-permute-start(bf16[272,512]{1,0:T(8,128)(2,1)} %inclusive.4.refs_0_), channel_id=1, source_target_pairs={{0,16},{4,20},{8,24},{12,28},{1,17},{5,21},{9,25},{13,29},{2,18},{... | collective-permute-start | bytes 835592 | tf_op jit(solution)/shard_map/ppermute | solution.py:600
  80.9 2.2 %pair.5 = (f32[264,1024]{1,0:T(8,128)S(1)}, bf16[272,1024]{1,0:T(8,128)(2,1)}) custom-call(s32[2]{0:T(128)S(1)} %copy-done.38, f32[264,1024]{1,0:T(8,128)S(1)} %get-tuple-element.58.kept_ref, bf16[272,1024]{1,0:T(8,128)(2,1)} %collective-permute-done.8.got_ref, bf16[272,512]{1,0:T(8,128)(2,1)} %inclusive.4.refs_0_), custom_call_target="tpu_custom_call" | custom-call | flops 700000000 | bytes 1 | tf_op jit(solution)/shard_map/pair/pallas_call | solution.py:425
  83.0 2.6 %collective-permute-start.9 = (bf16[272,1024]{1,0:T(8,128)(2,1)}, bf16[272,1024]{1,0:T(8,128)(2,1)}, u32[]{:S(2)}, u32[]{:S(2)}) collective-permute-start(bf16[272,1024]{1,0:T(8,128)(2,1)} %get-tuple-element.61), channel_id=1, source_target_pairs={{0,8},{4,12},{8,16},{12,20},{16,24},{20,28},{1,9},{5,13},{9,17},{1... | collective-permute-start | bytes 1671176 | tf_op jit(solution)/shard_map/ppermute | solution.py:600
  85.7 3.1 %back_first.2 = (bf16[256,1024]{1,0:T(8,128)(2,1)}, f32[256,128]{1,0:T(8,128)S(1)}) custom-call(s32[2]{0:T(128)S(1)} %copy-done.38, bf16[1024,512]{1,0:T(8,128)(2,1)S(1)} %get-tuple-element.40.refs_0_.map_ref.out_ref, bf16[1024,512]{1,0:T(8,128)(2,1)S(1)} %get-tuple-element.38.dev_ref.edev_ref.table_ref, bf16[1024,1024]{1,0:T(8,128)(2,1)S(1)} %spans.3.refs_0_, ...), custom_call_target="tpu_custom_call" | custom-call | flops 1000000000 | bytes 1 | tf_op jit(solution)/shard_map/back_first/pallas_call | solution.py:565
  88.8 3.1 %back_first.3 = (bf16[256,1024]{1,0:T(8,128)(2,1)}, f32[256,128]{1,0:T(8,128)S(1)}) custom-call(s32[2]{0:T(128)S(1)} %copy-done.38, bf16[1024,512]{1,0:T(8,128)(2,1)S(1)} %get-tuple-element.40.refs_0_.map_ref.out_ref, bf16[1024,512]{1,0:T(8,128)(2,1)S(1)} %get-tuple-element.38.dev_ref.edev_ref.table_ref, bf16[1024,1024]{1,0:T(8,128)(2,1)S(1)} %spans.3.refs_0_, ...), custom_call_target="tpu_custom_call" | custom-call | flops 1000000000 | bytes 1 | tf_op jit(solution)/shard_map/back_first/pallas_call | solution.py:565
  91.9 1.5 collective-permute-start.14
  93.4 3.5 %collective-permute-done.9.before_ref = bf16[272,1024]{1,0:T(8,128)(2,1)} collective-permute-done((bf16[272,1024]{1,0:T(8,128)(2,1)}, bf16[272,1024]{1,0:T(8,128)(2,1)}, u32[]{:S(2)}, u32[]{:S(2)}) %collective-permute-start.9) | collective-permute-done | bytes 557088 | tf_op jit(solution)/shard_map/ppermute | solution.py:600
  96.9 1.2 inclusive.5.refs_0_
  98.1 8.3 %collective-permute-start.11 = (bf16[272,1024]{1,0:T(8,128)(2,1)S(1)}, bf16[272,1024]{1,0:T(8,128)(2,1)S(1)}, u32[]{:S(2)}, u32[]{:S(2)}) collective-permute-start(bf16[272,1024]{1,0:T(8,128)(2,1)S(1)} %inclusive.5.refs_0_), channel_id=1, source_target_pairs={{0,16},{4,20},{8,24},{12,28},{1,17},{5,21},{9,25},{13,29},{2,18},{... | collective-permute-start | bytes 1671176 | tf_op jit(solution)/shard_map/ppermute | solution.py:600
  106.4 1.5 last.4
  109.0 6.3 %spans.4.refs_0_.refs_6_ = bf16[1024,1024]{1,0:T(8,128)(2,1)S(1)} custom-call(bf16[1024,1024]{1,0:T(8,128)(2,1)S(1)} %copy-done.18, bf16[1024,512]{1,0:T(8,128)(2,1)S(1)} %get-tuple-element.40.refs_0_.map_ref.out_ref, f32[1024,128]{1,0:T(8,128)S(1)} %get-tuple-element.49.col_ref, f32[64,1024]{1,0:T(8,128)S(1)} %get-tuple-element.50.row_ref, ...), custom_call_target="tpu_custom_call" | custom-call | flops 1000000000 | bytes 1 | tf_op jit(solution)/shard_map/spans/pallas_call | solution.py:343
  115.3 12.5 %spans.5.refs_7_.refs_0_ = bf16[1024,2048]{1,0:T(8,128)(2,1)S(1)} custom-call(bf16[1024,2048]{1,0:T(8,128)(2,1)} %copy-done.14, bf16[1024,512]{1,0:T(8,128)(2,1)S(1)} %get-tuple-element.46.refs_0_.map_ref.out_ref, f32[1024,128]{1,0:T(8,128)S(1)} %get-tuple-element.49.col_ref, f32[64,1024]{1,0:T(8,128)S(1)} %get-tuple-element.50.row_ref, ...), custom_call_target="tpu_custom_call" | custom-call | flops 1000000000 | bytes 1 | tf_op jit(solution)/shard_map/spans/pallas_call | solution.py:343
  127.8 2.0 copy-done.2
  129.9 3.4 %back_rest.2.refs_0_ = bf16[272,1024]{1,0:T(8,128)(2,1)} custom-call(s32[2]{0:T(128)S(1)} %copy-done.39, bf16[1024,512]{1,0:T(8,128)(2,1)S(1)} %get-tuple-element.40.refs_0_.map_ref.out_ref, bf16[1024,512]{1,0:T(8,128)(2,1)S(1)} %get-tuple-element.38.dev_ref.edev_ref.table_ref, bf16[1024,1024]{1,0:T(8,128)(2,1)S(1)} %spans.4.refs_0_.refs_6_, ...), custom_call_target="tpu_custom_call" | custom-call | flops 1000000000 | bytes 1 | tf_op jit(solution)/shard_map/back_rest/pallas_call | solution.py:565
  133.4 2.7 %last.5 = (bf16[256,1024]{1,0:T(8,128)(2,1)S(1)}, bf16[256,1024]{1,0:T(8,128)(2,1)}) custom-call(s32[2]{0:T(128)S(1)} %copy-done.39, bf16[272,1024]{1,0:T(8,128)(2,1)} %collective-permute-done.9.before_ref, bf16[272,1024]{1,0:T(8,128)(2,1)S(1)} %collective-permute-done.11.far_ref, f32[264,1024]{1,0:T(8,128)S(1)} %copy-done.36, ...), custom_call_target="tpu_custom_call" | custom-call | flops 700000000 | bytes 1 | tf_op jit(solution)/shard_map/last/pallas_call | solution.py:425
  137.1 3.4 %back_rest.3.refs_12_ = bf16[272,1024]{1,0:T(8,128)(2,1)} custom-call(s32[2]{0:T(128)S(1)} %copy-done.39, bf16[1024,512]{1,0:T(8,128)(2,1)S(1)} %get-tuple-element.40.refs_0_.map_ref.out_ref, bf16[1024,512]{1,0:T(8,128)(2,1)S(1)} %get-tuple-element.38.dev_ref.edev_ref.table_ref, bf16[1024,1024]{1,0:T(8,128)(2,1)S(1)} %spans.4.refs_0_.refs_6_, ...), custom_call_target="tpu_custom_call" | custom-call | flops 1000000000 | bytes 1 | tf_op jit(solution)/shard_map/back_rest/pallas_call | solution.py:565
  140.6 1.5 collective-permute-start.17
  142.1 1.2 copy-done.5
  143.3 1.6 copy-done.7
  144.9 1.2 copy-done.10
  149.0 3.3 %back_whole.6.refs_6_ = bf16[256,2048]{1,0:T(8,128)(2,1)S(1)} custom-call(s32[2]{0:T(128)S(1)} %copy-done.39, bf16[1024,512]{1,0:T(8,128)(2,1)S(1)} %copy-done.10, bf16[1024,512]{1,0:T(8,128)(2,1)S(1)} %copy-done.5, bf16[1024,1024]{1,0:T(8,128)(2,1)S(1)} %copy-done.7, bf16[256,512]{1,0:T(8,128)(2,1)S(1)} %copy-done.20, bf16[256,512]{1,0:T(8,128)(2,1)S(1)} %copy-done.23, ...), custom_call_target="tpu_custom_call" | custom-call | flops 1000000000 | bytes 1 | tf_op jit(solution)/shard_map/back_whole/pallas_call | solution.py:565
  153.1 3.6 %back_whole.7.refs_6_ = bf16[256,2048]{1,0:T(8,128)(2,1)S(1)} custom-call(s32[2]{0:T(128)S(1)} %copy-done.39, bf16[1024,512]{1,0:T(8,128)(2,1)S(1)} %copy-done.13, bf16[1024,512]{1,0:T(8,128)(2,1)S(1)} %copy-done.5, bf16[1024,2048]{1,0:T(8,128)(2,1)} %copy-done.2, bf16[256,1024]{1,0:T(8,128)(2,1)S(1)} %copy-done.16, ...), custom_call_target="tpu_custom_call" | custom-call | flops 1000000000 | bytes 1 | tf_op jit(solution)/shard_map/back_whole/pallas_call | solution.py:565
  158.0 3.6 %back_whole.8.refs_6_ = bf16[256,2048]{1,0:T(8,128)(2,1)S(1)} custom-call(s32[2]{0:T(128)S(1)} %copy-done.39, bf16[1024,512]{1,0:T(8,128)(2,1)S(1)} %copy-done.13, bf16[1024,512]{1,0:T(8,128)(2,1)S(1)} %copy-done.5, bf16[1024,2048]{1,0:T(8,128)(2,1)} %copy-done.2, bf16[256,1024]{1,0:T(8,128)(2,1)S(1)} %copy-done.16, ...), custom_call_target="tpu_custom_call" | custom-call | flops 1000000000 | bytes 1 | tf_op jit(solution)/shard_map/back_whole/pallas_call | solution.py:565
  162.2 3.6 %back_whole.9.refs_12_.refs_7_ = bf16[256,2048]{1,0:T(8,128)(2,1)S(1)} custom-call(s32[2]{0:T(128)S(1)} %copy-done.39, bf16[1024,512]{1,0:T(8,128)(2,1)S(1)} %copy-done.13, bf16[1024,512]{1,0:T(8,128)(2,1)S(1)} %copy-done.5, bf16[1024,2048]{1,0:T(8,128)(2,1)} %copy-done.2, bf16[256,1024]{1,0:T(8,128)(2,1)S(1)} %copy-done.16, ...), custom_call_target="tpu_custom_call" | custom-call | flops 1000000000 | bytes 1 | tf_op jit(solution)/shard_map/back_whole/pallas_call | solution.py:565
  166.8 4.0 %back_whole.10 = bf16[256,16384]{1,0:T(8,128)(2,1)} custom-call(s32[2]{0:T(128)S(1)} %copy-done.39, bf16[1024,512]{1,0:T(8,128)(2,1)S(1)} %copy-done.11, bf16[1024,512]{1,0:T(8,128)(2,1)S(1)} %copy-done.5, bf16[1024,1024]{1,0:T(8,128)(2,1)S(1)} %copy-done.8, bf16[256,512]{1,0:T(8,128)(2,1)S(1)} %copy-done.21, bf16[256,512]{1,0:T(8,128)(2,1)S(1)} %copy-done.24, ...), custom_call_target="tpu_custom_call" | custom-call | flops 1000000000 | bytes 1 | tf_op jit(solution)/shard_map/back_whole/pallas_call | solution.py:565
  170.8 2.1 %fusion = bf16[256,16384]{1,0:T(8,128)(2,1)} fusion(bf16[256,16384]{1,0:T(8,128)(2,1)} %back_whole.10, s32[]{:T(128)S(6)} %select_n.32, bf16[256,1024]{1,0:T(8,128)(2,1)} %collective-permute-done.13.refs_8_, f32[256]{0:T(256)S(1)} %bitcast.19), kind=kLoop, calls=%fused_computation.2 | loop fusion | flops 786432 | bytes 1049604 | tf_op jit(solution)/shard_map/dynamic_update_slice | solution.py:761
  173.0 1.9 slice_dynamic-update-slice_fusion.1
  175.5 2.0 fusion.1
  177.5 1.9 slice_dynamic-update-slice_fusion
  180.5 4.3 %back_whole.11 = bf16[256,16384]{1,0:T(8,128)(2,1)} custom-call(s32[2]{0:T(128)S(1)} %copy-done.39, bf16[1024,512]{1,0:T(8,128)(2,1)S(1)} %copy-done.13, bf16[1024,512]{1,0:T(8,128)(2,1)S(1)} %copy-done.5, bf16[1024,2048]{1,0:T(8,128)(2,1)S(1)} %copy-done.3, bf16[256,1024]{1,0:T(8,128)(2,1)S(1)} %copy-done.16, ...), custom_call_target="tpu_custom_call", output_to_operand_aliasing={{}: (9, {})} | custom-call | flops 1000000000 | bytes 1 | tf_op jit(solution)/shard_map/back_whole/pallas_call | solution.py:565
  186.9 18.5 %collective-permute-done.21 = bf16[256,2048]{1,0:T(8,128)(2,1)S(1)} collective-permute-done((bf16[256,2048]{1,0:T(8,128)(2,1)S(1)}, bf16[256,2048]{1,0:T(8,128)(2,1)S(1)}, u32[]{:S(2)}, u32[]{:S(2)}) %collective-permute-start.21) | collective-permute-done | bytes 1048608 | tf_op jit(solution)/shard_map/ppermute | solution.py:716
  (146 shorter events, 24.2 us)
Async XLA Ops:
  0.7 13.1 %collective-permute-start = (bf16[3,2,512]{2,1,0:T(2,128)(2,1)S(1)}, bf16[3,2,512]{2,1,0:T(2,128)(2,1)S(1)}, u32[]{:S(2)}, u32[]{:S(2)}) collective-permute-start(bf16[3,2,512]{2,1,0:T(2,128)(2,1)S(1)} %slice.24), channel_id=1, source_target_pairs={{0,4},{4,8},{8,12},{12,16},{16,20},{20,24},{24,28},{1,5},{5,9},{9,... | collective-permute-start | bytes 18440 | tf_op jit(solution)/shard_map/ppermute | solution.py:675
  6.4 12.8 %collective-permute-start.1 = (bf16[3,4096]{1,0:T(4,128)(2,1)S(1)}, bf16[3,4096]{1,0:T(4,128)(2,1)S(1)}, u32[]{:S(2)}, u32[]{:S(2)}) collective-permute-start(bf16[3,4096]{1,0:T(4,128)(2,1)S(1)} %slice.25), channel_id=1, source_target_pairs={{0,4},{4,8},{8,12},{12,16},{16,20},{20,24},{24,28},{1,5},{5,9},{9,... | collective-permute-start | bytes 73736 | tf_op jit(solution)/shard_map/ppermute | solution.py:674
  12.4 6.8 %copy-start = (bf16[128,4096]{1,0:T(8,128)(2,1)S(1)}, bf16[128,4096]{1,0:T(8,128)(2,1)}, u32[]{:S(2)}) copy-start(bf16[128,4096]{1,0:T(8,128)(2,1)} %constant.47.clone.spread_ref.refs_3_.refs_9_) | copy-start | bytes 3145732
  12.4 6.8 %copy-start.50 = (bf16[4,4096]{1,0:T(4,128)(2,1)S(1)}, bf16[4,4096]{1,0:T(4,128)(2,1)}, u32[]{:S(2)}) copy-start(bf16[4,4096]{1,0:T(4,128)(2,1)} %taps_ref.9) | copy-start | bytes 98308
  13.7 48.7 %copy-start.40 = (bf16[16,128]{1,0:T(8,128)(2,1)}, bf16[16,128]{1,0:T(8,128)(2,1)S(1)}, u32[]{:S(2)}) copy-start(bf16[16,128]{1,0:T(8,128)(2,1)S(1)} %get-tuple-element.51.skips_ref) | copy-start | bytes 12292
  13.7 123.4 %copy-start.4 = (bf16[1024,512]{1,0:T(8,128)(2,1)}, bf16[1024,512]{1,0:T(8,128)(2,1)S(1)}, u32[]{:S(2)}) copy-start(bf16[1024,512]{1,0:T(8,128)(2,1)S(1)} %get-tuple-element.38.dev_ref.edev_ref.table_ref) | copy-start | bytes 3145732
  13.8 44.6 %copy-start.37 = (s32[2]{0:T(128)}, s32[2]{0:T(128)S(1)}, u32[]{:S(2)}) copy-start(s32[2]{0:T(128)S(1)} %pad_add_fusion.where_ref) | copy-start | bytes 28
  19.2 118.0 %copy-start.9 = (bf16[1024,512]{1,0:T(8,128)(2,1)}, bf16[1024,512]{1,0:T(8,128)(2,1)S(1)}, u32[]{:S(2)}) copy-start(bf16[1024,512]{1,0:T(8,128)(2,1)S(1)} %get-tuple-element.40.refs_0_.map_ref.out_ref) | copy-start | bytes 3145732
  25.3 9.2 %copy-start.29 = (f32[264,512]{1,0:T(8,128)}, f32[264,512]{1,0:T(8,128)S(1)}, u32[]{:S(2)}) copy-start(f32[264,512]{1,0:T(8,128)S(1)} %get-tuple-element.41.kept_ref) | copy-start | bytes 1622020
  25.4 8.3 %collective-permute-start.2 = (bf16[272,512]{1,0:T(8,128)(2,1)S(1)}, bf16[272,512]{1,0:T(8,128)(2,1)S(1)}, u32[]{:S(2)}, u32[]{:S(2)}) collective-permute-start(bf16[272,512]{1,0:T(8,128)(2,1)S(1)} %get-tuple-element.42), channel_id=1, source_target_pairs={{0,4},{4,0},{8,12},{12,8},{16,20},{20,16},{24,28},{28,24},{1,5},{5... | collective-permute-start | bytes 835592 | tf_op jit(solution)/shard_map/ppermute | solution.py:608
  26.9 7.6 %copy-start.45 = (bf16[1024,2,512]{2,1,0:T(2,128)(2,1)S(1)}, bf16[1024,2,512]{2,1,0:T(2,128)(2,1)}, u32[]{:S(2)}) copy-start(bf16[1024,2,512]{2,1,0:T(2,128)(2,1)} %io_ref.3) | copy-start | bytes 6291460
  33.1 7.8 %copy-start.17 = (bf16[1024,1024]{1,0:T(8,128)(2,1)}, bf16[1024,1024]{1,0:T(8,128)(2,1)S(1)}, u32[]{:S(2)}) copy-start(bf16[1024,1024]{1,0:T(8,128)(2,1)S(1)} %get-tuple-element.44.refs_0_.xh_ref) | copy-start | bytes 6291460
  33.1 25.3 %collective-permute-start.3 = (bf16[272,512]{1,0:T(8,128)(2,1)S(1)}, bf16[272,512]{1,0:T(8,128)(2,1)S(1)}, u32[]{:S(2)}, u32[]{:S(2)}) collective-permute-start(bf16[272,512]{1,0:T(8,128)(2,1)S(1)} %get-tuple-element.53), channel_id=1, source_target_pairs={{0,4},{4,0},{8,12},{12,8},{16,20},{20,16},{24,28},{28,24},{1,5},{5... | collective-permute-start | bytes 835592 | tf_op jit(solution)/shard_map/ppermute | solution.py:608
  37.4 77.9 %copy-start.12 = (bf16[1024,512]{1,0:T(8,128)(2,1)}, bf16[1024,512]{1,0:T(8,128)(2,1)S(1)}, u32[]{:S(2)}) copy-start(bf16[1024,512]{1,0:T(8,128)(2,1)S(1)} %get-tuple-element.46.refs_0_.map_ref.out_ref) | copy-start | bytes 3145732
  37.4 16.3 %collective-permute-start.4 = (bf16[272,512]{1,0:T(8,128)(2,1)S(1)}, bf16[272,512]{1,0:T(8,128)(2,1)S(1)}, u32[]{:S(2)}, u32[]{:S(2)}) collective-permute-start(bf16[272,512]{1,0:T(8,128)(2,1)S(1)} %get-tuple-element.54), channel_id=1, source_target_pairs={{0,8},{4,12},{8,16},{12,20},{16,24},{20,28},{1,9},{5,13},{9,17},{1... | collective-permute-start | bytes 835592 | tf_op jit(solution)/shard_map/ppermute | solution.py:600
  40.9 21.5 %copy-start.42 = (bf16[2,128]{1,0:T(2,128)(2,1)S(1)}, bf16[2,128]{1,0:T(2,128)(2,1)}, u32[]{:S(2)}) copy-start(bf16[2,128]{1,0:T(2,128)(2,1)} %constant.48.clone.halves_ref) | copy-start | bytes 1540
  52.2 10.2 %copy-start.14 = (bf16[1024,2048]{1,0:T(8,128)(2,1)}, bf16[1024,2048]{1,0:T(8,128)(2,1)S(1)}, u32[]{:S(2)}) copy-start(bf16[1024,2048]{1,0:T(8,128)(2,1)S(1)} %get-tuple-element.48.refs_0_.xh_ref) | copy-start | bytes 12582916
  52.2 28.7 %copy-start.35 = (f32[264,1024]{1,0:T(8,128)}, f32[264,1024]{1,0:T(8,128)S(1)}, u32[]{:S(2)}) copy-start(f32[264,1024]{1,0:T(8,128)S(1)} %get-tuple-element.58.kept_ref) | copy-start | bytes 3244036
  52.2 28.7 %collective-permute-start.8 = (bf16[272,1024]{1,0:T(8,128)(2,1)}, bf16[272,1024]{1,0:T(8,128)(2,1)}, u32[]{:S(2)}, u32[]{:S(2)}) collective-permute-start(bf16[272,1024]{1,0:T(8,128)(2,1)} %get-tuple-element.59), channel_id=1, source_target_pairs={{0,4},{4,0},{8,12},{12,8},{16,20},{20,16},{24,28},{28,24},{1,5},{5... | collective-permute-start | bytes 1671176 | tf_op jit(solution)/shard_map/ppermute | solution.py:608
  53.7 15.0 %copy-start.33 = (bf16[272,512]{1,0:T(8,128)(2,1)}, bf16[272,512]{1,0:T(8,128)(2,1)S(1)}, u32[]{:S(2)}) copy-start(bf16[272,512]{1,0:T(8,128)(2,1)S(1)} %collective-permute-done.4.before_ref) | copy-start | bytes 835588
  54.7 14.1 %collective-permute-start.6 = (bf16[272,512]{1,0:T(8,128)(2,1)}, bf16[272,512]{1,0:T(8,128)(2,1)}, u32[]{:S(2)}, u32[]{:S(2)}) collective-permute-start(bf16[272,512]{1,0:T(8,128)(2,1)} %inclusive.3.refs_0_), channel_id=1, source_target_pairs={{0,16},{4,20},{8,24},{12,28},{1,17},{5,21},{9,25},{13,29},{2,18},{... | collective-permute-start | bytes 835592 | tf_op jit(solution)/shard_map/ppermute | solution.py:600
  59.9 12.1 %collective-permute-start.5 = (bf16[272,512]{1,0:T(8,128)(2,1)}, bf16[272,512]{1,0:T(8,128)(2,1)}, u32[]{:S(2)}, u32[]{:S(2)}) collective-permute-start(bf16[272,512]{1,0:T(8,128)(2,1)} %get-tuple-element.55), channel_id=1, source_target_pairs={{0,8},{4,12},{8,16},{12,20},{16,24},{20,28},{1,9},{5,13},{9,17},{1... | collective-permute-start | bytes 835592 | tf_op jit(solution)/shard_map/ppermute | solution.py:600
  68.7 20.0 %copy-start.6 = (bf16[1024,1024]{1,0:T(8,128)(2,1)}, bf16[1024,1024]{1,0:T(8,128)(2,1)S(1)}, u32[]{:S(2)}) copy-start(bf16[1024,1024]{1,0:T(8,128)(2,1)S(1)} %spans.3.refs_0_) | copy-start | bytes 6291460
  68.8 16.9 %copy-start.27 = (f32[4096]{0:T(1024)S(1)}, f32[4096]{0:T(1024)}, u32[]{:S(2)}) copy-start(f32[4096]{0:T(1024)} %param.19) | copy-start | bytes 49156
  71.1 17.6 %copy-start.19 = (bf16[256,512]{1,0:T(8,128)(2,1)}, bf16[256,512]{1,0:T(8,128)(2,1)S(1)}, u32[]{:S(2)}) copy-start(bf16[256,512]{1,0:T(8,128)(2,1)S(1)} %get-tuple-element.57.refs_0_.refs_1_) | copy-start | bytes 786436
  71.1 14.6 %collective-permute-start.10 = (bf16[256,512]{1,0:T(8,128)(2,1)S(1)}, bf16[256,512]{1,0:T(8,128)(2,1)S(1)}, u32[]{:S(2)}, u32[]{:S(2)}) collective-permute-start(bf16[256,512]{1,0:T(8,128)(2,1)S(1)} %get-tuple-element.62), channel_id=1, source_target_pairs={{0,4},{4,0},{8,12},{12,8},{16,20},{20,16},{24,28},{28,24},{1,5},{5... | collective-permute-start | bytes 786440 | tf_op jit(solution)/shard_map/ppermute | solution.py:608
  73.7 32.7 %collective-permute-start.7 = (bf16[272,512]{1,0:T(8,128)(2,1)}, bf16[272,512]{1,0:T(8,128)(2,1)}, u32[]{:S(2)}, u32[]{:S(2)}) collective-permute-start(bf16[272,512]{1,0:T(8,128)(2,1)} %inclusive.4.refs_0_), channel_id=1, source_target_pairs={{0,16},{4,20},{8,24},{12,28},{1,17},{5,21},{9,25},{13,29},{2,18},{... | collective-permute-start | bytes 835592 | tf_op jit(solution)/shard_map/ppermute | solution.py:600
  83.0 13.9 %collective-permute-start.9 = (bf16[272,1024]{1,0:T(8,128)(2,1)}, bf16[272,1024]{1,0:T(8,128)(2,1)}, u32[]{:S(2)}, u32[]{:S(2)}) collective-permute-start(bf16[272,1024]{1,0:T(8,128)(2,1)} %get-tuple-element.61), channel_id=1, source_target_pairs={{0,8},{4,12},{8,16},{12,20},{16,24},{20,28},{1,9},{5,13},{9,17},{1... | collective-permute-start | bytes 1671176 | tf_op jit(solution)/shard_map/ppermute | solution.py:600
  88.8 41.1 %collective-permute-start.13 = (bf16[256,1024]{1,0:T(8,128)(2,1)}, bf16[256,1024]{1,0:T(8,128)(2,1)}, u32[]{:S(2)}, u32[]{:S(2)}) collective-permute-start(bf16[256,1024]{1,0:T(8,128)(2,1)} %get-tuple-element.63.refs_6_), channel_id=1, source_target_pairs={{0,3},{1,2},{2,1},{3,0},{4,7},{5,6},{6,5},{7,4},{8,11},{9,10},{10,... | collective-permute-start | bytes 1572872 | tf_op jit(solution)/shard_map/ppermute | solution.py:716
  91.9 38.0 %collective-permute-start.14 = (bf16[256,1024]{1,0:T(8,128)(2,1)}, bf16[256,1024]{1,0:T(8,128)(2,1)}, u32[]{:S(2)}, u32[]{:S(2)}) collective-permute-start(bf16[256,1024]{1,0:T(8,128)(2,1)} %get-tuple-element.64.refs_0_), channel_id=1, source_target_pairs={{0,2},{1,3},{2,0},{3,1},{4,6},{5,7},{6,4},{7,5},{8,10},{9,11},{10,... | collective-permute-start | bytes 1572872 | tf_op jit(solution)/shard_map/ppermute | solution.py:716
  93.4 13.0 %copy-start.39 = (s32[2]{0:T(128)S(1)}, s32[2]{0:T(128)}, u32[]{:S(2)}) copy-start(s32[2]{0:T(128)} %copy-done.37) | copy-start | bytes 28
  93.4 13.0 %copy-start.47 = (bf16[272,512]{1,0:T(8,128)(2,1)S(1)}, bf16[272,512]{1,0:T(8,128)(2,1)}, u32[]{:S(2)}) copy-start(bf16[272,512]{1,0:T(8,128)(2,1)} %copy-done.46) | copy-start | bytes 835588
  93.4 15.6 %copy-start.18 = (bf16[1024,1024]{1,0:T(8,128)(2,1)S(1)}, bf16[1024,1024]{1,0:T(8,128)(2,1)}, u32[]{:S(2)}) copy-start(bf16[1024,1024]{1,0:T(8,128)(2,1)} %copy-done.17) | copy-start | bytes 6291460
  93.4 15.6 %copy-start.41 = (bf16[16,128]{1,0:T(8,128)(2,1)S(1)}, bf16[16,128]{1,0:T(8,128)(2,1)}, u32[]{:S(2)}) copy-start(bf16[16,128]{1,0:T(8,128)(2,1)} %copy-done.40) | copy-start | bytes 12292
  93.4 15.6 %copy-start.43 = (bf16[2,128]{1,0:T(2,128)(2,1)S(1)}, bf16[2,128]{1,0:T(2,128)(2,1)}, u32[]{:S(2)}) copy-start(bf16[2,128]{1,0:T(2,128)(2,1)} %constant.48.clone.halves_ref) | copy-start | bytes 1540
  93.4 21.9 %copy-start.1 = (bf16[128,4096]{1,0:T(8,128)(2,1)S(1)}, bf16[128,4096]{1,0:T(8,128)(2,1)}, u32[]{:S(2)}) copy-start(bf16[128,4096]{1,0:T(8,128)(2,1)} %constant.47.clone.spread_ref.refs_3_.refs_9_) | copy-start | bytes 3145732
  98.1 35.2 %collective-permute-start.11 = (bf16[272,1024]{1,0:T(8,128)(2,1)S(1)}, bf16[272,1024]{1,0:T(8,128)(2,1)S(1)}, u32[]{:S(2)}, u32[]{:S(2)}) collective-permute-start(bf16[272,1024]{1,0:T(8,128)(2,1)S(1)} %inclusive.5.refs_0_), channel_id=1, source_target_pairs={{0,16},{4,20},{8,24},{12,28},{1,17},{5,21},{9,25},{13,29},{2,18},{... | collective-permute-start | bytes 1671176 | tf_op jit(solution)/shard_map/ppermute | solution.py:600
  107.9 22.0 %collective-permute-start.12 = (bf16[256,512]{1,0:T(8,128)(2,1)S(1)}, bf16[256,512]{1,0:T(8,128)(2,1)S(1)}, u32[]{:S(2)}, u32[]{:S(2)}) collective-permute-start(bf16[256,512]{1,0:T(8,128)(2,1)S(1)} %get-tuple-element.66), channel_id=1, source_target_pairs={{0,4},{4,0},{8,12},{12,8},{16,20},{20,16},{24,28},{28,24},{1,5},{5... | collective-permute-start | bytes 786440 | tf_op jit(solution)/shard_map/ppermute | solution.py:608
  115.3 14.6 %copy-start.28 = (f32[4096]{0:T(1024)S(1)}, f32[4096]{0:T(1024)}, u32[]{:S(2)}) copy-start(f32[4096]{0:T(1024)} %param.19) | copy-start | bytes 49156
  129.9 7.3 %copy-start.25 = (bf16[256,512]{1,0:T(8,128)(2,1)}, bf16[256,512]{1,0:T(8,128)(2,1)S(1)}, u32[]{:S(2)}) copy-start(bf16[256,512]{1,0:T(8,128)(2,1)S(1)} %collective-permute-done.12.refs_2_.refs_8_) | copy-start | bytes 786436
  133.3 19.0 %collective-permute-start.16 = (bf16[272,1024]{1,0:T(8,128)(2,1)}, bf16[272,1024]{1,0:T(8,128)(2,1)}, u32[]{:S(2)}, u32[]{:S(2)}) collective-permute-start(bf16[272,1024]{1,0:T(8,128)(2,1)} %back_rest.2.refs_0_), channel_id=1, source_target_pairs={{0,3},{1,2},{2,1},{3,0},{4,7},{5,6},{6,5},{7,4},{8,11},{9,10},{10,... | collective-permute-start | bytes 1671176 | tf_op jit(solution)/shard_map/ppermute | solution.py:716
  136.1 17.0 %collective-permute-start.15 = (bf16[256,1024]{1,0:T(8,128)(2,1)}, bf16[256,1024]{1,0:T(8,128)(2,1)}, u32[]{:S(2)}, u32[]{:S(2)}) collective-permute-start(bf16[256,1024]{1,0:T(8,128)(2,1)} %get-tuple-element.69), channel_id=1, source_target_pairs={{0,4},{4,0},{8,12},{12,8},{16,20},{20,16},{24,28},{28,24},{1,5},{5... | collective-permute-start | bytes 1572872 | tf_op jit(solution)/shard_map/ppermute | solution.py:608
  140.6 21.6 %collective-permute-start.17 = (bf16[272,1024]{1,0:T(8,128)(2,1)}, bf16[272,1024]{1,0:T(8,128)(2,1)}, u32[]{:S(2)}, u32[]{:S(2)}) collective-permute-start(bf16[272,1024]{1,0:T(8,128)(2,1)} %back_rest.3.refs_12_), channel_id=1, source_target_pairs={{0,2},{1,3},{2,0},{3,1},{4,6},{5,7},{6,4},{7,5},{8,10},{9,11},{10,... | collective-permute-start | bytes 1671176 | tf_op jit(solution)/shard_map/ppermute | solution.py:716
  152.3 27.1 %collective-permute-start.18 = (bf16[256,2048]{1,0:T(8,128)(2,1)S(1)}, bf16[256,2048]{1,0:T(8,128)(2,1)S(1)}, u32[]{:S(2)}, u32[]{:S(2)}) collective-permute-start(bf16[256,2048]{1,0:T(8,128)(2,1)S(1)} %back_whole.6.refs_6_), channel_id=1, source_target_pairs={{0,1},{1,0},{2,3},{3,2},{4,5},{5,4},{6,7},{7,6},{8,9},{9,8},{10,11... | collective-permute-start | bytes 3145736 | tf_op jit(solution)/shard_map/ppermute | solution.py:716
  156.8 28.0 %collective-permute-start.19 = (bf16[256,2048]{1,0:T(8,128)(2,1)S(1)}, bf16[256,2048]{1,0:T(8,128)(2,1)S(1)}, u32[]{:S(2)}, u32[]{:S(2)}) collective-permute-start(bf16[256,2048]{1,0:T(8,128)(2,1)S(1)} %back_whole.7.refs_6_), channel_id=1, source_target_pairs={{0,3},{1,2},{2,1},{3,0},{4,7},{5,6},{6,5},{7,4},{8,11},{9,10},{10,... | collective-permute-start | bytes 3145736 | tf_op jit(solution)/shard_map/ppermute | solution.py:716
  161.7 24.2 %collective-permute-start.20 = (bf16[256,2048]{1,0:T(8,128)(2,1)S(1)}, bf16[256,2048]{1,0:T(8,128)(2,1)S(1)}, u32[]{:S(2)}, u32[]{:S(2)}) collective-permute-start(bf16[256,2048]{1,0:T(8,128)(2,1)S(1)} %back_whole.8.refs_6_), channel_id=1, source_target_pairs={{0,1},{1,0},{2,3},{3,2},{4,5},{5,4},{6,7},{7,6},{8,9},{9,8},{10,11... | collective-permute-start | bytes 3145736 | tf_op jit(solution)/shard_map/ppermute | solution.py:716
  165.9 39.5 %collective-permute-start.21 = (bf16[256,2048]{1,0:T(8,128)(2,1)S(1)}, bf16[256,2048]{1,0:T(8,128)(2,1)S(1)}, u32[]{:S(2)}, u32[]{:S(2)}) collective-permute-start(bf16[256,2048]{1,0:T(8,128)(2,1)S(1)} %back_whole.9.refs_12_.refs_7_), channel_id=1, source_target_pairs={{0,2},{1,3},{2,0},{3,1},{4,6},{5,7},{6,4},{7,5},{8,10},{9,11},{10,... | collective-permute-start | bytes 3145736 | tf_op jit(solution)/shard_map/ppermute | solution.py:716
  170.8 9.6 %copy-start.3 = (bf16[1024,2048]{1,0:T(8,128)(2,1)S(1)}, bf16[1024,2048]{1,0:T(8,128)(2,1)}, u32[]{:S(2)}) copy-start(bf16[1024,2048]{1,0:T(8,128)(2,1)} %copy-done.2) | copy-start | bytes 12582916
  (27 other events, 82.2 us)

commit v3 on v1

--- a/solution.py
+++ b/solution.py
@@ -114,7 +114,7 @@
         ),
         compiler_params=params(),
         name="decays",
-        cost_estimate=cost(1.5),
+        cost_estimate=cost(50),
     )(log_decay, step_size, skip_gain[None])
 
 

time: 201 us -> 198 us (0.985)
  local copies, waits for them, and re-layouts: 21.3 us -> 18.9 us
    unnamed x92 -> x90, local copies, waits for them, and re-layouts: 11.6 us -> 9.23 us
  transfers between devices with their start and end apart: 22 -> 22, of which waited for: 4 -> 4; matrix products, arithmetic and copies ran while one was open for 7% -> 7% of each run, Pallas kernels for 51% -> 52%
where the time goes in v3:
time: 198 us; the launch traced here: 197 us
  Pallas kernels  109 us (55%)
  starting transfers between devices  38.6 us (19%)
  waiting for transfers between devices  24.8 us (13%)
  local copies, waits for them, and re-layouts  18.9 us (10%)
  other arithmetic  5.44 us (3%)
    pallas_call x10, Pallas kernels, back(): pl.pallas_call(functools.partial(back_kernel, mode, [len(ys) for _, ys, _...  35.9 us
    pallas_call x3, Pallas kernels, spans_of(): pl.pallas_call(functools.partial(span_kernel, index * some, len(after)),...  28 us
    pallas_call x3, Pallas kernels, front(): pl.pallas_call(functools.partial(front_kernel, len(after), blocks), grid_...  24.3 us
    ppermute x8, waiting for transfers between devices, ship(): return lax.ppermute(piece, 'head', [(i, i ^ r) for i in range(head_size)])  20.8 us
    ppermute x6, starting transfers between devices, shifted(): lax.ppermute(value, 'ctx', [(2 * q + y, 2 * (q + steps) + y) for q in ran...  19.1 us
    pallas_call x9, Pallas kernels, join(): pl.pallas_call(kernel, in_specs=[pl.BlockSpec(memory_space=pltpu.SMEM)] *...  13.6 us
    unnamed x90, local copies, waits for them, and re-layouts  9.23 us
    ppermute x6, starting transfers between devices, swapped(): lax.ppermute(value, 'ctx', [(2 * q + y, 2 * q + 1 - y) for q in range(pai...  6.34 us
  transfers between devices with their start and end apart: 22, of which 4 were waited for; matrix products, arithmetic and copies ran while one was open for 7% of the time, Pallas kernels for 52%

profile of v3, /device:TPU:0, one launch (start us, length us, event | category | flops | bytes accessed | tf_op | source)
XLA Modules:
  0.0 196.9 jit_solution(7355168345623555462)
XLA Ops:
  0.7 4.9 %collective-permute-start = (bf16[3,2,512]{2,1,0:T(2,128)(2,1)S(1)}, bf16[3,2,512]{2,1,0:T(2,128)(2,1)S(1)}, u32[]{:S(2)}, u32[]{:S(2)}) collective-permute-start(bf16[3,2,512]{2,1,0:T(2,128)(2,1)S(1)} %slice.24), channel_id=1, source_target_pairs={{0,4},{4,8},{8,12},{12,16},{16,20},{20,24},{24,28},{1,5},{5,9},{9,... | collective-permute-start | bytes 18440 | tf_op jit(solution)/shard_map/ppermute | solution.py:675
  6.4 3.4 %collective-permute-start.1 = (bf16[3,4096]{1,0:T(4,128)(2,1)S(1)}, bf16[3,4096]{1,0:T(4,128)(2,1)S(1)}, u32[]{:S(2)}, u32[]{:S(2)}) collective-permute-start(bf16[3,4096]{1,0:T(4,128)(2,1)S(1)} %slice.25), channel_id=1, source_target_pairs={{0,4},{4,8},{8,12},{12,16},{16,20},{20,24},{24,28},{1,5},{5,9},{9,... | collective-permute-start | bytes 73736 | tf_op jit(solution)/shard_map/ppermute | solution.py:674
  12.4 1.2 decays.1
  14.0 2.8 %maps.2 = (bf16[1024,512]{1,0:T(8,128)(2,1)S(1)}, bf16[256,1024]{1,0:T(8,128)(2,1)S(1)}) custom-call(bf16[1024,2,512]{2,1,0:T(2,128)(2,1)S(1)} %copy-done.39, bf16[16,2,512]{2,1,0:T(2,128)(2,1)S(1)} %pad.8.halo_ref, bf16[4,2,512]{2,1,0:T(2,128)(2,1)S(1)} %copy-done.43), custom_call_target="tpu_custom_call" | custom-call | flops 3000000000 | bytes 1 | tf_op jit(solution)/shard_map/maps/pallas_call | solution.py:182
  16.9 6.9 %front.3 = (bf16[1024,1024]{1,0:T(8,128)(2,1)}, bf16[272,512]{1,0:T(8,128)(2,1)S(1)}, f32[264,512]{1,0:T(8,128)S(1)}) custom-call(s32[2]{0:T(128)S(1)} %pad_add_fusion.where_ref, bf16[1024,4096]{1,0:T(8,128)(2,1)} %feat_ref.5, bf16[16,4096]{1,0:T(8,128)(2,1)S(1)} %pad.9.halo_ref, bf16[4,4096]{1,0:T(4,128)(2,1)S(1)} %copy-done.42, ...), custom_call_target="tpu_custom_call" | custom-call | flops 4000000000 | bytes 1 | tf_op jit(solution)/shard_map/front/pallas_call | solution.py:252
  23.8 1.6 collective-permute-start.2
  25.4 6.1 %front.4 = (bf16[1024,1024]{1,0:T(8,128)(2,1)S(1)}, bf16[272,512]{1,0:T(8,128)(2,1)S(1)}, f32[264,512]{1,0:T(8,128)S(1)}) custom-call(s32[2]{0:T(128)S(1)} %pad_add_fusion.where_ref, bf16[1024,4096]{1,0:T(8,128)(2,1)} %feat_ref.5, bf16[16,4096]{1,0:T(8,128)(2,1)S(1)} %pad.9.halo_ref, bf16[4,4096]{1,0:T(4,128)(2,1)S(1)} %copy-done.42, ...), custom_call_target="tpu_custom_call" | custom-call | flops 4000000000 | bytes 1 | tf_op jit(solution)/shard_map/front/pallas_call | solution.py:252
  32.8 3.7 %collective-permute-start.4 = (bf16[272,512]{1,0:T(8,128)(2,1)S(1)}, bf16[272,512]{1,0:T(8,128)(2,1)S(1)}, u32[]{:S(2)}, u32[]{:S(2)}) collective-permute-start(bf16[272,512]{1,0:T(8,128)(2,1)S(1)} %get-tuple-element.50), channel_id=1, source_target_pairs={{0,8},{4,12},{8,16},{12,20},{16,24},{20,28},{1,9},{5,13},{9,17},{1... | collective-permute-start | bytes 835592 | tf_op jit(solution)/shard_map/ppermute | solution.py:600
  36.4 2.8 %maps.3 = (bf16[1024,512]{1,0:T(8,128)(2,1)S(1)}, bf16[256,1024]{1,0:T(8,128)(2,1)S(1)}) custom-call(bf16[1024,2,512]{2,1,0:T(2,128)(2,1)S(1)} %copy-done.39, bf16[16,2,512]{2,1,0:T(2,128)(2,1)S(1)} %pad.8.halo_ref, bf16[4,2,512]{2,1,0:T(2,128)(2,1)S(1)} %copy-done.43, f32[264,512]{1,0:T(8,128)S(1)} %get-tuple-element.45.refs_0_.total_ref), custom_call_target="tpu_custom_call" | custom-call | flops 3000000000 | bytes 1 | tf_op jit(solution)/shard_map/maps/pallas_call | solution.py:182
  39.2 1.8 collective-permute-done.4.before_ref
  42.9 6.1 %collective-permute-start.7 = (bf16[272,512]{1,0:T(8,128)(2,1)}, bf16[272,512]{1,0:T(8,128)(2,1)}, u32[]{:S(2)}, u32[]{:S(2)}) collective-permute-start(bf16[272,512]{1,0:T(8,128)(2,1)} %inclusive.3.refs_0_), channel_id=1, source_target_pairs={{0,16},{4,20},{8,24},{12,28},{1,17},{5,21},{9,25},{13,29},{2,18},{... | collective-permute-start | bytes 835592 | tf_op jit(solution)/shard_map/ppermute | solution.py:600
  49.0 1.4 pair.4
  50.4 3.0 %collective-permute-start.6 = (bf16[272,512]{1,0:T(8,128)(2,1)}, bf16[272,512]{1,0:T(8,128)(2,1)}, u32[]{:S(2)}, u32[]{:S(2)}) collective-permute-start(bf16[272,512]{1,0:T(8,128)(2,1)} %get-tuple-element.58), channel_id=1, source_target_pairs={{0,8},{4,12},{8,16},{12,20},{16,24},{20,28},{1,9},{5,13},{9,17},{1... | collective-permute-start | bytes 835592 | tf_op jit(solution)/shard_map/ppermute | solution.py:600
  53.4 11.3 %front.5 = (bf16[1024,2048]{1,0:T(8,128)(2,1)}, bf16[272,1024]{1,0:T(8,128)(2,1)}, f32[264,1024]{1,0:T(8,128)S(1)}) custom-call(s32[2]{0:T(128)S(1)} %pad_add_fusion.where_ref, bf16[1024,4096]{1,0:T(8,128)(2,1)} %feat_ref.5, bf16[16,4096]{1,0:T(8,128)(2,1)S(1)} %pad.9.halo_ref, bf16[4,4096]{1,0:T(4,128)(2,1)S(1)} %copy-done.42, ...), custom_call_target="tpu_custom_call" | custom-call | flops 4000000000 | bytes 1 | tf_op jit(solution)/shard_map/front/pallas_call | solution.py:252
  64.7 1.5 collective-permute-start.5
  66.2 7.3 %spans.3.refs_0_ = bf16[1024,1024]{1,0:T(8,128)(2,1)S(1)} custom-call(bf16[1024,1024]{1,0:T(8,128)(2,1)} %get-tuple-element.43.refs_0_.xh_ref, bf16[1024,512]{1,0:T(8,128)(2,1)S(1)} %get-tuple-element.40.refs_0_.map_ref.out_ref, f32[1024,128]{1,0:T(8,128)S(1)} %get-tuple-element.53.col_ref, f32[64,1024]{1,0:T(8,128)S(1)} %get-tuple-element.54.row_ref, ...), custom_call_target="tpu_custom_call" | custom-call | flops 199999995904 | bytes 1 | tf_op jit(solution)/shard_map/spans/pallas_call | solution.py:343
  73.5 1.4 last.3
  75.5 1.8 inclusive.4.refs_0_
  77.3 2.0 %collective-permute-start.9 = (bf16[272,512]{1,0:T(8,128)(2,1)}, bf16[272,512]{1,0:T(8,128)(2,1)}, u32[]{:S(2)}, u32[]{:S(2)}) collective-permute-start(bf16[272,512]{1,0:T(8,128)(2,1)} %inclusive.4.refs_0_), channel_id=1, source_target_pairs={{0,16},{4,20},{8,24},{12,28},{1,17},{5,21},{9,25},{13,29},{2,18},{... | collective-permute-start | bytes 835592 | tf_op jit(solution)/shard_map/ppermute | solution.py:600
  79.3 2.2 %pair.5 = (f32[264,1024]{1,0:T(8,128)S(1)}, bf16[272,1024]{1,0:T(8,128)(2,1)}) custom-call(s32[2]{0:T(128)S(1)} %pad_add_fusion.where_ref, f32[264,1024]{1,0:T(8,128)S(1)} %get-tuple-element.56.kept_ref, bf16[272,1024]{1,0:T(8,128)(2,1)} %collective-permute-done.5.got_ref, bf16[272,512]{1,0:T(8,128)(2,1)} %inclusive.4.refs_0_), custom_call_target="tpu_custom_call" | custom-call | flops 700000000 | bytes 1 | tf_op jit(solution)/shard_map/pair/pallas_call | solution.py:425
  81.5 2.2 %collective-permute-start.8 = (bf16[272,1024]{1,0:T(8,128)(2,1)}, bf16[272,1024]{1,0:T(8,128)(2,1)}, u32[]{:S(2)}, u32[]{:S(2)}) collective-permute-start(bf16[272,1024]{1,0:T(8,128)(2,1)} %get-tuple-element.61), channel_id=1, source_target_pairs={{0,8},{4,12},{8,16},{12,20},{16,24},{20,28},{1,9},{5,13},{9,17},{1... | collective-permute-start | bytes 1671176 | tf_op jit(solution)/shard_map/ppermute | solution.py:600
  83.7 3.2 %back_first.2 = (bf16[256,1024]{1,0:T(8,128)(2,1)}, f32[256,128]{1,0:T(8,128)S(1)}) custom-call(s32[2]{0:T(128)S(1)} %pad_add_fusion.where_ref, bf16[1024,512]{1,0:T(8,128)(2,1)S(1)} %get-tuple-element.40.refs_0_.map_ref.out_ref, bf16[1024,512]{1,0:T(8,128)(2,1)S(1)} %get-tuple-element.38.dev_ref.edev_ref.table_ref, bf16[1024,1024]{1,0:T(8,128)(2,1)} %copy-done.5, ...), custom_call_target="tpu_custom_call" | custom-call | flops 1000000000 | bytes 1 | tf_op jit(solution)/shard_map/back_first/pallas_call | solution.py:565
  86.9 3.2 %back_first.3 = (bf16[256,1024]{1,0:T(8,128)(2,1)}, f32[256,128]{1,0:T(8,128)S(1)}) custom-call(s32[2]{0:T(128)S(1)} %pad_add_fusion.where_ref, bf16[1024,512]{1,0:T(8,128)(2,1)S(1)} %get-tuple-element.40.refs_0_.map_ref.out_ref, bf16[1024,512]{1,0:T(8,128)(2,1)S(1)} %get-tuple-element.38.dev_ref.edev_ref.table_ref, bf16[1024,1024]{1,0:T(8,128)(2,1)} %copy-done.5, ...), custom_call_target="tpu_custom_call" | custom-call | flops 1000000000 | bytes 1 | tf_op jit(solution)/shard_map/back_first/pallas_call | solution.py:565
  90.1 1.3 collective-permute-start.14
  92.6 7.3 %spans.4.refs_0_.refs_6_ = bf16[1024,1024]{1,0:T(8,128)(2,1)S(1)} custom-call(bf16[1024,1024]{1,0:T(8,128)(2,1)} %copy-done.12, bf16[1024,512]{1,0:T(8,128)(2,1)S(1)} %get-tuple-element.40.refs_0_.map_ref.out_ref, f32[1024,128]{1,0:T(8,128)S(1)} %get-tuple-element.53.col_ref, f32[64,1024]{1,0:T(8,128)S(1)} %get-tuple-element.54.row_ref, ...), custom_call_target="tpu_custom_call" | custom-call | flops 1000000000 | bytes 1 | tf_op jit(solution)/shard_map/spans/pallas_call | solution.py:343
  100.0 1.7 last.4
  101.7 1.2 inclusive.5.refs_0_
  102.9 2.1 %collective-permute-start.11 = (bf16[272,1024]{1,0:T(8,128)(2,1)S(1)}, bf16[272,1024]{1,0:T(8,128)(2,1)S(1)}, u32[]{:S(2)}, u32[]{:S(2)}) collective-permute-start(bf16[272,1024]{1,0:T(8,128)(2,1)S(1)} %inclusive.5.refs_0_), channel_id=1, source_target_pairs={{0,16},{4,20},{8,24},{12,28},{1,17},{5,21},{9,25},{13,29},{2,18},{... | collective-permute-start | bytes 1671176 | tf_op jit(solution)/shard_map/ppermute | solution.py:600
  105.1 1.7 collective-permute-start.12
  106.8 13.4 %spans.5.refs_7_.refs_0_ = bf16[1024,2048]{1,0:T(8,128)(2,1)} custom-call(bf16[1024,2048]{1,0:T(8,128)(2,1)} %get-tuple-element.52.refs_0_.xh_ref, bf16[1024,512]{1,0:T(8,128)(2,1)S(1)} %copy-done.10, f32[1024,128]{1,0:T(8,128)S(1)} %get-tuple-element.53.col_ref, f32[64,1024]{1,0:T(8,128)S(1)} %get-tuple-element.54.row_ref, ...), custom_call_target="tpu_custom_call" | custom-call | flops 1000000000 | bytes 1 | tf_op jit(solution)/shard_map/spans/pallas_call | solution.py:343
  120.2 3.5 %back_rest.2.refs_0_ = bf16[272,1024]{1,0:T(8,128)(2,1)} custom-call(s32[2]{0:T(128)S(1)} %copy-done.37, bf16[1024,512]{1,0:T(8,128)(2,1)S(1)} %get-tuple-element.40.refs_0_.map_ref.out_ref, bf16[1024,512]{1,0:T(8,128)(2,1)S(1)} %get-tuple-element.38.dev_ref.edev_ref.table_ref, bf16[1024,1024]{1,0:T(8,128)(2,1)} %copy-done.4, ...), custom_call_target="tpu_custom_call" | custom-call | flops 1000000000 | bytes 1 | tf_op jit(solution)/shard_map/back_rest/pallas_call | solution.py:565
  124.9 2.5 %last.5 = (bf16[256,1024]{1,0:T(8,128)(2,1)S(1)}, bf16[256,1024]{1,0:T(8,128)(2,1)}) custom-call(s32[2]{0:T(128)S(1)} %copy-done.37, bf16[272,1024]{1,0:T(8,128)(2,1)} %collective-permute-done.8.before_ref, bf16[272,1024]{1,0:T(8,128)(2,1)S(1)} %collective-permute-done.11.far_ref, f32[264,1024]{1,0:T(8,128)S(1)} %copy-done.29, ...), custom_call_target="tpu_custom_call" | custom-call | flops 700000000 | bytes 1 | tf_op jit(solution)/shard_map/last/pallas_call | solution.py:425
  127.8 3.5 %back_rest.3.refs_12_ = bf16[272,1024]{1,0:T(8,128)(2,1)} custom-call(s32[2]{0:T(128)S(1)} %copy-done.37, bf16[1024,512]{1,0:T(8,128)(2,1)S(1)} %get-tuple-element.40.refs_0_.map_ref.out_ref, bf16[1024,512]{1,0:T(8,128)(2,1)S(1)} %get-tuple-element.38.dev_ref.edev_ref.table_ref, bf16[1024,1024]{1,0:T(8,128)(2,1)} %copy-done.4, ...), custom_call_target="tpu_custom_call" | custom-call | flops 1000000000 | bytes 1 | tf_op jit(solution)/shard_map/back_rest/pallas_call | solution.py:565
  133.1 1.2 copy-done.7
  135.3 3.4 %back_whole.6.refs_6_ = bf16[256,2048]{1,0:T(8,128)(2,1)S(1)} custom-call(s32[2]{0:T(128)S(1)} %copy-done.37, bf16[1024,512]{1,0:T(8,128)(2,1)S(1)} %copy-done.7, bf16[1024,512]{1,0:T(8,128)(2,1)S(1)} %copy-done.3, bf16[1024,1024]{1,0:T(8,128)(2,1)} %copy-done.5, bf16[256,512]{1,0:T(8,128)(2,1)S(1)} %copy-done.14, bf16[256,512]{1,0:T(8,128)(2,1)S(1)} %copy-done.16, ...), custom_call_target="tpu_custom_call" | custom-call | flops 1000000000 | bytes 1 | tf_op jit(solution)/shard_map/back_whole/pallas_call | solution.py:565
  139.5 2.2 %collective-permute-done.15.refs_2_ = bf16[256,1024]{1,0:T(8,128)(2,1)S(1)} collective-permute-done((bf16[256,1024]{1,0:T(8,128)(2,1)}, bf16[256,1024]{1,0:T(8,128)(2,1)S(1)}, u32[]{:S(2)}, u32[]{:S(2)}) %collective-permute-start.15) | collective-permute-done | bytes 524320 | tf_op jit(solution)/shard_map/ppermute | solution.py:608
  141.7 3.5 %back_whole.7.refs_6_ = bf16[256,2048]{1,0:T(8,128)(2,1)S(1)} custom-call(s32[2]{0:T(128)S(1)} %copy-done.37, bf16[1024,512]{1,0:T(8,128)(2,1)S(1)} %copy-done.11, bf16[1024,512]{1,0:T(8,128)(2,1)S(1)} %copy-done.3, bf16[1024,2048]{1,0:T(8,128)(2,1)} %spans.5.refs_7_.refs_0_, bf16[256,1024]{1,0:T(8,128)(2,1)S(1)} %get-tuple-element.68.refs_7_.refs_1_, ...), custom_call_target="tpu_custom_call" | custom-call | flops 1000000000 | bytes 1 | tf_op jit(solution)/shard_map/back_whole/pallas_call | solution.py:565
  146.2 3.5 %back_whole.8.refs_6_ = bf16[256,2048]{1,0:T(8,128)(2,1)S(1)} custom-call(s32[2]{0:T(128)S(1)} %copy-done.37, bf16[1024,512]{1,0:T(8,128)(2,1)S(1)} %copy-done.11, bf16[1024,512]{1,0:T(8,128)(2,1)S(1)} %copy-done.3, bf16[1024,2048]{1,0:T(8,128)(2,1)} %spans.5.refs_7_.refs_0_, bf16[256,1024]{1,0:T(8,128)(2,1)S(1)} %get-tuple-element.68.refs_7_.refs_1_, ...), custom_call_target="tpu_custom_call" | custom-call | flops 1000000000 | bytes 1 | tf_op jit(solution)/shard_map/back_whole/pallas_call | solution.py:565
  149.9 1.3 collective-permute-done.17.refs_7_
  151.2 3.5 %back_whole.9.refs_12_.refs_7_ = bf16[256,2048]{1,0:T(8,128)(2,1)S(1)} custom-call(s32[2]{0:T(128)S(1)} %copy-done.37, bf16[1024,512]{1,0:T(8,128)(2,1)S(1)} %copy-done.11, bf16[1024,512]{1,0:T(8,128)(2,1)S(1)} %copy-done.3, bf16[1024,2048]{1,0:T(8,128)(2,1)} %spans.5.refs_7_.refs_0_, bf16[256,1024]{1,0:T(8,128)(2,1)S(1)} %get-tuple-element.68.refs_7_.refs_1_, ...), custom_call_target="tpu_custom_call" | custom-call | flops 1000000000 | bytes 1 | tf_op jit(solution)/shard_map/back_whole/pallas_call | solution.py:565
  154.7 1.5 collective-permute-start.21
  156.2 4.2 %back_whole.10 = bf16[256,16384]{1,0:T(8,128)(2,1)} custom-call(s32[2]{0:T(128)S(1)} %copy-done.37, bf16[1024,512]{1,0:T(8,128)(2,1)S(1)} %copy-done.8, bf16[1024,512]{1,0:T(8,128)(2,1)S(1)} %copy-done.3, bf16[1024,1024]{1,0:T(8,128)(2,1)} %copy-done.5, bf16[256,512]{1,0:T(8,128)(2,1)S(1)} %copy-done.14, bf16[256,512]{1,0:T(8,128)(2,1)S(1)} %copy-done.16, ...), custom_call_target="tpu_custom_call" | custom-call | flops 1000000000 | bytes 1 | tf_op jit(solution)/shard_map/back_whole/pallas_call | solution.py:565
  160.4 2.0 %fusion = bf16[256,16384]{1,0:T(8,128)(2,1)} fusion(bf16[256,16384]{1,0:T(8,128)(2,1)} %back_whole.10, s32[]{:T(128)S(6)} %select_n.32, bf16[256,1024]{1,0:T(8,128)(2,1)} %collective-permute-done.13.refs_8_, f32[256]{0:T(256)S(1)} %bitcast.19), kind=kLoop, calls=%fused_computation.2 | loop fusion | flops 786432 | bytes 1049604 | tf_op jit(solution)/shard_map/dynamic_update_slice | solution.py:761
  162.4 1.9 slice_dynamic-update-slice_fusion.1
  165.0 2.0 %fusion.1 = bf16[256,16384]{1,0:T(8,128)(2,1)} fusion(bf16[256,16384]{1,0:T(8,128)(2,1)} %slice_dynamic-update-slice_fusion.1, s32[]{:T(128)S(6)} %select_n.34, bf16[256,1024]{1,0:T(8,128)(2,1)} %collective-permute-done.14.refs_9_, f32[256]{0:T(256)S(1)} %bitcast.20), kind=kLoop, calls=%fused_computation.3 | loop fusion | flops 786432 | bytes 1049604 | tf_op jit(solution)/shard_map/dynamic_update_slice | solution.py:761
  167.0 1.9 slice_dynamic-update-slice_fusion
  169.9 4.3 %back_whole.11 = bf16[256,16384]{1,0:T(8,128)(2,1)} custom-call(s32[2]{0:T(128)S(1)} %copy-done.37, bf16[1024,512]{1,0:T(8,128)(2,1)S(1)} %copy-done.11, bf16[1024,512]{1,0:T(8,128)(2,1)S(1)} %copy-done.3, bf16[1024,2048]{1,0:T(8,128)(2,1)} %spans.5.refs_7_.refs_0_, ...), custom_call_target="tpu_custom_call", output_to_operand_aliasing={{}: (9, {})} | custom-call | flops 1000000000 | bytes 1 | tf_op jit(solution)/shard_map/back_whole/pallas_call | solution.py:565
  176.4 19.4 %collective-permute-done.21 = bf16[256,2048]{1,0:T(8,128)(2,1)S(1)} collective-permute-done((bf16[256,2048]{1,0:T(8,128)(2,1)S(1)}, bf16[256,2048]{1,0:T(8,128)(2,1)S(1)}, u32[]{:S(2)}, u32[]{:S(2)}) %collective-permute-start.21) | collective-permute-done | bytes 1048608 | tf_op jit(solution)/shard_map/ppermute | solution.py:716
  (130 shorter events, 20.6 us)
Async XLA Ops:
  0.7 13.1 %collective-permute-start = (bf16[3,2,512]{2,1,0:T(2,128)(2,1)S(1)}, bf16[3,2,512]{2,1,0:T(2,128)(2,1)S(1)}, u32[]{:S(2)}, u32[]{:S(2)}) collective-permute-start(bf16[3,2,512]{2,1,0:T(2,128)(2,1)S(1)} %slice.24), channel_id=1, source_target_pairs={{0,4},{4,8},{8,12},{12,16},{16,20},{20,24},{24,28},{1,5},{5,9},{9,... | collective-permute-start | bytes 18440 | tf_op jit(solution)/shard_map/ppermute | solution.py:675
  6.4 10.4 %collective-permute-start.1 = (bf16[3,4096]{1,0:T(4,128)(2,1)S(1)}, bf16[3,4096]{1,0:T(4,128)(2,1)S(1)}, u32[]{:S(2)}, u32[]{:S(2)}) collective-permute-start(bf16[3,4096]{1,0:T(4,128)(2,1)S(1)} %slice.25), channel_id=1, source_target_pairs={{0,4},{4,8},{8,12},{12,16},{16,20},{20,24},{24,28},{1,5},{5,9},{9,... | collective-permute-start | bytes 73736 | tf_op jit(solution)/shard_map/ppermute | solution.py:674
  13.7 114.1 %copy-start.2 = (bf16[1024,512]{1,0:T(8,128)(2,1)}, bf16[1024,512]{1,0:T(8,128)(2,1)S(1)}, u32[]{:S(2)}) copy-start(bf16[1024,512]{1,0:T(8,128)(2,1)S(1)} %get-tuple-element.38.dev_ref.edev_ref.table_ref) | copy-start | bytes 3145732
  13.8 86.1 %copy-start.36 = (s32[2]{0:T(128)}, s32[2]{0:T(128)S(1)}, u32[]{:S(2)}) copy-start(s32[2]{0:T(128)S(1)} %pad_add_fusion.where_ref) | copy-start | bytes 28
  16.8 111.0 %copy-start.6 = (bf16[1024,512]{1,0:T(8,128)(2,1)}, bf16[1024,512]{1,0:T(8,128)(2,1)S(1)}, u32[]{:S(2)}) copy-start(bf16[1024,512]{1,0:T(8,128)(2,1)S(1)} %get-tuple-element.40.refs_0_.map_ref.out_ref) | copy-start | bytes 3145732
  23.8 8.9 %copy-start.24 = (f32[264,512]{1,0:T(8,128)}, f32[264,512]{1,0:T(8,128)S(1)}, u32[]{:S(2)}) copy-start(f32[264,512]{1,0:T(8,128)S(1)} %get-tuple-element.41.kept_ref) | copy-start | bytes 1622020
  23.8 8.2 %collective-permute-start.2 = (bf16[272,512]{1,0:T(8,128)(2,1)S(1)}, bf16[272,512]{1,0:T(8,128)(2,1)S(1)}, u32[]{:S(2)}, u32[]{:S(2)}) collective-permute-start(bf16[272,512]{1,0:T(8,128)(2,1)S(1)} %get-tuple-element.42), channel_id=1, source_target_pairs={{0,4},{4,0},{8,12},{12,8},{16,20},{20,16},{24,28},{28,24},{1,5},{5... | collective-permute-start | bytes 835592 | tf_op jit(solution)/shard_map/ppermute | solution.py:608
  31.5 18.9 %copy-start.12 = (bf16[1024,1024]{1,0:T(8,128)(2,1)}, bf16[1024,1024]{1,0:T(8,128)(2,1)S(1)}, u32[]{:S(2)}) copy-start(bf16[1024,1024]{1,0:T(8,128)(2,1)S(1)} %get-tuple-element.44.refs_0_.xh_ref) | copy-start | bytes 6291460
  31.5 18.9 %copy-start.30 = (f32[264,512]{1,0:T(8,128)}, f32[264,512]{1,0:T(8,128)S(1)}, u32[]{:S(2)}) copy-start(f32[264,512]{1,0:T(8,128)S(1)} %get-tuple-element.48.kept_ref) | copy-start | bytes 1622020
  31.5 17.5 %collective-permute-start.3 = (bf16[272,512]{1,0:T(8,128)(2,1)S(1)}, bf16[272,512]{1,0:T(8,128)(2,1)S(1)}, u32[]{:S(2)}, u32[]{:S(2)}) collective-permute-start(bf16[272,512]{1,0:T(8,128)(2,1)S(1)} %get-tuple-element.49), channel_id=1, source_target_pairs={{0,4},{4,0},{8,12},{12,8},{16,20},{20,16},{24,28},{28,24},{1,5},{5... | collective-permute-start | bytes 835592 | tf_op jit(solution)/shard_map/ppermute | solution.py:608
  32.0 18.4 %copy-start.26 = (bf16[272,512]{1,0:T(8,128)(2,1)}, bf16[272,512]{1,0:T(8,128)(2,1)S(1)}, u32[]{:S(2)}) copy-start(bf16[272,512]{1,0:T(8,128)(2,1)S(1)} %collective-permute-done.2.got_ref) | copy-start | bytes 835588
  32.8 8.3 %collective-permute-start.4 = (bf16[272,512]{1,0:T(8,128)(2,1)S(1)}, bf16[272,512]{1,0:T(8,128)(2,1)S(1)}, u32[]{:S(2)}, u32[]{:S(2)}) collective-permute-start(bf16[272,512]{1,0:T(8,128)(2,1)S(1)} %get-tuple-element.50), channel_id=1, source_target_pairs={{0,8},{4,12},{8,16},{12,20},{16,24},{20,28},{1,9},{5,13},{9,17},{1... | collective-permute-start | bytes 835592 | tf_op jit(solution)/shard_map/ppermute | solution.py:600
  41.1 12.3 %copy-start.34 = (bf16[272,512]{1,0:T(8,128)(2,1)}, bf16[272,512]{1,0:T(8,128)(2,1)S(1)}, u32[]{:S(2)}) copy-start(bf16[272,512]{1,0:T(8,128)(2,1)S(1)} %collective-permute-done.4.before_ref) | copy-start | bytes 835588
  42.9 30.6 %collective-permute-start.7 = (bf16[272,512]{1,0:T(8,128)(2,1)}, bf16[272,512]{1,0:T(8,128)(2,1)}, u32[]{:S(2)}, u32[]{:S(2)}) collective-permute-start(bf16[272,512]{1,0:T(8,128)(2,1)} %inclusive.3.refs_0_), channel_id=1, source_target_pairs={{0,16},{4,20},{8,24},{12,28},{1,17},{5,21},{9,25},{13,29},{2,18},{... | collective-permute-start | bytes 835592 | tf_op jit(solution)/shard_map/ppermute | solution.py:600
  49.0 17.2 %copy-start.38 = (bf16[2,128]{1,0:T(2,128)(2,1)S(1)}, bf16[2,128]{1,0:T(2,128)(2,1)}, u32[]{:S(2)}) copy-start(bf16[2,128]{1,0:T(2,128)(2,1)} %constant.48.clone.halves_ref) | copy-start | bytes 1540
  50.4 25.1 %collective-permute-start.6 = (bf16[272,512]{1,0:T(8,128)(2,1)}, bf16[272,512]{1,0:T(8,128)(2,1)}, u32[]{:S(2)}, u32[]{:S(2)}) collective-permute-start(bf16[272,512]{1,0:T(8,128)(2,1)} %get-tuple-element.58), channel_id=1, source_target_pairs={{0,8},{4,12},{8,16},{12,20},{16,24},{20,28},{1,9},{5,13},{9,17},{1... | collective-permute-start | bytes 835592 | tf_op jit(solution)/shard_map/ppermute | solution.py:600
  64.7 14.6 %copy-start.28 = (f32[264,1024]{1,0:T(8,128)}, f32[264,1024]{1,0:T(8,128)S(1)}, u32[]{:S(2)}) copy-start(f32[264,1024]{1,0:T(8,128)S(1)} %get-tuple-element.56.kept_ref) | copy-start | bytes 3244036
  64.7 14.6 %collective-permute-start.5 = (bf16[272,1024]{1,0:T(8,128)(2,1)}, bf16[272,1024]{1,0:T(8,128)(2,1)}, u32[]{:S(2)}, u32[]{:S(2)}) collective-permute-start(bf16[272,1024]{1,0:T(8,128)(2,1)} %get-tuple-element.57), channel_id=1, source_target_pairs={{0,4},{4,0},{8,12},{12,8},{16,20},{20,16},{24,28},{28,24},{1,5},{5... | collective-permute-start | bytes 1671176 | tf_op jit(solution)/shard_map/ppermute | solution.py:608
  66.1 7.3 %copy-start.25 = (f32[264,512]{1,0:T(8,128)S(1)}, f32[264,512]{1,0:T(8,128)}, u32[]{:S(2)}) copy-start(f32[264,512]{1,0:T(8,128)} %copy-done.24) | copy-start | bytes 1622020
  66.1 7.3 %copy-start.27 = (bf16[272,512]{1,0:T(8,128)(2,1)S(1)}, bf16[272,512]{1,0:T(8,128)(2,1)}, u32[]{:S(2)}) copy-start(bf16[272,512]{1,0:T(8,128)(2,1)} %copy-done.26) | copy-start | bytes 835588
  66.2 7.4 %copy-start.35 = (bf16[272,512]{1,0:T(8,128)(2,1)S(1)}, bf16[272,512]{1,0:T(8,128)(2,1)}, u32[]{:S(2)}) copy-start(bf16[272,512]{1,0:T(8,128)(2,1)} %copy-done.34) | copy-start | bytes 835588
  73.5 10.3 %copy-start.5 = (bf16[1024,1024]{1,0:T(8,128)(2,1)}, bf16[1024,1024]{1,0:T(8,128)(2,1)S(1)}, u32[]{:S(2)}) copy-start(bf16[1024,1024]{1,0:T(8,128)(2,1)S(1)} %spans.3.refs_0_) | copy-start | bytes 6291460
  73.5 10.3 %copy-start.22 = (f32[4096]{0:T(1024)S(1)}, f32[4096]{0:T(1024)}, u32[]{:S(2)}) copy-start(f32[4096]{0:T(1024)} %param.19) | copy-start | bytes 49156
  74.9 12.0 %copy-start.13 = (bf16[256,512]{1,0:T(8,128)(2,1)}, bf16[256,512]{1,0:T(8,128)(2,1)S(1)}, u32[]{:S(2)}) copy-start(bf16[256,512]{1,0:T(8,128)(2,1)S(1)} %get-tuple-element.59.refs_0_.refs_1_) | copy-start | bytes 786436
  74.9 8.8 %collective-permute-start.10 = (bf16[256,512]{1,0:T(8,128)(2,1)S(1)}, bf16[256,512]{1,0:T(8,128)(2,1)S(1)}, u32[]{:S(2)}, u32[]{:S(2)}) collective-permute-start(bf16[256,512]{1,0:T(8,128)(2,1)S(1)} %get-tuple-element.62), channel_id=1, source_target_pairs={{0,4},{4,0},{8,12},{12,8},{16,20},{20,16},{24,28},{28,24},{1,5},{5... | collective-permute-start | bytes 786440 | tf_op jit(solution)/shard_map/ppermute | solution.py:608
  77.3 22.6 %collective-permute-start.9 = (bf16[272,512]{1,0:T(8,128)(2,1)}, bf16[272,512]{1,0:T(8,128)(2,1)}, u32[]{:S(2)}, u32[]{:S(2)}) collective-permute-start(bf16[272,512]{1,0:T(8,128)(2,1)} %inclusive.4.refs_0_), channel_id=1, source_target_pairs={{0,16},{4,20},{8,24},{12,28},{1,17},{5,21},{9,25},{13,29},{2,18},{... | collective-permute-start | bytes 835592 | tf_op jit(solution)/shard_map/ppermute | solution.py:600
  81.5 20.1 %collective-permute-start.8 = (bf16[272,1024]{1,0:T(8,128)(2,1)}, bf16[272,1024]{1,0:T(8,128)(2,1)}, u32[]{:S(2)}, u32[]{:S(2)}) collective-permute-start(bf16[272,1024]{1,0:T(8,128)(2,1)} %get-tuple-element.61), channel_id=1, source_target_pairs={{0,8},{4,12},{8,16},{12,20},{16,24},{20,28},{1,9},{5,13},{9,17},{1... | collective-permute-start | bytes 1671176 | tf_op jit(solution)/shard_map/ppermute | solution.py:600
  83.7 6.3 %copy-start.15 = (bf16[256,512]{1,0:T(8,128)(2,1)}, bf16[256,512]{1,0:T(8,128)(2,1)S(1)}, u32[]{:S(2)}) copy-start(bf16[256,512]{1,0:T(8,128)(2,1)S(1)} %collective-permute-done.10.refs_2_) | copy-start | bytes 786436
  86.9 33.3 %collective-permute-start.13 = (bf16[256,1024]{1,0:T(8,128)(2,1)}, bf16[256,1024]{1,0:T(8,128)(2,1)}, u32[]{:S(2)}, u32[]{:S(2)}) collective-permute-start(bf16[256,1024]{1,0:T(8,128)(2,1)} %get-tuple-element.63.refs_6_), channel_id=1, source_target_pairs={{0,3},{1,2},{2,1},{3,0},{4,7},{5,6},{6,5},{7,4},{8,11},{9,10},{10,... | collective-permute-start | bytes 1572872 | tf_op jit(solution)/shard_map/ppermute | solution.py:716
  90.1 30.1 %collective-permute-start.14 = (bf16[256,1024]{1,0:T(8,128)(2,1)}, bf16[256,1024]{1,0:T(8,128)(2,1)}, u32[]{:S(2)}, u32[]{:S(2)}) collective-permute-start(bf16[256,1024]{1,0:T(8,128)(2,1)} %get-tuple-element.64.refs_0_), channel_id=1, source_target_pairs={{0,2},{1,3},{2,0},{3,1},{4,6},{5,7},{6,4},{7,5},{8,10},{9,11},{10,... | collective-permute-start | bytes 1572872 | tf_op jit(solution)/shard_map/ppermute | solution.py:716
  91.4 8.6 %copy-start.33 = (bf16[272,512]{1,0:T(8,128)(2,1)S(1)}, bf16[272,512]{1,0:T(8,128)(2,1)}, u32[]{:S(2)}) copy-start(bf16[272,512]{1,0:T(8,128)(2,1)} %copy-done.32) | copy-start | bytes 835588
  92.6 7.4 %copy-start.31 = (f32[264,512]{1,0:T(8,128)S(1)}, f32[264,512]{1,0:T(8,128)}, u32[]{:S(2)}) copy-start(f32[264,512]{1,0:T(8,128)} %copy-done.30) | copy-start | bytes 1622020
  92.6 14.2 %copy-start.10 = (bf16[1024,512]{1,0:T(8,128)(2,1)S(1)}, bf16[1024,512]{1,0:T(8,128)(2,1)}, u32[]{:S(2)}) copy-start(bf16[1024,512]{1,0:T(8,128)(2,1)} %copy-done.9) | copy-start | bytes 3145732
  99.9 20.3 %copy-start.4 = (bf16[1024,1024]{1,0:T(8,128)(2,1)}, bf16[1024,1024]{1,0:T(8,128)(2,1)S(1)}, u32[]{:S(2)}) copy-start(bf16[1024,1024]{1,0:T(8,128)(2,1)S(1)} %spans.4.refs_0_.refs_6_) | copy-start | bytes 6291460
  101.7 18.6 %copy-start.37 = (s32[2]{0:T(128)S(1)}, s32[2]{0:T(128)}, u32[]{:S(2)}) copy-start(s32[2]{0:T(128)} %copy-done.36) | copy-start | bytes 28
  102.9 22.0 %collective-permute-start.11 = (bf16[272,1024]{1,0:T(8,128)(2,1)S(1)}, bf16[272,1024]{1,0:T(8,128)(2,1)S(1)}, u32[]{:S(2)}, u32[]{:S(2)}) collective-permute-start(bf16[272,1024]{1,0:T(8,128)(2,1)S(1)} %inclusive.5.refs_0_), channel_id=1, source_target_pairs={{0,16},{4,20},{8,24},{12,28},{1,17},{5,21},{9,25},{13,29},{2,18},{... | collective-permute-start | bytes 1671176 | tf_op jit(solution)/shard_map/ppermute | solution.py:600
  105.1 15.1 %collective-permute-start.12 = (bf16[256,512]{1,0:T(8,128)(2,1)S(1)}, bf16[256,512]{1,0:T(8,128)(2,1)S(1)}, u32[]{:S(2)}, u32[]{:S(2)}) collective-permute-start(bf16[256,512]{1,0:T(8,128)(2,1)S(1)} %get-tuple-element.66), channel_id=1, source_target_pairs={{0,4},{4,0},{8,12},{12,8},{16,20},{20,16},{24,28},{28,24},{1,5},{5... | collective-permute-start | bytes 786440 | tf_op jit(solution)/shard_map/ppermute | solution.py:608
  120.2 7.6 %copy-start.17 = (bf16[256,512]{1,0:T(8,128)(2,1)}, bf16[256,512]{1,0:T(8,128)(2,1)S(1)}, u32[]{:S(2)}) copy-start(bf16[256,512]{1,0:T(8,128)(2,1)S(1)} %collective-permute-done.12.refs_2_.refs_8_) | copy-start | bytes 786436
  120.2 4.7 %copy-start.29 = (f32[264,1024]{1,0:T(8,128)S(1)}, f32[264,1024]{1,0:T(8,128)}, u32[]{:S(2)}) copy-start(f32[264,1024]{1,0:T(8,128)} %copy-done.28) | copy-start | bytes 3244036
  123.8 15.0 %collective-permute-start.16 = (bf16[272,1024]{1,0:T(8,128)(2,1)}, bf16[272,1024]{1,0:T(8,128)(2,1)}, u32[]{:S(2)}, u32[]{:S(2)}) collective-permute-start(bf16[272,1024]{1,0:T(8,128)(2,1)} %back_rest.2.refs_0_), channel_id=1, source_target_pairs={{0,3},{1,2},{2,1},{3,0},{4,7},{5,6},{6,5},{7,4},{8,11},{9,10},{10,... | collective-permute-start | bytes 1671176 | tf_op jit(solution)/shard_map/ppermute | solution.py:716
  127.4 14.3 %collective-permute-start.15 = (bf16[256,1024]{1,0:T(8,128)(2,1)}, bf16[256,1024]{1,0:T(8,128)(2,1)S(1)}, u32[]{:S(2)}, u32[]{:S(2)}) collective-permute-start(bf16[256,1024]{1,0:T(8,128)(2,1)} %get-tuple-element.69), channel_id=1, source_target_pairs={{0,4},{4,0},{8,12},{12,8},{16,20},{20,16},{24,28},{28,24},{1,5},{5... | collective-permute-start | bytes 1572872 | tf_op jit(solution)/shard_map/ppermute | solution.py:608
  131.3 19.9 %collective-permute-start.17 = (bf16[272,1024]{1,0:T(8,128)(2,1)}, bf16[272,1024]{1,0:T(8,128)(2,1)}, u32[]{:S(2)}, u32[]{:S(2)}) collective-permute-start(bf16[272,1024]{1,0:T(8,128)(2,1)} %back_rest.3.refs_12_), channel_id=1, source_target_pairs={{0,2},{1,3},{2,0},{3,1},{4,6},{5,7},{6,4},{7,5},{8,10},{9,11},{10,... | collective-permute-start | bytes 1671176 | tf_op jit(solution)/shard_map/ppermute | solution.py:716
  135.3 6.4 %copy-start.11 = (bf16[1024,512]{1,0:T(8,128)(2,1)S(1)}, bf16[1024,512]{1,0:T(8,128)(2,1)}, u32[]{:S(2)}) copy-start(bf16[1024,512]{1,0:T(8,128)(2,1)} %copy-done.9) | copy-start | bytes 3145732
  138.7 30.1 %collective-permute-start.18 = (bf16[256,2048]{1,0:T(8,128)(2,1)S(1)}, bf16[256,2048]{1,0:T(8,128)(2,1)S(1)}, u32[]{:S(2)}, u32[]{:S(2)}) collective-permute-start(bf16[256,2048]{1,0:T(8,128)(2,1)S(1)} %back_whole.6.refs_6_), channel_id=1, source_target_pairs={{0,1},{1,0},{2,3},{3,2},{4,5},{5,4},{6,7},{7,6},{8,9},{9,8},{10,11... | collective-permute-start | bytes 3145736 | tf_op jit(solution)/shard_map/ppermute | solution.py:716
  145.2 29.0 %collective-permute-start.19 = (bf16[256,2048]{1,0:T(8,128)(2,1)S(1)}, bf16[256,2048]{1,0:T(8,128)(2,1)S(1)}, u32[]{:S(2)}, u32[]{:S(2)}) collective-permute-start(bf16[256,2048]{1,0:T(8,128)(2,1)S(1)} %back_whole.7.refs_6_), channel_id=1, source_target_pairs={{0,3},{1,2},{2,1},{3,0},{4,7},{5,6},{6,5},{7,4},{8,11},{9,10},{10,... | collective-permute-start | bytes 3145736 | tf_op jit(solution)/shard_map/ppermute | solution.py:716
  149.7 6.5 %copy-start.8 = (bf16[1024,512]{1,0:T(8,128)(2,1)S(1)}, bf16[1024,512]{1,0:T(8,128)(2,1)}, u32[]{:S(2)}) copy-start(bf16[1024,512]{1,0:T(8,128)(2,1)} %copy-done.6) | copy-start | bytes 3145732
  149.8 25.6 %collective-permute-start.20 = (bf16[256,2048]{1,0:T(8,128)(2,1)S(1)}, bf16[256,2048]{1,0:T(8,128)(2,1)S(1)}, u32[]{:S(2)}, u32[]{:S(2)}) collective-permute-start(bf16[256,2048]{1,0:T(8,128)(2,1)S(1)} %back_whole.8.refs_6_), channel_id=1, source_target_pairs={{0,1},{1,0},{2,3},{3,2},{4,5},{5,4},{6,7},{7,6},{8,9},{9,8},{10,11... | collective-permute-start | bytes 3145736 | tf_op jit(solution)/shard_map/ppermute | solution.py:716
  154.7 41.1 %collective-permute-start.21 = (bf16[256,2048]{1,0:T(8,128)(2,1)S(1)}, bf16[256,2048]{1,0:T(8,128)(2,1)S(1)}, u32[]{:S(2)}, u32[]{:S(2)}) collective-permute-start(bf16[256,2048]{1,0:T(8,128)(2,1)S(1)} %back_whole.9.refs_12_.refs_7_), channel_id=1, source_target_pairs={{0,2},{1,3},{2,0},{3,1},{4,6},{5,7},{6,4},{7,5},{8,10},{9,11},{10,... | collective-permute-start | bytes 3145736 | tf_op jit(solution)/shard_map/ppermute | solution.py:716
  (19 other events, 40.9 us)

commit v4 on v3

--- a/solution.py
+++ b/solution.py
@@ -648,7 +648,9 @@
         self.mine, sent = self.line.run(
             join, last_kernel, "last", self.where, [self.before, self.far, self.kept, self.got], ["state", "state"]
         )
-        self.other = swapped(sent, self.pairs)
+        self.other = lax.ppermute(
+            sent, "ctx", [(2 * q + y, 2 * q + 1 - y) for q in range(self.pairs) for y in range(2) if q or not y]
+        )
 
 
 def shards(

time: 198 us -> 202 us (1.020)
  starting transfers between devices: 38.6 us -> 43.9 us
    ppermute x0 -> x3, starting transfers between devices: none -> 7.8 us  [finish(): lax.ppermute(sent, 'ctx', [(2 * q + y, 2 * q + 1 - y) for q in range(self...]
    ppermute x6 -> x3, starting transfers between devices: 6.34 us -> 3.58 us  [swapped(): lax.ppermute(value, 'ctx', [(2 * q + y, 2 * q + 1 - y) for q in range(pai...]
    ppermute x6 -> x3, waiting for transfers between devices: 2.18 us -> 0.01 us  [swapped(): lax.ppermute(value, 'ctx', [(2 * q + y, 2 * q + 1 - y) for q in range(pai...]
  transfers between devices with their start and end apart: 22 -> 22, of which waited for: 4 -> 4; matrix products, arithmetic and copies ran while one was open for 7% -> 7% of each run, Pallas kernels for 52% -> 51%
where the time goes in v4:
time: 202 us; the launch traced here: 200 us
  Pallas kernels  109 us (54%)
  starting transfers between devices  43.9 us (22%)
  waiting for transfers between devices  23.7 us (12%)
  local copies, waits for them, and re-layouts  18.2 us (9%)
  other arithmetic  5.43 us (3%)
    pallas_call x10, Pallas kernels, back(): pl.pallas_call(functools.partial(back_kernel, mode, [len(ys) for _, ys, _...  35.9 us
    pallas_call x3, Pallas kernels, spans_of(): pl.pallas_call(functools.partial(span_kernel, index * some, len(after)),...  28 us
    pallas_call x3, Pallas kernels, front(): pl.pallas_call(functools.partial(front_kernel, len(after), blocks), grid_...  24.3 us
    ppermute x8, waiting for transfers between devices, ship(): return lax.ppermute(piece, 'head', [(i, i ^ r) for i in range(head_size)])  21.6 us
    ppermute x6, starting transfers between devices, shifted(): lax.ppermute(value, 'ctx', [(2 * q + y, 2 * (q + steps) + y) for q in ran...  18.7 us
    pallas_call x9, Pallas kernels, join(): pl.pallas_call(kernel, in_specs=[pl.BlockSpec(memory_space=pltpu.SMEM)] *...  13.6 us
    unnamed x90, local copies, waits for them, and re-layouts  8.52 us
    ppermute x3, starting transfers between devices, finish(): lax.ppermute(sent, 'ctx', [(2 * q + y, 2 * q + 1 - y) for q in range(self...  7.8 us
  transfers between devices with their start and end apart: 22, of which 4 were waited for; matrix products, arithmetic and copies ran while one was open for 7% of the time, Pallas kernels for 51%

profile of v4, /device:TPU:0, one launch (start us, length us, event | category | flops | bytes accessed | tf_op | source)
XLA Modules:
  0.0 200.4 jit_solution(12520743524727080945)
XLA Ops:
  0.7 4.9 %collective-permute-start = (bf16[3,2,512]{2,1,0:T(2,128)(2,1)S(1)}, bf16[3,2,512]{2,1,0:T(2,128)(2,1)S(1)}, u32[]{:S(2)}, u32[]{:S(2)}) collective-permute-start(bf16[3,2,512]{2,1,0:T(2,128)(2,1)S(1)} %slice.24), channel_id=1, source_target_pairs={{0,4},{4,8},{8,12},{12,16},{16,20},{20,24},{24,28},{1,5},{5,9},{9,... | collective-permute-start | bytes 18440 | tf_op jit(solution)/shard_map/ppermute | solution.py:677
  6.4 3.4 %collective-permute-start.1 = (bf16[3,4096]{1,0:T(4,128)(2,1)S(1)}, bf16[3,4096]{1,0:T(4,128)(2,1)S(1)}, u32[]{:S(2)}, u32[]{:S(2)}) collective-permute-start(bf16[3,4096]{1,0:T(4,128)(2,1)S(1)} %slice.25), channel_id=1, source_target_pairs={{0,4},{4,8},{8,12},{12,16},{16,20},{20,24},{24,28},{1,5},{5,9},{9,... | collective-permute-start | bytes 73736 | tf_op jit(solution)/shard_map/ppermute | solution.py:676
  12.4 1.2 decays.1
  14.0 2.8 %maps.2 = (bf16[1024,512]{1,0:T(8,128)(2,1)S(1)}, bf16[256,1024]{1,0:T(8,128)(2,1)S(1)}) custom-call(bf16[1024,2,512]{2,1,0:T(2,128)(2,1)S(1)} %copy-done.39, bf16[16,2,512]{2,1,0:T(2,128)(2,1)S(1)} %pad.8.halo_ref, bf16[4,2,512]{2,1,0:T(2,128)(2,1)S(1)} %copy-done.43), custom_call_target="tpu_custom_call" | custom-call | flops 3000000000 | bytes 1 | tf_op jit(solution)/shard_map/maps/pallas_call | solution.py:182
  16.9 6.9 %front.3 = (bf16[1024,1024]{1,0:T(8,128)(2,1)}, bf16[272,512]{1,0:T(8,128)(2,1)S(1)}, f32[264,512]{1,0:T(8,128)S(1)}) custom-call(s32[2]{0:T(128)S(1)} %pad_add_fusion.where_ref, bf16[1024,4096]{1,0:T(8,128)(2,1)} %feat_ref.5, bf16[16,4096]{1,0:T(8,128)(2,1)S(1)} %pad.9.halo_ref, bf16[4,4096]{1,0:T(4,128)(2,1)S(1)} %copy-done.42, ...), custom_call_target="tpu_custom_call" | custom-call | flops 4000000000 | bytes 1 | tf_op jit(solution)/shard_map/front/pallas_call | solution.py:252
  23.8 1.6 collective-permute-start.2
  25.4 6.1 %front.4 = (bf16[1024,1024]{1,0:T(8,128)(2,1)S(1)}, bf16[272,512]{1,0:T(8,128)(2,1)S(1)}, f32[264,512]{1,0:T(8,128)S(1)}) custom-call(s32[2]{0:T(128)S(1)} %pad_add_fusion.where_ref, bf16[1024,4096]{1,0:T(8,128)(2,1)} %feat_ref.5, bf16[16,4096]{1,0:T(8,128)(2,1)S(1)} %pad.9.halo_ref, bf16[4,4096]{1,0:T(4,128)(2,1)S(1)} %copy-done.42, ...), custom_call_target="tpu_custom_call" | custom-call | flops 4000000000 | bytes 1 | tf_op jit(solution)/shard_map/front/pallas_call | solution.py:252
  32.8 3.7 %collective-permute-start.4 = (bf16[272,512]{1,0:T(8,128)(2,1)S(1)}, bf16[272,512]{1,0:T(8,128)(2,1)S(1)}, u32[]{:S(2)}, u32[]{:S(2)}) collective-permute-start(bf16[272,512]{1,0:T(8,128)(2,1)S(1)} %get-tuple-element.50), channel_id=1, source_target_pairs={{0,8},{4,12},{8,16},{12,20},{16,24},{20,28},{1,9},{5,13},{9,17},{1... | collective-permute-start | bytes 835592 | tf_op jit(solution)/shard_map/ppermute | solution.py:600
  36.4 2.8 %maps.3 = (bf16[1024,512]{1,0:T(8,128)(2,1)S(1)}, bf16[256,1024]{1,0:T(8,128)(2,1)S(1)}) custom-call(bf16[1024,2,512]{2,1,0:T(2,128)(2,1)S(1)} %copy-done.39, bf16[16,2,512]{2,1,0:T(2,128)(2,1)S(1)} %pad.8.halo_ref, bf16[4,2,512]{2,1,0:T(2,128)(2,1)S(1)} %copy-done.43, f32[264,512]{1,0:T(8,128)S(1)} %get-tuple-element.45.refs_0_.total_ref), custom_call_target="tpu_custom_call" | custom-call | flops 3000000000 | bytes 1 | tf_op jit(solution)/shard_map/maps/pallas_call | solution.py:182
  39.2 1.8 collective-permute-done.4.before_ref
  42.9 6.1 %collective-permute-start.7 = (bf16[272,512]{1,0:T(8,128)(2,1)}, bf16[272,512]{1,0:T(8,128)(2,1)}, u32[]{:S(2)}, u32[]{:S(2)}) collective-permute-start(bf16[272,512]{1,0:T(8,128)(2,1)} %inclusive.3.refs_0_), channel_id=1, source_target_pairs={{0,16},{4,20},{8,24},{12,28},{1,17},{5,21},{9,25},{13,29},{2,18},{... | collective-permute-start | bytes 835592 | tf_op jit(solution)/shard_map/ppermute | solution.py:600
  49.0 1.4 pair.4
  50.4 3.0 %collective-permute-start.6 = (bf16[272,512]{1,0:T(8,128)(2,1)}, bf16[272,512]{1,0:T(8,128)(2,1)}, u32[]{:S(2)}, u32[]{:S(2)}) collective-permute-start(bf16[272,512]{1,0:T(8,128)(2,1)} %get-tuple-element.58), channel_id=1, source_target_pairs={{0,8},{4,12},{8,16},{12,20},{16,24},{20,28},{1,9},{5,13},{9,17},{1... | collective-permute-start | bytes 835592 | tf_op jit(solution)/shard_map/ppermute | solution.py:600
  53.4 11.3 %front.5 = (bf16[1024,2048]{1,0:T(8,128)(2,1)}, bf16[272,1024]{1,0:T(8,128)(2,1)}, f32[264,1024]{1,0:T(8,128)S(1)}) custom-call(s32[2]{0:T(128)S(1)} %pad_add_fusion.where_ref, bf16[1024,4096]{1,0:T(8,128)(2,1)} %feat_ref.5, bf16[16,4096]{1,0:T(8,128)(2,1)S(1)} %pad.9.halo_ref, bf16[4,4096]{1,0:T(4,128)(2,1)S(1)} %copy-done.42, ...), custom_call_target="tpu_custom_call" | custom-call | flops 4000000000 | bytes 1 | tf_op jit(solution)/shard_map/front/pallas_call | solution.py:252
  64.7 1.5 collective-permute-start.5
  66.2 7.3 %spans.3.refs_0_ = bf16[1024,1024]{1,0:T(8,128)(2,1)S(1)} custom-call(bf16[1024,1024]{1,0:T(8,128)(2,1)} %get-tuple-element.43.refs_0_.xh_ref, bf16[1024,512]{1,0:T(8,128)(2,1)S(1)} %get-tuple-element.40.refs_0_.map_ref.out_ref, f32[1024,128]{1,0:T(8,128)S(1)} %get-tuple-element.53.col_ref, f32[64,1024]{1,0:T(8,128)S(1)} %get-tuple-element.54.row_ref, ...), custom_call_target="tpu_custom_call" | custom-call | flops 199999995904 | bytes 1 | tf_op jit(solution)/shard_map/spans/pallas_call | solution.py:343
  73.5 1.4 last.3
  74.9 2.5 %collective-permute-start.10 = (bf16[256,512]{1,0:T(8,128)(2,1)S(1)}, bf16[256,512]{1,0:T(8,128)(2,1)S(1)}, u32[]{:S(2)}, u32[]{:S(2)}) collective-permute-start(bf16[256,512]{1,0:T(8,128)(2,1)S(1)} %get-tuple-element.62), channel_id=1, source_target_pairs={{0,4},{8,12},{12,8},{16,20},{20,16},{24,28},{28,24},{1,5},{9,13},{... | collective-permute-start | bytes 786440 | tf_op jit(solution)/shard_map/ppermute | solution.py:651
  77.4 1.8 inclusive.4.refs_0_
  79.2 2.0 collective-permute-start.9
  81.2 2.2 %pair.5 = (f32[264,1024]{1,0:T(8,128)S(1)}, bf16[272,1024]{1,0:T(8,128)(2,1)}) custom-call(s32[2]{0:T(128)S(1)} %pad_add_fusion.where_ref, f32[264,1024]{1,0:T(8,128)S(1)} %get-tuple-element.56.kept_ref, bf16[272,1024]{1,0:T(8,128)(2,1)} %collective-permute-done.5.got_ref, bf16[272,512]{1,0:T(8,128)(2,1)} %inclusive.4.refs_0_), custom_call_target="tpu_custom_call" | custom-call | flops 700000000 | bytes 1 | tf_op jit(solution)/shard_map/pair/pallas_call | solution.py:425
  83.4 2.1 %collective-permute-start.8 = (bf16[272,1024]{1,0:T(8,128)(2,1)}, bf16[272,1024]{1,0:T(8,128)(2,1)}, u32[]{:S(2)}, u32[]{:S(2)}) collective-permute-start(bf16[272,1024]{1,0:T(8,128)(2,1)} %get-tuple-element.61), channel_id=1, source_target_pairs={{0,8},{4,12},{8,16},{12,20},{16,24},{20,28},{1,9},{5,13},{9,17},{1... | collective-permute-start | bytes 1671176 | tf_op jit(solution)/shard_map/ppermute | solution.py:600
  85.5 3.2 %back_first.2 = (bf16[256,1024]{1,0:T(8,128)(2,1)}, f32[256,128]{1,0:T(8,128)S(1)}) custom-call(s32[2]{0:T(128)S(1)} %pad_add_fusion.where_ref, bf16[1024,512]{1,0:T(8,128)(2,1)S(1)} %get-tuple-element.40.refs_0_.map_ref.out_ref, bf16[1024,512]{1,0:T(8,128)(2,1)S(1)} %get-tuple-element.38.dev_ref.edev_ref.table_ref, bf16[1024,1024]{1,0:T(8,128)(2,1)} %copy-done.5, ...), custom_call_target="tpu_custom_call" | custom-call | flops 1000000000 | bytes 1 | tf_op jit(solution)/shard_map/back_first/pallas_call | solution.py:565
  88.6 3.2 %back_first.3 = (bf16[256,1024]{1,0:T(8,128)(2,1)}, f32[256,128]{1,0:T(8,128)S(1)}) custom-call(s32[2]{0:T(128)S(1)} %pad_add_fusion.where_ref, bf16[1024,512]{1,0:T(8,128)(2,1)S(1)} %get-tuple-element.40.refs_0_.map_ref.out_ref, bf16[1024,512]{1,0:T(8,128)(2,1)S(1)} %get-tuple-element.38.dev_ref.edev_ref.table_ref, bf16[1024,1024]{1,0:T(8,128)(2,1)} %copy-done.5, ...), custom_call_target="tpu_custom_call" | custom-call | flops 1000000000 | bytes 1 | tf_op jit(solution)/shard_map/back_first/pallas_call | solution.py:565
  91.8 1.4 collective-permute-start.14
  94.5 7.3 %spans.4.refs_0_.refs_6_ = bf16[1024,1024]{1,0:T(8,128)(2,1)S(1)} custom-call(bf16[1024,1024]{1,0:T(8,128)(2,1)} %copy-done.12, bf16[1024,512]{1,0:T(8,128)(2,1)S(1)} %get-tuple-element.40.refs_0_.map_ref.out_ref, f32[1024,128]{1,0:T(8,128)S(1)} %get-tuple-element.53.col_ref, f32[64,1024]{1,0:T(8,128)S(1)} %get-tuple-element.54.row_ref, ...), custom_call_target="tpu_custom_call" | custom-call | flops 1000000000 | bytes 1 | tf_op jit(solution)/shard_map/spans/pallas_call | solution.py:343
  101.8 1.7 last.4
  103.5 1.2 inclusive.5.refs_0_
  104.8 1.9 collective-permute-start.11
  106.7 3.6 %collective-permute-start.12 = (bf16[256,512]{1,0:T(8,128)(2,1)S(1)}, bf16[256,512]{1,0:T(8,128)(2,1)S(1)}, u32[]{:S(2)}, u32[]{:S(2)}) collective-permute-start(bf16[256,512]{1,0:T(8,128)(2,1)S(1)} %get-tuple-element.66), channel_id=1, source_target_pairs={{0,4},{8,12},{12,8},{16,20},{20,16},{24,28},{28,24},{1,5},{9,13},{... | collective-permute-start | bytes 786440 | tf_op jit(solution)/shard_map/ppermute | solution.py:651
  110.3 13.4 %spans.5.refs_7_.refs_0_ = bf16[1024,2048]{1,0:T(8,128)(2,1)} custom-call(bf16[1024,2048]{1,0:T(8,128)(2,1)} %get-tuple-element.52.refs_0_.xh_ref, bf16[1024,512]{1,0:T(8,128)(2,1)S(1)} %copy-done.10, f32[1024,128]{1,0:T(8,128)S(1)} %get-tuple-element.53.col_ref, f32[64,1024]{1,0:T(8,128)S(1)} %get-tuple-element.54.row_ref, ...), custom_call_target="tpu_custom_call" | custom-call | flops 1000000000 | bytes 1 | tf_op jit(solution)/shard_map/spans/pallas_call | solution.py:343
  123.8 3.5 %back_rest.2.refs_0_ = bf16[272,1024]{1,0:T(8,128)(2,1)} custom-call(s32[2]{0:T(128)S(1)} %copy-done.37, bf16[1024,512]{1,0:T(8,128)(2,1)S(1)} %get-tuple-element.40.refs_0_.map_ref.out_ref, bf16[1024,512]{1,0:T(8,128)(2,1)S(1)} %get-tuple-element.38.dev_ref.edev_ref.table_ref, bf16[1024,1024]{1,0:T(8,128)(2,1)} %copy-done.4, ...), custom_call_target="tpu_custom_call" | custom-call | flops 1000000000 | bytes 1 | tf_op jit(solution)/shard_map/back_rest/pallas_call | solution.py:565
  127.9 2.5 %last.5 = (bf16[256,1024]{1,0:T(8,128)(2,1)S(1)}, bf16[256,1024]{1,0:T(8,128)(2,1)}) custom-call(s32[2]{0:T(128)S(1)} %copy-done.37, bf16[272,1024]{1,0:T(8,128)(2,1)} %collective-permute-done.8.before_ref, bf16[272,1024]{1,0:T(8,128)(2,1)S(1)} %collective-permute-done.11.far_ref, f32[264,1024]{1,0:T(8,128)S(1)} %copy-done.29, ...), custom_call_target="tpu_custom_call" | custom-call | flops 700000000 | bytes 1 | tf_op jit(solution)/shard_map/last/pallas_call | solution.py:425
  130.3 1.7 collective-permute-start.15
  132.1 3.5 %back_rest.3.refs_12_ = bf16[272,1024]{1,0:T(8,128)(2,1)} custom-call(s32[2]{0:T(128)S(1)} %copy-done.37, bf16[1024,512]{1,0:T(8,128)(2,1)S(1)} %get-tuple-element.40.refs_0_.map_ref.out_ref, bf16[1024,512]{1,0:T(8,128)(2,1)S(1)} %get-tuple-element.38.dev_ref.edev_ref.table_ref, bf16[1024,1024]{1,0:T(8,128)(2,1)} %copy-done.4, ...), custom_call_target="tpu_custom_call" | custom-call | flops 1000000000 | bytes 1 | tf_op jit(solution)/shard_map/back_rest/pallas_call | solution.py:565
  137.6 1.2 copy-done.7
  139.7 3.4 %back_whole.6.refs_6_ = bf16[256,2048]{1,0:T(8,128)(2,1)S(1)} custom-call(s32[2]{0:T(128)S(1)} %copy-done.37, bf16[1024,512]{1,0:T(8,128)(2,1)S(1)} %copy-done.7, bf16[1024,512]{1,0:T(8,128)(2,1)S(1)} %copy-done.3, bf16[1024,1024]{1,0:T(8,128)(2,1)} %copy-done.5, bf16[256,512]{1,0:T(8,128)(2,1)S(1)} %copy-done.14, bf16[256,512]{1,0:T(8,128)(2,1)S(1)} %copy-done.16, ...), custom_call_target="tpu_custom_call" | custom-call | flops 1000000000 | bytes 1 | tf_op jit(solution)/shard_map/back_whole/pallas_call | solution.py:565
  144.5 3.5 %back_whole.7.refs_6_ = bf16[256,2048]{1,0:T(8,128)(2,1)S(1)} custom-call(s32[2]{0:T(128)S(1)} %copy-done.37, bf16[1024,512]{1,0:T(8,128)(2,1)S(1)} %copy-done.11, bf16[1024,512]{1,0:T(8,128)(2,1)S(1)} %copy-done.3, bf16[1024,2048]{1,0:T(8,128)(2,1)} %spans.5.refs_7_.refs_0_, bf16[256,1024]{1,0:T(8,128)(2,1)S(1)} %get-tuple-element.68.refs_7_.refs_1_, ...), custom_call_target="tpu_custom_call" | custom-call | flops 1000000000 | bytes 1 | tf_op jit(solution)/shard_map/back_whole/pallas_call | solution.py:565
  149.2 3.5 %back_whole.8.refs_6_ = bf16[256,2048]{1,0:T(8,128)(2,1)S(1)} custom-call(s32[2]{0:T(128)S(1)} %copy-done.37, bf16[1024,512]{1,0:T(8,128)(2,1)S(1)} %copy-done.11, bf16[1024,512]{1,0:T(8,128)(2,1)S(1)} %copy-done.3, bf16[1024,2048]{1,0:T(8,128)(2,1)} %spans.5.refs_7_.refs_0_, bf16[256,1024]{1,0:T(8,128)(2,1)S(1)} %get-tuple-element.68.refs_7_.refs_1_, ...), custom_call_target="tpu_custom_call" | custom-call | flops 1000000000 | bytes 1 | tf_op jit(solution)/shard_map/back_whole/pallas_call | solution.py:565
  153.2 1.4 collective-permute-done.17.refs_7_
  154.5 3.5 %back_whole.9.refs_12_.refs_7_ = bf16[256,2048]{1,0:T(8,128)(2,1)S(1)} custom-call(s32[2]{0:T(128)S(1)} %copy-done.37, bf16[1024,512]{1,0:T(8,128)(2,1)S(1)} %copy-done.11, bf16[1024,512]{1,0:T(8,128)(2,1)S(1)} %copy-done.3, bf16[1024,2048]{1,0:T(8,128)(2,1)} %spans.5.refs_7_.refs_0_, bf16[256,1024]{1,0:T(8,128)(2,1)S(1)} %get-tuple-element.68.refs_7_.refs_1_, ...), custom_call_target="tpu_custom_call" | custom-call | flops 1000000000 | bytes 1 | tf_op jit(solution)/shard_map/back_whole/pallas_call | solution.py:565
  159.0 4.2 %back_whole.10 = bf16[256,16384]{1,0:T(8,128)(2,1)} custom-call(s32[2]{0:T(128)S(1)} %copy-done.37, bf16[1024,512]{1,0:T(8,128)(2,1)S(1)} %copy-done.8, bf16[1024,512]{1,0:T(8,128)(2,1)S(1)} %copy-done.3, bf16[1024,1024]{1,0:T(8,128)(2,1)} %copy-done.5, bf16[256,512]{1,0:T(8,128)(2,1)S(1)} %copy-done.14, bf16[256,512]{1,0:T(8,128)(2,1)S(1)} %copy-done.16, ...), custom_call_target="tpu_custom_call" | custom-call | flops 1000000000 | bytes 1 | tf_op jit(solution)/shard_map/back_whole/pallas_call | solution.py:565
  163.2 2.0 fusion
  165.2 1.9 slice_dynamic-update-slice_fusion.1
  167.7 2.0 fusion.1
  169.7 1.9 slice_dynamic-update-slice_fusion
  172.7 4.3 %back_whole.11 = bf16[256,16384]{1,0:T(8,128)(2,1)} custom-call(s32[2]{0:T(128)S(1)} %copy-done.37, bf16[1024,512]{1,0:T(8,128)(2,1)S(1)} %copy-done.11, bf16[1024,512]{1,0:T(8,128)(2,1)S(1)} %copy-done.3, bf16[1024,2048]{1,0:T(8,128)(2,1)} %spans.5.refs_7_.refs_0_, ...), custom_call_target="tpu_custom_call", output_to_operand_aliasing={{}: (9, {})} | custom-call | flops 1000000000 | bytes 1 | tf_op jit(solution)/shard_map/back_whole/pallas_call | solution.py:565
  179.1 20.2 %collective-permute-done.21 = bf16[256,2048]{1,0:T(8,128)(2,1)S(1)} collective-permute-done((bf16[256,2048]{1,0:T(8,128)(2,1)S(1)}, bf16[256,2048]{1,0:T(8,128)(2,1)S(1)}, u32[]{:S(2)}, u32[]{:S(2)}) %collective-permute-start.21) | collective-permute-done | bytes 1048608 | tf_op jit(solution)/shard_map/ppermute | solution.py:718
  (130 shorter events, 21.1 us)
Async XLA Ops:
  0.7 13.1 %collective-permute-start = (bf16[3,2,512]{2,1,0:T(2,128)(2,1)S(1)}, bf16[3,2,512]{2,1,0:T(2,128)(2,1)S(1)}, u32[]{:S(2)}, u32[]{:S(2)}) collective-permute-start(bf16[3,2,512]{2,1,0:T(2,128)(2,1)S(1)} %slice.24), channel_id=1, source_target_pairs={{0,4},{4,8},{8,12},{12,16},{16,20},{20,24},{24,28},{1,5},{5,9},{9,... | collective-permute-start | bytes 18440 | tf_op jit(solution)/shard_map/ppermute | solution.py:677
  6.4 10.4 %collective-permute-start.1 = (bf16[3,4096]{1,0:T(4,128)(2,1)S(1)}, bf16[3,4096]{1,0:T(4,128)(2,1)S(1)}, u32[]{:S(2)}, u32[]{:S(2)}) collective-permute-start(bf16[3,4096]{1,0:T(4,128)(2,1)S(1)} %slice.25), channel_id=1, source_target_pairs={{0,4},{4,8},{8,12},{12,16},{16,20},{20,24},{24,28},{1,5},{5,9},{9,... | collective-permute-start | bytes 73736 | tf_op jit(solution)/shard_map/ppermute | solution.py:676
  13.7 118.4 %copy-start.2 = (bf16[1024,512]{1,0:T(8,128)(2,1)}, bf16[1024,512]{1,0:T(8,128)(2,1)S(1)}, u32[]{:S(2)}) copy-start(bf16[1024,512]{1,0:T(8,128)(2,1)S(1)} %get-tuple-element.38.dev_ref.edev_ref.table_ref) | copy-start | bytes 3145732
  13.8 88.0 %copy-start.36 = (s32[2]{0:T(128)}, s32[2]{0:T(128)S(1)}, u32[]{:S(2)}) copy-start(s32[2]{0:T(128)S(1)} %pad_add_fusion.where_ref) | copy-start | bytes 28
  16.8 115.2 %copy-start.6 = (bf16[1024,512]{1,0:T(8,128)(2,1)}, bf16[1024,512]{1,0:T(8,128)(2,1)S(1)}, u32[]{:S(2)}) copy-start(bf16[1024,512]{1,0:T(8,128)(2,1)S(1)} %get-tuple-element.40.refs_0_.map_ref.out_ref) | copy-start | bytes 3145732
  23.8 8.9 %copy-start.24 = (f32[264,512]{1,0:T(8,128)}, f32[264,512]{1,0:T(8,128)S(1)}, u32[]{:S(2)}) copy-start(f32[264,512]{1,0:T(8,128)S(1)} %get-tuple-element.41.kept_ref) | copy-start | bytes 1622020
  23.8 8.2 %collective-permute-start.2 = (bf16[272,512]{1,0:T(8,128)(2,1)S(1)}, bf16[272,512]{1,0:T(8,128)(2,1)S(1)}, u32[]{:S(2)}, u32[]{:S(2)}) collective-permute-start(bf16[272,512]{1,0:T(8,128)(2,1)S(1)} %get-tuple-element.42), channel_id=1, source_target_pairs={{0,4},{4,0},{8,12},{12,8},{16,20},{20,16},{24,28},{28,24},{1,5},{5... | collective-permute-start | bytes 835592 | tf_op jit(solution)/shard_map/ppermute | solution.py:608
  31.5 18.9 %copy-start.12 = (bf16[1024,1024]{1,0:T(8,128)(2,1)}, bf16[1024,1024]{1,0:T(8,128)(2,1)S(1)}, u32[]{:S(2)}) copy-start(bf16[1024,1024]{1,0:T(8,128)(2,1)S(1)} %get-tuple-element.44.refs_0_.xh_ref) | copy-start | bytes 6291460
  31.5 18.9 %copy-start.30 = (f32[264,512]{1,0:T(8,128)}, f32[264,512]{1,0:T(8,128)S(1)}, u32[]{:S(2)}) copy-start(f32[264,512]{1,0:T(8,128)S(1)} %get-tuple-element.48.kept_ref) | copy-start | bytes 1622020
  31.5 17.5 %collective-permute-start.3 = (bf16[272,512]{1,0:T(8,128)(2,1)S(1)}, bf16[272,512]{1,0:T(8,128)(2,1)S(1)}, u32[]{:S(2)}, u32[]{:S(2)}) collective-permute-start(bf16[272,512]{1,0:T(8,128)(2,1)S(1)} %get-tuple-element.49), channel_id=1, source_target_pairs={{0,4},{4,0},{8,12},{12,8},{16,20},{20,16},{24,28},{28,24},{1,5},{5... | collective-permute-start | bytes 835592 | tf_op jit(solution)/shard_map/ppermute | solution.py:608
  32.0 18.4 %copy-start.26 = (bf16[272,512]{1,0:T(8,128)(2,1)}, bf16[272,512]{1,0:T(8,128)(2,1)S(1)}, u32[]{:S(2)}) copy-start(bf16[272,512]{1,0:T(8,128)(2,1)S(1)} %collective-permute-done.2.got_ref) | copy-start | bytes 835588
  32.8 8.3 %collective-permute-start.4 = (bf16[272,512]{1,0:T(8,128)(2,1)S(1)}, bf16[272,512]{1,0:T(8,128)(2,1)S(1)}, u32[]{:S(2)}, u32[]{:S(2)}) collective-permute-start(bf16[272,512]{1,0:T(8,128)(2,1)S(1)} %get-tuple-element.50), channel_id=1, source_target_pairs={{0,8},{4,12},{8,16},{12,20},{16,24},{20,28},{1,9},{5,13},{9,17},{1... | collective-permute-start | bytes 835592 | tf_op jit(solution)/shard_map/ppermute | solution.py:600
  41.1 12.3 %copy-start.34 = (bf16[272,512]{1,0:T(8,128)(2,1)}, bf16[272,512]{1,0:T(8,128)(2,1)S(1)}, u32[]{:S(2)}) copy-start(bf16[272,512]{1,0:T(8,128)(2,1)S(1)} %collective-permute-done.4.before_ref) | copy-start | bytes 835588
  42.9 30.6 %collective-permute-start.7 = (bf16[272,512]{1,0:T(8,128)(2,1)}, bf16[272,512]{1,0:T(8,128)(2,1)}, u32[]{:S(2)}, u32[]{:S(2)}) collective-permute-start(bf16[272,512]{1,0:T(8,128)(2,1)} %inclusive.3.refs_0_), channel_id=1, source_target_pairs={{0,16},{4,20},{8,24},{12,28},{1,17},{5,21},{9,25},{13,29},{2,18},{... | collective-permute-start | bytes 835592 | tf_op jit(solution)/shard_map/ppermute | solution.py:600
  49.0 17.2 %copy-start.38 = (bf16[2,128]{1,0:T(2,128)(2,1)S(1)}, bf16[2,128]{1,0:T(2,128)(2,1)}, u32[]{:S(2)}) copy-start(bf16[2,128]{1,0:T(2,128)(2,1)} %constant.48.clone.halves_ref) | copy-start | bytes 1540
  50.4 27.0 %collective-permute-start.6 = (bf16[272,512]{1,0:T(8,128)(2,1)}, bf16[272,512]{1,0:T(8,128)(2,1)}, u32[]{:S(2)}, u32[]{:S(2)}) collective-permute-start(bf16[272,512]{1,0:T(8,128)(2,1)} %get-tuple-element.58), channel_id=1, source_target_pairs={{0,8},{4,12},{8,16},{12,20},{16,24},{20,28},{1,9},{5,13},{9,17},{1... | collective-permute-start | bytes 835592 | tf_op jit(solution)/shard_map/ppermute | solution.py:600
  64.7 16.5 %copy-start.28 = (f32[264,1024]{1,0:T(8,128)}, f32[264,1024]{1,0:T(8,128)S(1)}, u32[]{:S(2)}) copy-start(f32[264,1024]{1,0:T(8,128)S(1)} %get-tuple-element.56.kept_ref) | copy-start | bytes 3244036
  64.7 16.5 %collective-permute-start.5 = (bf16[272,1024]{1,0:T(8,128)(2,1)}, bf16[272,1024]{1,0:T(8,128)(2,1)}, u32[]{:S(2)}, u32[]{:S(2)}) collective-permute-start(bf16[272,1024]{1,0:T(8,128)(2,1)} %get-tuple-element.57), channel_id=1, source_target_pairs={{0,4},{4,0},{8,12},{12,8},{16,20},{20,16},{24,28},{28,24},{1,5},{5... | collective-permute-start | bytes 1671176 | tf_op jit(solution)/shard_map/ppermute | solution.py:608
  66.1 7.3 %copy-start.25 = (f32[264,512]{1,0:T(8,128)S(1)}, f32[264,512]{1,0:T(8,128)}, u32[]{:S(2)}) copy-start(f32[264,512]{1,0:T(8,128)} %copy-done.24) | copy-start | bytes 1622020
  66.1 7.3 %copy-start.27 = (bf16[272,512]{1,0:T(8,128)(2,1)S(1)}, bf16[272,512]{1,0:T(8,128)(2,1)}, u32[]{:S(2)}) copy-start(bf16[272,512]{1,0:T(8,128)(2,1)} %copy-done.26) | copy-start | bytes 835588
  66.2 7.4 %copy-start.35 = (bf16[272,512]{1,0:T(8,128)(2,1)S(1)}, bf16[272,512]{1,0:T(8,128)(2,1)}, u32[]{:S(2)}) copy-start(bf16[272,512]{1,0:T(8,128)(2,1)} %copy-done.34) | copy-start | bytes 835588
  73.5 12.0 %copy-start.5 = (bf16[1024,1024]{1,0:T(8,128)(2,1)}, bf16[1024,1024]{1,0:T(8,128)(2,1)S(1)}, u32[]{:S(2)}) copy-start(bf16[1024,1024]{1,0:T(8,128)(2,1)S(1)} %spans.3.refs_0_) | copy-start | bytes 6291460
  73.5 12.0 %copy-start.22 = (f32[4096]{0:T(1024)S(1)}, f32[4096]{0:T(1024)}, u32[]{:S(2)}) copy-start(f32[4096]{0:T(1024)} %param.19) | copy-start | bytes 49156
  74.9 13.8 %copy-start.13 = (bf16[256,512]{1,0:T(8,128)(2,1)}, bf16[256,512]{1,0:T(8,128)(2,1)S(1)}, u32[]{:S(2)}) copy-start(bf16[256,512]{1,0:T(8,128)(2,1)S(1)} %get-tuple-element.59.refs_0_.refs_1_) | copy-start | bytes 786436
  74.9 10.6 %collective-permute-start.10 = (bf16[256,512]{1,0:T(8,128)(2,1)S(1)}, bf16[256,512]{1,0:T(8,128)(2,1)S(1)}, u32[]{:S(2)}, u32[]{:S(2)}) collective-permute-start(bf16[256,512]{1,0:T(8,128)(2,1)S(1)} %get-tuple-element.62), channel_id=1, source_target_pairs={{0,4},{8,12},{12,8},{16,20},{20,16},{24,28},{28,24},{1,5},{9,13},{... | collective-permute-start | bytes 786440 | tf_op jit(solution)/shard_map/ppermute | solution.py:651
  79.2 22.6 %collective-permute-start.9 = (bf16[272,512]{1,0:T(8,128)(2,1)}, bf16[272,512]{1,0:T(8,128)(2,1)}, u32[]{:S(2)}, u32[]{:S(2)}) collective-permute-start(bf16[272,512]{1,0:T(8,128)(2,1)} %inclusive.4.refs_0_), channel_id=1, source_target_pairs={{0,16},{4,20},{8,24},{12,28},{1,17},{5,21},{9,25},{13,29},{2,18},{... | collective-permute-start | bytes 835592 | tf_op jit(solution)/shard_map/ppermute | solution.py:600
  83.4 20.1 %collective-permute-start.8 = (bf16[272,1024]{1,0:T(8,128)(2,1)}, bf16[272,1024]{1,0:T(8,128)(2,1)}, u32[]{:S(2)}, u32[]{:S(2)}) collective-permute-start(bf16[272,1024]{1,0:T(8,128)(2,1)} %get-tuple-element.61), channel_id=1, source_target_pairs={{0,8},{4,12},{8,16},{12,20},{16,24},{20,28},{1,9},{5,13},{9,17},{1... | collective-permute-start | bytes 1671176 | tf_op jit(solution)/shard_map/ppermute | solution.py:600
  85.5 6.3 %copy-start.15 = (bf16[256,512]{1,0:T(8,128)(2,1)}, bf16[256,512]{1,0:T(8,128)(2,1)S(1)}, u32[]{:S(2)}) copy-start(bf16[256,512]{1,0:T(8,128)(2,1)S(1)} %collective-permute-done.10.refs_2_) | copy-start | bytes 786436
  88.6 35.1 %collective-permute-start.13 = (bf16[256,1024]{1,0:T(8,128)(2,1)}, bf16[256,1024]{1,0:T(8,128)(2,1)}, u32[]{:S(2)}, u32[]{:S(2)}) collective-permute-start(bf16[256,1024]{1,0:T(8,128)(2,1)} %get-tuple-element.63.refs_6_), channel_id=1, source_target_pairs={{0,3},{1,2},{2,1},{3,0},{4,7},{5,6},{6,5},{7,4},{8,11},{9,10},{10,... | collective-permute-start | bytes 1572872 | tf_op jit(solution)/shard_map/ppermute | solution.py:718
  91.8 31.9 %collective-permute-start.14 = (bf16[256,1024]{1,0:T(8,128)(2,1)}, bf16[256,1024]{1,0:T(8,128)(2,1)}, u32[]{:S(2)}, u32[]{:S(2)}) collective-permute-start(bf16[256,1024]{1,0:T(8,128)(2,1)} %get-tuple-element.64.refs_0_), channel_id=1, source_target_pairs={{0,2},{1,3},{2,0},{3,1},{4,6},{5,7},{6,4},{7,5},{8,10},{9,11},{10,... | collective-permute-start | bytes 1572872 | tf_op jit(solution)/shard_map/ppermute | solution.py:718
  93.3 8.6 %copy-start.33 = (bf16[272,512]{1,0:T(8,128)(2,1)S(1)}, bf16[272,512]{1,0:T(8,128)(2,1)}, u32[]{:S(2)}) copy-start(bf16[272,512]{1,0:T(8,128)(2,1)} %copy-done.32) | copy-start | bytes 835588
  94.5 7.4 %copy-start.31 = (f32[264,512]{1,0:T(8,128)S(1)}, f32[264,512]{1,0:T(8,128)}, u32[]{:S(2)}) copy-start(f32[264,512]{1,0:T(8,128)} %copy-done.30) | copy-start | bytes 1622020
  94.5 15.8 %copy-start.10 = (bf16[1024,512]{1,0:T(8,128)(2,1)S(1)}, bf16[1024,512]{1,0:T(8,128)(2,1)}, u32[]{:S(2)}) copy-start(bf16[1024,512]{1,0:T(8,128)(2,1)} %copy-done.9) | copy-start | bytes 3145732
  101.8 21.9 %copy-start.4 = (bf16[1024,1024]{1,0:T(8,128)(2,1)}, bf16[1024,1024]{1,0:T(8,128)(2,1)S(1)}, u32[]{:S(2)}) copy-start(bf16[1024,1024]{1,0:T(8,128)(2,1)S(1)} %spans.4.refs_0_.refs_6_) | copy-start | bytes 6291460
  103.5 20.2 %copy-start.37 = (s32[2]{0:T(128)S(1)}, s32[2]{0:T(128)}, u32[]{:S(2)}) copy-start(s32[2]{0:T(128)} %copy-done.36) | copy-start | bytes 28
  104.8 23.1 %collective-permute-start.11 = (bf16[272,1024]{1,0:T(8,128)(2,1)S(1)}, bf16[272,1024]{1,0:T(8,128)(2,1)S(1)}, u32[]{:S(2)}, u32[]{:S(2)}) collective-permute-start(bf16[272,1024]{1,0:T(8,128)(2,1)S(1)} %inclusive.5.refs_0_), channel_id=1, source_target_pairs={{0,16},{4,20},{8,24},{12,28},{1,17},{5,21},{9,25},{13,29},{2,18},{... | collective-permute-start | bytes 1671176 | tf_op jit(solution)/shard_map/ppermute | solution.py:600
  106.7 17.0 %collective-permute-start.12 = (bf16[256,512]{1,0:T(8,128)(2,1)S(1)}, bf16[256,512]{1,0:T(8,128)(2,1)S(1)}, u32[]{:S(2)}, u32[]{:S(2)}) collective-permute-start(bf16[256,512]{1,0:T(8,128)(2,1)S(1)} %get-tuple-element.66), channel_id=1, source_target_pairs={{0,4},{8,12},{12,8},{16,20},{20,16},{24,28},{28,24},{1,5},{9,13},{... | collective-permute-start | bytes 786440 | tf_op jit(solution)/shard_map/ppermute | solution.py:651
  123.7 8.3 %copy-start.17 = (bf16[256,512]{1,0:T(8,128)(2,1)}, bf16[256,512]{1,0:T(8,128)(2,1)S(1)}, u32[]{:S(2)}) copy-start(bf16[256,512]{1,0:T(8,128)(2,1)S(1)} %collective-permute-done.12.refs_2_.refs_8_) | copy-start | bytes 786436
  127.3 16.3 %collective-permute-start.16 = (bf16[272,1024]{1,0:T(8,128)(2,1)}, bf16[272,1024]{1,0:T(8,128)(2,1)}, u32[]{:S(2)}, u32[]{:S(2)}) collective-permute-start(bf16[272,1024]{1,0:T(8,128)(2,1)} %back_rest.2.refs_0_), channel_id=1, source_target_pairs={{0,3},{1,2},{2,1},{3,0},{4,7},{5,6},{6,5},{7,4},{8,11},{9,10},{10,... | collective-permute-start | bytes 1671176 | tf_op jit(solution)/shard_map/ppermute | solution.py:718
  130.3 6.0 %copy-start.16 = (bf16[256,512]{1,0:T(8,128)(2,1)S(1)}, bf16[256,512]{1,0:T(8,128)(2,1)}, u32[]{:S(2)}) copy-start(bf16[256,512]{1,0:T(8,128)(2,1)} %copy-done.15) | copy-start | bytes 786436
  130.3 6.0 %copy-start.23 = (f32[4096]{0:T(1024)S(1)}, f32[4096]{0:T(1024)}, u32[]{:S(2)}) copy-start(f32[4096]{0:T(1024)} %param.19) | copy-start | bytes 49156
  130.3 14.2 %collective-permute-start.15 = (bf16[256,1024]{1,0:T(8,128)(2,1)}, bf16[256,1024]{1,0:T(8,128)(2,1)S(1)}, u32[]{:S(2)}, u32[]{:S(2)}) collective-permute-start(bf16[256,1024]{1,0:T(8,128)(2,1)} %get-tuple-element.69), channel_id=1, source_target_pairs={{0,4},{8,12},{12,8},{16,20},{20,16},{24,28},{28,24},{1,5},{9,13},{... | collective-permute-start | bytes 1572872 | tf_op jit(solution)/shard_map/ppermute | solution.py:651
  135.6 18.9 %collective-permute-start.17 = (bf16[272,1024]{1,0:T(8,128)(2,1)}, bf16[272,1024]{1,0:T(8,128)(2,1)}, u32[]{:S(2)}, u32[]{:S(2)}) collective-permute-start(bf16[272,1024]{1,0:T(8,128)(2,1)} %back_rest.3.refs_12_), channel_id=1, source_target_pairs={{0,2},{1,3},{2,0},{3,1},{4,6},{5,7},{6,4},{7,5},{8,10},{9,11},{10,... | collective-permute-start | bytes 1671176 | tf_op jit(solution)/shard_map/ppermute | solution.py:718
  143.2 28.4 %collective-permute-start.18 = (bf16[256,2048]{1,0:T(8,128)(2,1)S(1)}, bf16[256,2048]{1,0:T(8,128)(2,1)S(1)}, u32[]{:S(2)}, u32[]{:S(2)}) collective-permute-start(bf16[256,2048]{1,0:T(8,128)(2,1)S(1)} %back_whole.6.refs_6_), channel_id=1, source_target_pairs={{0,1},{1,0},{2,3},{3,2},{4,5},{5,4},{6,7},{7,6},{8,9},{9,8},{10,11... | collective-permute-start | bytes 3145736 | tf_op jit(solution)/shard_map/ppermute | solution.py:718
  148.1 28.9 %collective-permute-start.19 = (bf16[256,2048]{1,0:T(8,128)(2,1)S(1)}, bf16[256,2048]{1,0:T(8,128)(2,1)S(1)}, u32[]{:S(2)}, u32[]{:S(2)}) collective-permute-start(bf16[256,2048]{1,0:T(8,128)(2,1)S(1)} %back_whole.7.refs_6_), channel_id=1, source_target_pairs={{0,3},{1,2},{2,1},{3,0},{4,7},{5,6},{6,5},{7,4},{8,11},{9,10},{10,... | collective-permute-start | bytes 3145736 | tf_op jit(solution)/shard_map/ppermute | solution.py:718
  152.8 6.2 %copy-start.8 = (bf16[1024,512]{1,0:T(8,128)(2,1)S(1)}, bf16[1024,512]{1,0:T(8,128)(2,1)}, u32[]{:S(2)}) copy-start(bf16[1024,512]{1,0:T(8,128)(2,1)} %copy-done.6) | copy-start | bytes 3145732
  152.8 25.3 %collective-permute-start.20 = (bf16[256,2048]{1,0:T(8,128)(2,1)S(1)}, bf16[256,2048]{1,0:T(8,128)(2,1)S(1)}, u32[]{:S(2)}, u32[]{:S(2)}) collective-permute-start(bf16[256,2048]{1,0:T(8,128)(2,1)S(1)} %back_whole.8.refs_6_), channel_id=1, source_target_pairs={{0,1},{1,0},{2,3},{3,2},{4,5},{5,4},{6,7},{7,6},{8,9},{9,8},{10,11... | collective-permute-start | bytes 3145736 | tf_op jit(solution)/shard_map/ppermute | solution.py:718
  158.1 41.3 %collective-permute-start.21 = (bf16[256,2048]{1,0:T(8,128)(2,1)S(1)}, bf16[256,2048]{1,0:T(8,128)(2,1)S(1)}, u32[]{:S(2)}, u32[]{:S(2)}) collective-permute-start(bf16[256,2048]{1,0:T(8,128)(2,1)S(1)} %back_whole.9.refs_12_.refs_7_), channel_id=1, source_target_pairs={{0,2},{1,3},{2,0},{3,1},{4,6},{5,7},{6,4},{7,5},{8,10},{9,11},{10,... | collective-permute-start | bytes 3145736 | tf_op jit(solution)/shard_map/ppermute | solution.py:718
  (19 other events, 41.3 us)
